TPU v7x, 256 devices: a whole 4x4x8 slice. The times are simulated.
256 devices in a mesh: seq: 64 (over z, x, core), head: 4 (over y).
Axes of the slice: x: 4, y: 4, z: 8, core: 2. Of those that a mesh axis runs over, the one named last changes fastest.
Arguments:
- inputs: bfloat16 [16384, 8192], P(('seq', 'head')), may hold values from -6 to 6
- gate: bfloat16 [16384, 8192], P('seq', 'head'), may hold values from -40 to 40
- in_b: bfloat16 [16384, 128], P('seq'), may hold values from -4 to 4
- in_c: bfloat16 [16384, 128], P('seq'), may hold values from -4 to 4
- log_decay: float32 [128, 16384], P('head', 'seq'), may hold values from -1 to 0
- step_size: float32 [128, 16384], P('head', 'seq'), may hold values from 0 to 1
- importance: float32 [16384], P('seq'), may hold values from 0.2 to 2
- skip: float32 [128], P('head'), may hold values from 0.5 to 1.5
- norm_gain: float32 [8192], P('head'), may hold values from 0.25 to 1.75
Outputs:
- outputs: bfloat16 [16384, 8192], P('seq', 'head')
All inputs are finite; a program needn't handle non-finite values.
Results may differ from a plain program's by a relative error of at most 0.0055.
Values may be sent and summed in bfloat16 or wider, within the bound.
No kernel may reach another device: no remote copies, remote signals or barrier semaphores. Data moves between devices by JAX's collectives and lax.ppermute only.
A program may use at most 192 MiB of HBM per device.

v0:
```python
import jax
import jax.numpy as jnp
from jax import lax
from jax.sharding import PartitionSpec as P

HEADS = 128
HEAD_DIM = 64
STATE = 128
STRETCH = 256


epsilon = 1e-05


def prefix(part, axis, combine, identity):
    place = lax.axis_index(axis)
    gathered = jax.tree.map(lambda a: lax.all_gather(a, axis), part)
    state = jax.tree.map(lambda a, e: jnp.zeros_like(a) + jnp.asarray(e, a.dtype), part, identity)

    def one(turn, state):
        return combine(
            state, jax.tree.map(lambda a: lax.dynamic_index_in_dim(a, turn, 0, False), gathered)
        )

    return lax.fori_loop(0, place, one, state)


def block_terms(scaled_in, b_rows, c_rows, log_rows):
    cumulative = jnp.cumsum(log_rows, axis=1)
    length = log_rows.shape[1]
    later = jnp.arange(length)[:, None] >= jnp.arange(length)[None, :]
    scores = jnp.dot(c_rows, b_rows.T, preferred_element_type=jnp.float32)
    spread = cumulative[:, :, None] - cumulative[:, None, :]
    weights = jnp.where(
        later[None], scores[None] * jnp.exp(jnp.where(later[None], spread, 0.0)), 0.0
    ).astype(jnp.bfloat16)
    within = jnp.einsum("hts,shp->thp", weights, scaled_in, preferred_element_type=jnp.float32)
    tail = jnp.exp(cumulative[:, -1:] - cumulative)
    decayed = (b_rows.astype(jnp.float32)[None, :, :] * tail[:, :, None]).astype(jnp.bfloat16)
    local_state = jnp.einsum("hsn,shp->hpn", decayed, scaled_in, preferred_element_type=jnp.float32)
    return (within, cumulative, local_state)


def combine_states(earlier, later):
    decay_early, state_early = earlier
    decay_late, state_late = later
    return (decay_early * decay_late, decay_late[:, None, None] * state_early + state_late)


def on_device(inputs, gate, in_b, in_c, log_decay, step_size, importance, skip, norm_gain):
    regrouped = lax.all_to_all(inputs, "head", split_axis=1, concat_axis=0, tiled=True)
    token_count = regrouped.shape[0]
    head_count = log_decay.shape[0]
    features_here = regrouped.shape[1]
    channels = regrouped.astype(jnp.float32).reshape(token_count, head_count, HEAD_DIM)
    scaled_all = (channels * step_size.T[:, :, None] * importance[:, None, None]).astype(
        jnp.bfloat16
    )
    within, cumulative, local_state = block_terms(scaled_all, in_b, in_c, log_decay)
    within_parts = [within]
    cum_parts = [cumulative]
    local_parts = [local_state]
    device_state = jnp.zeros((head_count, HEAD_DIM, STATE), jnp.float32)
    position = 0
    ending = cum_parts[position][:, -1]
    device_state = jnp.exp(ending)[:, None, None] * device_state + local_parts[position]
    unit_decay = jnp.ones((head_count,), jnp.float32)
    empty_state = jnp.zeros((head_count, HEAD_DIM, STATE), jnp.float32)
    decay_before, entering = prefix(
        (jnp.exp(ending), device_state), "seq", combine_states, (unit_decay, empty_state)
    )
    position = 0
    cumulative = cum_parts[position]
    rounded = entering.astype(jnp.bfloat16)
    carried = jnp.einsum("tn,hpn->thp", in_c, rounded, preferred_element_type=jnp.float32)
    carried = carried * jnp.exp(cumulative).T[:, :, None]
    mixed = within_parts[position] + carried + skip[None, :, None] * channels
    gated = mixed.reshape(STRETCH, features_here) * jax.nn.silu(gate.astype(jnp.float32))
    squares_here = jnp.sum(gated * gated, axis=1)
    total_squares = lax.psum(squares_here, "head")
    scaling = lax.rsqrt(total_squares / (HEADS * HEAD_DIM) + epsilon)
    return (gated * scaling[:, None] * norm_gain[None, :]).astype(jnp.bfloat16)


def solution(mesh):
    in_specs = (
        P(("seq", "head"), None),
        P("seq", "head"),
        P("seq", None),
        P("seq", None),
        P("head", "seq"),
        P("head", "seq"),
        P("seq"),
        P("head"),
        P("head"),
    )
    out_specs = P("seq", "head")
    return jax.shard_map(
        on_device, mesh=mesh, in_specs=in_specs, out_specs=out_specs, check_vma=False
    )
```

profile of v0, /device:TPU:231, one launch (start us, length us, event | category | flops | bytes accessed | tf_op | source)
XLA Modules:
  0.0 433.7 jit_solution(4513330620260844436)
XLA Ops:
  6.5 2.3 copy.51
  8.9 4.2 all-to-all-start
  15.0 12.2 %all-to-all-done = bf16[64,4,2048]{2,0,1:T(8,128)(2,1)S(1)} async-done(((bf16[64,4,2048]{2,0,1:T(8,128)(2,1)}), bf16[64,4,2048]{2,0,1:T(8,128)(2,1)S(1)}, u32[]{:S(2)}, u32[]{:S(2)}) %all-to-all-start) | async-done | bytes 1048608 | tf_op jit(solution)/shard_map/all_to_all | solution.py:51
  27.5 3.0 reshape.109
  30.6 4.3 multiply_convert_fusion.1
  34.9 1.7 copy.37
  36.6 2.5 fusion.15
  40.5 129.2 %all-reduce = f32[2048]{0:T(1024)S(1)} all-reduce(f32[2048]{0:T(1024)S(1)} %dynamic-update-slice), channel_id=2, replica_groups=mesh['seq'=64,'head'=4] {'seq'}, use_global_device_ids=true, to_apply=%add | all-reduce | flops 2048 | bytes 16384
  171.2 3.6 copy.39
  174.8 98.3 %all-gather.4.cloned.1.call-done = f32[2048,64,128]{2,1,0:T(8,128)} async-done(((f32[32,64,128]{2,1,0:T(8,128)}), f32[2048,64,128]{2,1,0:T(8,128)}) %all-gather.4.cloned.1.call-update) | async-done | bytes 67108880 | tf_op jit(solution)/shard_map/all_gather | solution.py:17
  273.3 135.6 %while.12 = (s32[]{:T(128)}, f32[32,64,128]{2,1,0:T(8,128)S(1)}, s32[]{:T(128)}, f32[64,32]{1,0:T(8,128)}, f32[64,32,64,128]{3,2,1,0:T(8,128)}, /*index=5*/s32[]{:T(128)}, s32[]{:T(128)}, s32[]{:T(128)}) while((s32[]{:T(128)}, f32[32,64,128]{2,1,0:T(8,128)S(1)}, s32[]{:T(128)}, f32[64,32]{1,0:T(8,128)}, f32[64,32,64,128]{3,2,1,0:T(8,128)}, ...), condition=%wide.region_3.4_spmd, body=%wide.region_2.3_spmd.sunk | while | flops 524293 | bytes 3146247 | solution.py:25
  274.0 1.4 bitcast_add_fusion.2
  276.1 1.4 bitcast_add_fusion.2
  278.3 1.4 bitcast_add_fusion.2
  280.4 1.4 bitcast_add_fusion.2
  282.6 1.4 bitcast_add_fusion.2
  284.7 1.4 bitcast_add_fusion.2
  286.9 1.4 bitcast_add_fusion.2
  289.0 1.4 bitcast_add_fusion.2
  291.2 1.4 bitcast_add_fusion.2
  293.3 1.4 bitcast_add_fusion.2
  295.5 1.4 bitcast_add_fusion.2
  297.7 1.4 bitcast_add_fusion.2
  299.8 1.4 bitcast_add_fusion.2
  302.0 1.4 bitcast_add_fusion.2
  304.1 1.4 bitcast_add_fusion.2
  306.3 1.4 bitcast_add_fusion.2
  308.4 1.4 bitcast_add_fusion.2
  310.6 1.4 bitcast_add_fusion.2
  312.7 1.4 bitcast_add_fusion.2
  314.9 1.4 bitcast_add_fusion.2
  317.0 1.4 bitcast_add_fusion.2
  319.2 1.4 bitcast_add_fusion.2
  321.3 1.4 bitcast_add_fusion.2
  323.5 1.4 bitcast_add_fusion.2
  325.6 1.4 bitcast_add_fusion.2
  327.8 1.4 bitcast_add_fusion.2
  329.9 1.4 bitcast_add_fusion.2
  332.1 1.4 bitcast_add_fusion.2
  334.2 1.4 bitcast_add_fusion.2
  336.4 1.4 bitcast_add_fusion.2
  338.5 1.4 bitcast_add_fusion.2
  340.7 1.4 bitcast_add_fusion.2
  342.9 1.4 bitcast_add_fusion.2
  345.0 1.4 bitcast_add_fusion.2
  347.1 1.4 bitcast_add_fusion.2
  349.3 1.4 bitcast_add_fusion.2
  351.4 1.4 bitcast_add_fusion.2
  353.6 1.4 bitcast_add_fusion.2
  355.7 1.4 bitcast_add_fusion.2
  357.9 1.4 bitcast_add_fusion.2
  360.0 1.4 bitcast_add_fusion.2
  362.2 1.4 bitcast_add_fusion.2
  364.4 1.4 bitcast_add_fusion.2
  366.5 1.4 bitcast_add_fusion.2
  370.8 1.4 bitcast_add_fusion.2
  379.5 1.4 bitcast_add_fusion.2
  385.9 1.4 bitcast_add_fusion.2
  392.4 1.4 bitcast_add_fusion.2
  394.5 1.4 bitcast_add_fusion.2
  410.2 3.8 fusion.12
  413.9 2.0 copy.40
  416.7 8.3 %psum.7 = f32[256]{0:T(256)S(1)} all-reduce(f32[256]{0:T(256)S(1)} %multiply_reduce_fusion), channel_id=1, replica_groups=mesh['seq'=64,'head'=4] {'head'}, use_global_device_ids=true, to_apply=%region_5.6 | all-reduce | flops 256 | bytes 2048 | tf_op jit(solution)/shard_map/psum | solution.py:80
  425.1 1.8 multiply_convert_fusion.3
  (133 shorter events, 70.0 us)
Async XLA Ops:
  6.5 164.5 %copy-start = (bf16[256,128]{1,0:T(8,128)(2,1)S(1)}, bf16[256,128]{1,0:T(8,128)(2,1)}, u32[]{:S(2)}) copy-start(bf16[256,128]{1,0:T(8,128)(2,1)} %param.14) | copy-start | bytes 196612
  6.5 6.5 %copy-start.11 = (f32[32,256]{1,0:T(8,128)S(1)}, f32[32,256]{1,0:T(8,128)}, u32[]{:S(2)}) copy-start(f32[32,256]{1,0:T(8,128)} %param.15) | copy-start | bytes 98308
  6.5 7.3 %copy-start.8 = (f32[32,256]{1,0:T(8,128)S(1)}, f32[32,256]{1,0:T(8,128)}, u32[]{:S(2)}) copy-start(f32[32,256]{1,0:T(8,128)} %param.16) | copy-start | bytes 98308
  6.5 7.4 %copy-start.4 = (bf16[256,128]{1,0:T(8,128)(2,1)S(1)}, bf16[256,128]{1,0:T(8,128)(2,1)}, u32[]{:S(2)}) copy-start(bf16[256,128]{1,0:T(8,128)(2,1)} %param.13) | copy-start | bytes 196612
  8.9 18.4 %all-to-all-start = ((bf16[64,4,2048]{2,0,1:T(8,128)(2,1)}), bf16[64,4,2048]{2,0,1:T(8,128)(2,1)S(1)}, u32[]{:S(2)}, u32[]{:S(2)}) async-start(bf16[64,4,2048]{2,0,1:T(8,128)(2,1)} %bitcast.45), calls=%async_computation | async-start | bytes 2097152 | tf_op jit(solution)/shard_map/all_to_all | solution.py:51
  13.1 260.1 %all-gather.4.cloned.1.call-start = ((), (), s32[]{:S(2)}) async-start(), calls=%async_computation.1 | async-start | bytes 68157440 | tf_op jit(solution)/shard_map/all_gather | solution.py:17
  14.1 0.9 copy-start.5
  27.5 3.1 copy-start.13
  34.9 1.7 copy-start.10
  36.6 134.7 %copy-start.2 = (bf16[256,32,64]{0,2,1:T(8,128)(2,1)}, bf16[256,32,64]{0,2,1:T(8,128)(2,1)S(1)}, u32[]{:S(2)}) copy-start(bf16[256,32,64]{0,2,1:T(8,128)(2,1)S(1)} %copy.37) | copy-start | bytes 3145732
  36.6 2.5 copy-start.15
  408.9 1.2 copy-start.3
  408.9 1.2 copy-start.6
  408.9 1.2 copy-start.7
  408.9 1.2 copy-start.9
  409.0 1.2 copy-start.14
  413.9 2.0 copy-start.1
  416.0 9.1 %copy-start.12 = (f32[2048]{0:T(1024)S(1)}, f32[2048]{0:T(1024)}, u32[]{:S(2)}) copy-start(f32[2048]{0:T(1024)} %param.19) | copy-start | bytes 24580
Sparse Core Ops, SparseCore 0:
  39.2 233.9 all-gather.3
where the time goes:
time: 438 us; the launch traced here: 434 us
  blocking collectives  138 us (32%)
  waiting for transfers between devices  111 us (25%)
  other arithmetic  99.9 us (23%)
  local copies, waits for them, and re-layouts  58.7 us (13%)
  between operations  14.2 us (3%)
  matrix products  6.84 us (2%)
    unnamed x1, blocking collectives  129 us
    all_gather x1, waiting for transfers between devices, prefix(): gathered = jax.tree.map(lambda a: lax.all_gather(a, axis), part)  98.3 us
    add x63, other arithmetic, combine_states(): decay_late[:, None, None] * state_early + state_late  90.7 us
    mul x63, local copies, waits for them, and re-layouts, combine_states(): decay_late[:, None, None] * state_early + state_late  43.2 us
    all_to_all x1, waiting for transfers between devices, on_device(): lax.all_to_all(inputs, 'head', split_axis=1, concat_axis=0, tiled=True)  12.2 us
  transfers between devices with their start and end apart: 2, of which 2 were waited for; matrix products, arithmetic and copies ran while one was open for 2% of the time, Pallas kernels for 0%

commit v1 on v0

v1 whole, which is shorter than its diff:
```python
import functools

import jax
import jax.numpy as jnp
from jax import lax
from jax.experimental import pallas as pl
from jax.experimental.pallas import tpu as pltpu
from jax.sharding import Mesh, PartitionSpec as P

HEADS = 128
HEAD_DIM = 64
STATE = 128
STRETCH = 256
epsilon = 1e-05

F32 = jnp.float32
BF16 = jnp.bfloat16
HERE = 32
FEATS = HERE * HEAD_DIM
HALF = FEATS // 2
PART = HALF // 4
LOGS = 16


def kernel_call(body, outs, *args, scratch=(), flops=0, bytes_accessed=0):
    vmem = pl.BlockSpec(memory_space=pltpu.VMEM)
    return pl.pallas_call(
        body,
        out_shape=[jax.ShapeDtypeStruct(s, d) for s, d in outs],
        in_specs=[vmem] * len(args),
        out_specs=[vmem] * len(outs),
        scratch_shapes=[pltpu.VMEM(s, d) for s, d in scratch],
        compiler_params=pltpu.CompilerParams(vmem_limit_bytes=40 * 1024 * 1024),
        cost_estimate=pl.CostEstimate(
            flops=flops, bytes_accessed=bytes_accessed, transcendentals=0
        ),
    )(*args)


def three_terms(v):
    hi = v.astype(BF16).astype(F32)
    rest = v - hi
    mid = rest.astype(BF16).astype(F32)
    return hi, mid, rest - mid


def pick(index, first, second):
    return jnp.where(jnp.full(first.shape, index, jnp.int32) == 0, first, second)


def place(axis, step, size):
    return lax.rem(lax.axis_index(axis) + (step + size), size)


def log_block(row):
    hi, mid, lo = three_terms(row)
    at = lax.broadcasted_iota(jnp.int32, (LOGS, row.shape[1]), 0)
    return jnp.where(at == 0, hi, jnp.where(at == 1, mid, jnp.where(at == 2, lo, 0.0))).astype(BF16)


def logs_of(message):
    block = message[STATE:, :].astype(F32)
    return jnp.sum(block[:8, :], axis=0, keepdims=True)


def state_of(message):
    return message[:STATE, :].astype(F32)


def prepare(log_ref, step_ref, imp_ref, b_ref, c_ref, gate_ref,
            w_ref, dt_ref, dtt_ref, q_ref, g_ref, bt_ref, tot_ref):
    lane = lax.broadcasted_iota(jnp.int32, (HERE, STRETCH), 1)
    cum = log_ref[...]
    shift = 1
    while shift < STRETCH:
        cum = cum + jnp.where(lane >= shift, pltpu.roll(cum, shift, 1), 0.0)
        shift *= 2
    step = step_ref[...] * imp_ref[...]
    tail = jnp.exp(cum[:, STRETCH - 1:] - cum)
    spread = (
        lax.broadcasted_iota(jnp.int32, (128, FEATS), 0) % HERE
        == lax.broadcasted_iota(jnp.int32, (128, FEATS), 1) // HEAD_DIM
    ).astype(F32).astype(BF16)
    blank = jnp.zeros((HERE, STRETCH), F32)

    def columns(v):
        hi, mid, lo = three_terms(v)
        return jnp.concatenate([hi, mid, lo, blank], axis=0).T.astype(BF16)

    def expand(v, into):
        for at in range(0, FEATS, 512):
            into(at, jnp.dot(v, spread[:, at:at + 512], preferred_element_type=F32))

    def put_dt(at, v):
        dt_ref[:, at:at + 512] = v

    def put_dtt(at, v):
        dtt_ref[:, at:at + 512] = v

    def put_gate(at, v):
        gate = gate_ref[:, at:at + 512].astype(F32)
        g = gate / (1.0 + jnp.exp(-gate))
        g_ref[:, at:at + 512] = g
        q_ref[:, at:at + 512] = v * g

    expand(columns(step), put_dt)
    expand(columns(step * tail), put_dtt)
    expand(columns(jnp.exp(cum)), put_gate)
    logs = columns(cum)
    last = jnp.broadcast_to(logs[STRETCH - 16:, :][15:, :], (16, 128))
    tot_ref[...] = jnp.dot(last, spread, preferred_element_type=F32)[:8]
    bt_ref[...] = b_ref[...].astype(F32).T.astype(BF16)

    scores = lax.dot_general(
        c_ref[...], b_ref[...], (((1,), (1,)), ((), ())), preferred_element_type=F32
    )
    cum_columns = jnp.concatenate([cum, blank, blank, blank], axis=0).T
    tri = (
        lax.broadcasted_iota(jnp.int32, (128, 128), 0)
        >= lax.broadcasted_iota(jnp.int32, (128, 128), 1)
    )
    for h in range(HERE):
        row = cum[h:h + 1, :]
        top = cum_columns[:128, h:h + 1]
        low = cum_columns[128:, h:h + 1]
        w_ref[h, :128, :128] = (
            jnp.exp(jnp.where(tri, top - row[:, :128], -1e30)) * scores[:128, :128]
        ).astype(BF16)
        w_ref[h, 128:, :128] = (jnp.exp(low - row[:, :128]) * scores[128:, :128]).astype(BF16)
        w_ref[h, 128:, 128:] = (
            jnp.exp(jnp.where(tri, low - row[:, 128:], -1e30)) * scores[128:, 128:]
        ).astype(BF16)


def end_state(x0, x1, x2, x3, dtt_ref, bt_ref, x_ref, keep_ref, send_ref, local):
    for k, piece in enumerate((x0, x1, x2, x3)):
        at = pl.multiple_of(place("head", -k, 4) * 64, 64)
        x_ref[pl.ds(at, 64), :] = piece[...]
    for at in range(0, FEATS, 256):
        decayed = (x_ref[:, at:at + 256].astype(F32) * dtt_ref[:, at:at + 256]).astype(BF16)
        local[:, at:at + 256] = jnp.dot(bt_ref[...], decayed, preferred_element_type=F32)
    core = lax.axis_index("core")
    keep_ref[...] = local[:, pl.ds(pl.multiple_of(core * HALF, HALF), HALF)]
    send_ref[...] = local[:, pl.ds(pl.multiple_of((1 - core) * HALF, HALF), HALF)].astype(BF16)


def inside(x_ref, dt_ref, w_ref, g_ref, skip_ref, p_ref):
    first = lax.broadcasted_iota(jnp.int32, (STRETCH, 128), 1) < HEAD_DIM
    for j in range(FEATS // 128):
        at = slice(j * 128, j * 128 + 128)
        x = x_ref[:, at].astype(F32)
        scaled = x * dt_ref[:, at]
        one = jnp.where(first, scaled, 0.0).astype(BF16)
        two = jnp.where(first, 0.0, scaled).astype(BF16)
        top = jnp.dot(w_ref[2 * j, :128, :128], one[:128], preferred_element_type=F32)
        top += jnp.dot(w_ref[2 * j + 1, :128, :128], two[:128], preferred_element_type=F32)
        low = jnp.dot(w_ref[2 * j, 128:, :], one, preferred_element_type=F32)
        low += jnp.dot(w_ref[2 * j + 1, 128:, :], two, preferred_element_type=F32)
        skip = skip_ref[:, at]
        p_ref[:128, at] = (top + skip * x[:128]) * g_ref[:128, at]
        p_ref[128:, at] = (low + skip * x[128:]) * g_ref[128:, at]


def halves(core, mine_ref, other_ref):
    at = pl.ds(pl.multiple_of(core * HALF, HALF), HALF)
    mine, other = mine_ref[:1, at], other_ref[:1, at]
    return pick(core, mine, other), pick(core, other, mine)


def chip_state(keep_ref, came_ref, tot_ref, tot_other_ref, s0, s1, s2, s3, message):
    core = lax.axis_index("core")
    log0, log1 = halves(core, tot_ref, tot_other_ref)
    keep, came = keep_ref[...], came_ref[...].astype(F32)
    message[:STATE, :] = (
        jnp.exp(log1) * pick(core, keep, came) + pick(core, came, keep)
    ).astype(BF16)
    message[STATE:, :] = log_block(log0 + log1)
    for k, out in enumerate((s0, s1, s2, s3)):
        out[...] = message[:, pl.ds(pl.multiple_of(place("x", k, 4) * PART, PART), PART)]


def row_state(m0, m1, m2, m3, all_ref, row_ref, state_ref):
    for k, piece in enumerate((m0, m1, m2, m3)):
        all_ref[place("x", -k, 4)] = piece[...]
    state = state_of(all_ref[0])
    logs = logs_of(all_ref[0])
    for x in range(1, 4):
        log = logs_of(all_ref[x])
        state = jnp.exp(log) * state + state_of(all_ref[x])
        logs = logs + log
    state_ref[...] = state
    row_ref[:STATE, :] = state.astype(BF16)
    row_ref[STATE:, :] = log_block(logs)


def window(row_ref, state_ref, before_ref, out_ref):
    z = lax.axis_index("z")
    log = logs_of(row_ref[...])
    before = state_of(before_ref[...])
    before = pick(jnp.minimum(z, 1), jnp.zeros_like(before), before)
    out_ref[:STATE, :] = (jnp.exp(log) * before + state_ref[...]).astype(BF16)
    out_ref[STATE:, :] = log_block(log + logs_of(before_ref[...]))


def enter(before_ref, p2, p4, p6, all_ref, e0, e1, e2, e3, every):
    z = lax.axis_index("z")
    state = jnp.zeros((STATE, PART), F32)
    for gap, piece in ((6, p6), (4, p4), (2, p2), (1, before_ref)):
        there = pick(lax.div(z, gap), jnp.zeros_like(state), state_of(piece[...]))
        state = jnp.exp(logs_of(piece[...])) * state + there
    for x in range(4):
        every[x] = state.astype(BF16)
        if x < 3:
            state = jnp.exp(logs_of(all_ref[x])) * state + state_of(all_ref[x])
    for k, out in enumerate((e0, e1, e2, e3)):
        out[...] = every[place("x", k, 4)]


def core_states(f0, f1, f2, f3, keep_ref, came_ref, tot_ref, tot_other_ref, own_ref, give_ref, chip):
    for k, piece in enumerate((f0, f1, f2, f3)):
        chip[:, pl.ds(pl.multiple_of(place("x", -k, 4) * PART, PART), PART)] = piece[...]
    core = lax.axis_index("core")
    log0, _ = halves(core, tot_ref, tot_other_ref)
    first = chip[...].astype(F32)
    local = pick(core, keep_ref[...], came_ref[...].astype(F32))
    second = jnp.exp(log0) * first + local
    own_ref[...] = pick(core, first, second).astype(BF16)
    give_ref[...] = pick(core, second, first).astype(BF16)


def gate_all(own_ref, came_ref, c_ref, p_ref, q_ref, gated_ref, sums_ref):
    core = lax.axis_index("core")
    total = jnp.zeros((STRETCH, 128), F32)
    for half in range(2):
        for at in range(0, HALF, 256):
            own, came = own_ref[:, at:at + 256].astype(F32), came_ref[:, at:at + 256].astype(F32)
            state = (pick(core, own, came) if half == 0 else pick(core, came, own)).astype(BF16)
            carried = jnp.dot(c_ref[...], state, preferred_element_type=F32)
            to = half * HALF + at
            gated = p_ref[:, to:to + 256] + q_ref[:, to:to + 256] * carried
            gated_ref[:, to:to + 256] = gated
            square = gated * gated
            total = total + square[:, :128] + square[:, 128:]
    sums_ref[...] = jnp.broadcast_to(jnp.sum(total.T, axis=0, keepdims=True), (8, STRETCH))


def normalize(gated_ref, q0, q1, q2, q3, gain_ref, out_ref):
    total = q0[:1, :] + q1[:1, :] + q2[:1, :] + q3[:1, :]
    scale = lax.rsqrt(total / (HEADS * HEAD_DIM) + epsilon)
    scale = jnp.broadcast_to(scale, (128, STRETCH)).T
    for at in range(0, FEATS, 128):
        out_ref[:, at:at + 128] = (
            gated_ref[:, at:at + 128] * scale * gain_ref[:, at:at + 128]
        ).astype(BF16)


def shifted(v, axis, step, size):
    return lax.ppermute(v, axis, [(i, (i + step) % size) for i in range(size)])


def on_device(inputs, gate, in_b, in_c, log_decay, step_size, importance, skip, norm_gain):
    y = lax.axis_index("head")
    pieces = [
        lax.dynamic_slice(inputs, (0, lax.rem(y + k, 4) * FEATS), (64, FEATS)) for k in range(4)
    ]
    pieces = [pieces[0]] + [shifted(pieces[k], "head", k, 4) for k in (1, 2, 3)]

    big = (STRETCH, FEATS)
    weights, dt, dtt, q, g, b_t, tot = kernel_call(
        prepare,
        [((HERE, STRETCH, STRETCH), BF16), (big, F32), (big, F32), (big, F32), (big, F32),
         ((STATE, STRETCH), BF16), ((8, FEATS), F32)],
        log_decay, step_size, importance.reshape(1, STRETCH), in_b, in_c, gate,
        flops=4 << 30, bytes_accessed=12 << 20,
    )
    tot_other = shifted(tot, "core", 1, 2)
    x, keep, send = kernel_call(
        end_state,
        [(big, BF16), ((STATE, HALF), F32), ((STATE, HALF), BF16)],
        *pieces, dtt, b_t,
        scratch=[((STATE, FEATS), F32)],
        flops=1 << 28, bytes_accessed=4 << 20,
    )
    came = shifted(send, "core", 1, 2)
    skip_row = jnp.repeat(skip, HEAD_DIM).reshape(1, FEATS)
    (p,) = kernel_call(
        inside, [(big, F32)], x, dt, weights, g, skip_row, flops=2 << 30, bytes_accessed=11 << 20
    )

    message = (STATE + LOGS, PART)
    slices = kernel_call(
        chip_state, [(message, BF16)] * 4, keep, came, tot, tot_other,
        scratch=[((STATE + LOGS, HALF), BF16)],
    )
    slices = [slices[0]] + [shifted(slices[k], "x", k, 4) for k in (1, 2, 3)]
    chips, row, state = kernel_call(
        row_state, [((4,) + message, BF16), (message, BF16), ((STATE, PART), F32)], *slices
    )
    before = shifted(row, "z", 1, 8)
    (pair,) = kernel_call(window, [(message, BF16)], row, state, before)
    back = [shifted(pair, "z", k, 8) for k in (2, 4, 6)]
    enters = kernel_call(
        enter, [((STATE, PART), BF16)] * 4, before, *back, chips,
        scratch=[((4, STATE, PART), BF16)],
    )
    enters = [enters[0]] + [shifted(enters[k], "x", k, 4) for k in (1, 2, 3)]
    own, give = kernel_call(
        core_states, [((STATE, HALF), BF16)] * 2, *enters, keep, came, tot, tot_other,
        scratch=[((STATE, HALF), BF16)],
    )
    got = shifted(give, "core", 1, 2)
    gated, sums = kernel_call(
        gate_all, [(big, F32), ((8, STRETCH), F32)], own, got, in_c, p, q
    )
    others = [shifted(sums, "head", k, 4) for k in (1, 2, 3)]
    (out,) = kernel_call(
        normalize, [(big, BF16)], gated, sums, *others, norm_gain.reshape(1, FEATS)
    )
    return out


def solution(mesh):
    fine = Mesh(mesh.devices.reshape(8, 4, 2, 4), ("z", "x", "core", "head"))
    seq = ("z", "x", "core")
    in_specs = (
        P(seq + ("head",), None),
        P(seq, "head"),
        P(seq, None),
        P(seq, None),
        P("head", seq),
        P("head", seq),
        P(seq),
        P("head"),
        P("head"),
    )
    return jax.shard_map(
        on_device, mesh=fine, in_specs=in_specs, out_specs=P(seq, "head"), check_vma=False
    )
```

time: 438 us -> 74.4 us (0.17)
  the two profiles are of different devices: /device:TPU:231 before, /device:TPU:32 now
where the time goes in v1:
time: 74.4 us; the launch traced here: 73.9 us
  starting transfers between devices  33.6 us (45%)
  waiting for transfers between devices  22.5 us (30%)
  Pallas kernels  9.68 us (13%)
  local copies, waits for them, and re-layouts  7.86 us (11%)
    ppermute x19, starting transfers between devices, shifted(): return lax.ppermute(v, axis, [(i, (i + step) % size) for i in range(size)])  33.6 us
    ppermute x19, waiting for transfers between devices, shifted(): return lax.ppermute(v, axis, [(i, (i + step) % size) for i in range(size)])  22.5 us
    pallas_call x10, Pallas kernels, kernel_call(): pl.pallas_call(body, out_shape=[jax.ShapeDtypeStruct(s, d) for s, d in ou...  9.68 us
    unnamed x28, local copies, waits for them, and re-layouts  6.32 us
  transfers between devices with their start and end apart: 19, of which 13 were waited for; matrix products, arithmetic and copies ran while one was open for 0% of the time, Pallas kernels for 6%

profile of v1, /device:TPU:32, one launch (start us, length us, event | category | flops | bytes accessed | tf_op | source)
XLA Modules:
  0.0 73.9 jit_solution(1602880942158996998)
XLA Ops:
  0.0 0.0 copy-start.6
  0.0 0.0 copy-start.10
  0.0 0.0 copy-start.11
  0.1 1.4 %constant_dynamic-slice_fusion = (bf16[64,2048]{1,0:T(8,128)(2,1)S(1)}, bf16[64,2048]{1,0:T(8,128)(2,1)S(1)}, bf16[64,2048]{1,0:T(8,128)(2,1)S(1)}, bf16[64,2048]{1,0:T(8,128)(2,1)S(1)}) fusion(bf16[64,8192]{1,0:T(8,128)(2,1)} %param.9, s32[]{:T(128)S(6)} %select_n.15, s32[]{:T(128)S(6)} %select_n.13, s32[]{:T(128)S(6)} %select_n.12, s32[]{:T(128)S(6)} %select_n.14), kind=kLoop, calls=%fused_computation | loop fusion | bytes 2097168 | tf_op jit(solution)/shard_map/dynamic_slice | solution.py:264
  1.5 1.7 %collective-permute-start = (bf16[64,2048]{1,0:T(8,128)(2,1)S(1)}, bf16[64,2048]{1,0:T(8,128)(2,1)S(1)}, u32[]{:S(2)}, u32[]{:S(2)}) collective-permute-start(bf16[64,2048]{1,0:T(8,128)(2,1)S(1)} %get-tuple-element.56), channel_id=1, source_target_pairs={{0,1},{1,2},{2,3},{3,0},{4,5},{5,6},{6,7},{7,4},{8,9},{9,10},{10,1... | collective-permute-start | bytes 786440 | tf_op jit(solution)/shard_map/ppermute | solution.py:258
  3.1 2.9 %collective-permute-start.1 = (bf16[64,2048]{1,0:T(8,128)(2,1)S(1)}, bf16[64,2048]{1,0:T(8,128)(2,1)S(1)}, u32[]{:S(2)}, u32[]{:S(2)}) collective-permute-start(bf16[64,2048]{1,0:T(8,128)(2,1)S(1)} %get-tuple-element.58), channel_id=1, source_target_pairs={{0,2},{1,3},{2,0},{3,1},{4,6},{5,7},{6,4},{7,5},{8,10},{9,11},{10,... | collective-permute-start | bytes 786440 | tf_op jit(solution)/shard_map/ppermute | solution.py:258
  6.0 1.3 %collective-permute-start.2 = (bf16[64,2048]{1,0:T(8,128)(2,1)S(1)}, bf16[64,2048]{1,0:T(8,128)(2,1)S(1)}, u32[]{:S(2)}, u32[]{:S(2)}) collective-permute-start(bf16[64,2048]{1,0:T(8,128)(2,1)S(1)} %get-tuple-element.55), channel_id=1, source_target_pairs={{0,3},{1,0},{2,1},{3,2},{4,7},{5,4},{6,5},{7,6},{8,11},{9,8},{10,9... | collective-permute-start | bytes 786440 | tf_op jit(solution)/shard_map/ppermute | solution.py:258
  7.4 0.0 copy-done.12
  7.4 0.0 copy-done.8
  7.4 0.0 copy-done.9
  7.4 0.0 copy-done.6
  7.4 0.0 copy-done.10
  7.4 3.5 %shard_map.91 = (bf16[32,256,256]{2,1,0:T(8,128)(2,1)S(1)}, f32[256,2048]{1,0:T(8,128)S(1)}, f32[256,2048]{1,0:T(8,128)S(1)}, f32[256,2048]{1,0:T(8,128)S(1)}, f...) custom-call(f32[32,256]{1,0:T(8,128)S(1)} %copy-done.10, f32[32,256]{1,0:T(8,128)S(1)} %copy-done.11, ...), custom_call_target="tpu_custom_call" | custom-call | flops 4294967296 | bytes 12582912 | tf_op jit(solution)/shard_map/pallas_call | solution.py:27
  10.9 0.0 copy-start
  11.0 2.0 %copy-done = bf16[32,256,256]{2,1,0:T(8,128)(2,1)} copy-done((bf16[32,256,256]{2,1,0:T(8,128)(2,1)}, bf16[32,256,256]{2,1,0:T(8,128)(2,1)S(1)}, u32[]{:S(2)}) %copy-start) | copy-done | bytes 4194328
  12.9 0.0 collective-permute-done.x1
  12.9 4.7 %collective-permute-done.1.x2 = bf16[64,2048]{1,0:T(8,128)(2,1)S(1)} collective-permute-done((bf16[64,2048]{1,0:T(8,128)(2,1)S(1)}, bf16[64,2048]{1,0:T(8,128)(2,1)S(1)}, u32[]{:S(2)}, u32[]{:S(2)}) %collective-permute-start.1) | collective-permute-done | bytes 262176 | tf_op jit(solution)/shard_map/ppermute | solution.py:258
  17.6 0.0 collective-permute-done.2.x3
  17.7 0.6 shard_map.92
  18.3 0.0 copy-start.13
  18.3 0.1 collective-permute-start.3
  18.4 0.5 collective-permute-start.4
  18.9 1.1 %collective-permute-done.4.tot_other_ref = f32[8,2048]{1,0:T(8,128)S(1)} collective-permute-done((f32[8,2048]{1,0:T(8,128)S(1)}, f32[8,2048]{1,0:T(8,128)S(1)}, u32[]{:S(2)}, u32[]{:S(2)}) %collective-permute-start.4) | collective-permute-done | bytes 65568 | tf_op jit(solution)/shard_map/ppermute | solution.py:258
  20.0 0.0 collective-permute-done.3.came_ref
  20.0 0.3 shard_map.93
  20.3 1.6 %collective-permute-start.5 = (bf16[144,256]{1,0:T(8,128)(2,1)S(1)}, bf16[144,256]{1,0:T(8,128)(2,1)S(1)}, u32[]{:S(2)}, u32[]{:S(2)}) collective-permute-start(bf16[144,256]{1,0:T(8,128)(2,1)S(1)} %get-tuple-element.36), channel_id=1, source_target_pairs={{0,8},{8,16},{16,24},{24,0},{1,9},{9,17},{17,25},{25,1},{2,10},{10... | collective-permute-start | bytes 221192 | tf_op jit(solution)/shard_map/ppermute | solution.py:258
  21.9 2.7 %collective-permute-start.6 = (bf16[144,256]{1,0:T(8,128)(2,1)S(1)}, bf16[144,256]{1,0:T(8,128)(2,1)S(1)}, u32[]{:S(2)}, u32[]{:S(2)}) collective-permute-start(bf16[144,256]{1,0:T(8,128)(2,1)S(1)} %get-tuple-element.37), channel_id=1, source_target_pairs={{0,16},{8,24},{16,0},{24,8},{1,17},{9,25},{17,1},{25,9},{2,18},{10... | collective-permute-start | bytes 221192 | tf_op jit(solution)/shard_map/ppermute | solution.py:258
  24.6 1.4 %collective-permute-start.7 = (bf16[144,256]{1,0:T(8,128)(2,1)S(1)}, bf16[144,256]{1,0:T(8,128)(2,1)S(1)}, u32[]{:S(2)}, u32[]{:S(2)}) collective-permute-start(bf16[144,256]{1,0:T(8,128)(2,1)S(1)} %get-tuple-element.38), channel_id=1, source_target_pairs={{0,24},{8,0},{16,8},{24,16},{1,25},{9,1},{17,9},{25,17},{2,26},{10... | collective-permute-start | bytes 221192 | tf_op jit(solution)/shard_map/ppermute | solution.py:258
  26.1 0.0 collective-permute-done.5.m1
  26.1 2.4 %collective-permute-done.6.m2 = bf16[144,256]{1,0:T(8,128)(2,1)S(1)} collective-permute-done((bf16[144,256]{1,0:T(8,128)(2,1)S(1)}, bf16[144,256]{1,0:T(8,128)(2,1)S(1)}, u32[]{:S(2)}, u32[]{:S(2)}) %collective-permute-start.6) | collective-permute-done | bytes 73760 | tf_op jit(solution)/shard_map/ppermute | solution.py:258
  28.5 0.5 collective-permute-done.7.m3
  29.0 0.1 shard_map.94
  29.1 2.0 %collective-permute-start.8 = (bf16[144,256]{1,0:T(8,128)(2,1)S(1)}, bf16[144,256]{1,0:T(8,128)(2,1)S(1)}, u32[]{:S(2)}, u32[]{:S(2)}) collective-permute-start(bf16[144,256]{1,0:T(8,128)(2,1)S(1)} %get-tuple-element.39.row_ref), channel_id=1, source_target_pairs={{0,32},{32,64},{64,96},{96,128},{128,160},{160,192},{192,224},{224... | collective-permute-start | bytes 221192 | tf_op jit(solution)/shard_map/ppermute | solution.py:258
  31.1 2.4 %collective-permute-done.8.before_ref = bf16[144,256]{1,0:T(8,128)(2,1)S(1)} collective-permute-done((bf16[144,256]{1,0:T(8,128)(2,1)S(1)}, bf16[144,256]{1,0:T(8,128)(2,1)S(1)}, u32[]{:S(2)}, u32[]{:S(2)}) %collective-permute-start.8) | collective-permute-done | bytes 73760 | tf_op jit(solution)/shard_map/ppermute | solution.py:258
  33.6 6.4 %collective-permute-start.10 = (bf16[144,256]{1,0:T(8,128)(2,1)S(1)}, bf16[144,256]{1,0:T(8,128)(2,1)S(1)}, u32[]{:S(2)}, u32[]{:S(2)}) collective-permute-start(bf16[144,256]{1,0:T(8,128)(2,1)S(1)} %shard_map.95), channel_id=1, source_target_pairs={{0,128},{32,160},{64,192},{96,224},{128,0},{160,32},{192,64},{224,... | collective-permute-start | bytes 221192 | tf_op jit(solution)/shard_map/ppermute | solution.py:258
  40.0 1.3 %collective-permute-start.11 = (bf16[144,256]{1,0:T(8,128)(2,1)S(1)}, bf16[144,256]{1,0:T(8,128)(2,1)S(1)}, u32[]{:S(2)}, u32[]{:S(2)}) collective-permute-start(bf16[144,256]{1,0:T(8,128)(2,1)S(1)} %shard_map.95), channel_id=1, source_target_pairs={{0,192},{32,224},{64,0},{96,32},{128,64},{160,96},{192,128},{224,1... | collective-permute-start | bytes 221192 | tf_op jit(solution)/shard_map/ppermute | solution.py:258
  41.3 1.6 %collective-permute-start.9 = (bf16[144,256]{1,0:T(8,128)(2,1)S(1)}, bf16[144,256]{1,0:T(8,128)(2,1)S(1)}, u32[]{:S(2)}, u32[]{:S(2)}) collective-permute-start(bf16[144,256]{1,0:T(8,128)(2,1)S(1)} %shard_map.95), channel_id=1, source_target_pairs={{0,64},{32,96},{64,128},{96,160},{128,192},{160,224},{192,0},{224,... | collective-permute-start | bytes 221192 | tf_op jit(solution)/shard_map/ppermute | solution.py:258
  42.9 0.8 %collective-permute-done.10.p4 = bf16[144,256]{1,0:T(8,128)(2,1)S(1)} collective-permute-done((bf16[144,256]{1,0:T(8,128)(2,1)S(1)}, bf16[144,256]{1,0:T(8,128)(2,1)S(1)}, u32[]{:S(2)}, u32[]{:S(2)}) %collective-permute-start.10) | collective-permute-done | bytes 73760 | tf_op jit(solution)/shard_map/ppermute | solution.py:258
  43.7 1.9 %collective-permute-done.11.p6 = bf16[144,256]{1,0:T(8,128)(2,1)S(1)} collective-permute-done((bf16[144,256]{1,0:T(8,128)(2,1)S(1)}, bf16[144,256]{1,0:T(8,128)(2,1)S(1)}, u32[]{:S(2)}, u32[]{:S(2)}) %collective-permute-start.11) | collective-permute-done | bytes 73760 | tf_op jit(solution)/shard_map/ppermute | solution.py:258
  45.5 3.0 %collective-permute-done.9.p2 = bf16[144,256]{1,0:T(8,128)(2,1)S(1)} collective-permute-done((bf16[144,256]{1,0:T(8,128)(2,1)S(1)}, bf16[144,256]{1,0:T(8,128)(2,1)S(1)}, u32[]{:S(2)}, u32[]{:S(2)}) %collective-permute-start.9) | collective-permute-done | bytes 73760 | tf_op jit(solution)/shard_map/ppermute | solution.py:258
  48.5 0.2 shard_map.96
  48.7 0.9 %collective-permute-start.12 = (bf16[128,256]{1,0:T(8,128)(2,1)S(1)}, bf16[128,256]{1,0:T(8,128)(2,1)S(1)}, u32[]{:S(2)}, u32[]{:S(2)}) collective-permute-start(bf16[128,256]{1,0:T(8,128)(2,1)S(1)} %get-tuple-element.43), channel_id=1, source_target_pairs={{0,8},{8,16},{16,24},{24,0},{1,9},{9,17},{17,25},{25,1},{2,10},{10... | collective-permute-start | bytes 196616 | tf_op jit(solution)/shard_map/ppermute | solution.py:258
  49.6 3.3 %collective-permute-start.13 = (bf16[128,256]{1,0:T(8,128)(2,1)S(1)}, bf16[128,256]{1,0:T(8,128)(2,1)S(1)}, u32[]{:S(2)}, u32[]{:S(2)}) collective-permute-start(bf16[128,256]{1,0:T(8,128)(2,1)S(1)} %get-tuple-element.44), channel_id=1, source_target_pairs={{0,16},{8,24},{16,0},{24,8},{1,17},{9,25},{17,1},{25,9},{2,18},{10... | collective-permute-start | bytes 196616 | tf_op jit(solution)/shard_map/ppermute | solution.py:258
  52.9 0.6 collective-permute-start.14
  53.5 0.7 collective-permute-done.12.f1
  54.3 1.6 %collective-permute-done.13.f2 = bf16[128,256]{1,0:T(8,128)(2,1)S(1)} collective-permute-done((bf16[128,256]{1,0:T(8,128)(2,1)S(1)}, bf16[128,256]{1,0:T(8,128)(2,1)S(1)}, u32[]{:S(2)}, u32[]{:S(2)}) %collective-permute-start.13) | collective-permute-done | bytes 65568 | tf_op jit(solution)/shard_map/ppermute | solution.py:258
  55.8 1.3 %collective-permute-done.14.f3 = bf16[128,256]{1,0:T(8,128)(2,1)S(1)} collective-permute-done((bf16[128,256]{1,0:T(8,128)(2,1)S(1)}, bf16[128,256]{1,0:T(8,128)(2,1)S(1)}, u32[]{:S(2)}, u32[]{:S(2)}) %collective-permute-start.14) | collective-permute-done | bytes 65568 | tf_op jit(solution)/shard_map/ppermute | solution.py:258
  57.2 1.0 %shard_map.97 = (bf16[128,1024]{1,0:T(8,128)(2,1)S(1)}, bf16[128,1024]{1,0:T(8,128)(2,1)}) custom-call(bf16[128,256]{1,0:T(8,128)(2,1)S(1)} %get-tuple-element.42.f0, bf16[128,256]{1,0:T(8,128)(2,1)S(1)} %collective-permute-done.12.f1, bf16[128,256]{1,0:T(8,128)(2,1)S(1)} %collective-permute-done.13.f2, bf16[128,256]{1,0:T(8,128)(2,1)S(1)} %collective-permute-done.14.f3, ...), custom_call_target="tpu_custom_call" | custom-call | tf_op jit(solution)/shard_map/pallas_call | solution.py:27
  58.2 0.0 collective-permute-start.15
  58.2 0.1 broadcast_in_dim.3
  58.2 0.1 reshape_reshape.3.skip_ref
  58.3 2.2 %copy-done.1 = bf16[32,256,256]{2,1,0:T(8,128)(2,1)S(1)} copy-done((bf16[32,256,256]{2,1,0:T(8,128)(2,1)S(1)}, bf16[32,256,256]{2,1,0:T(8,128)(2,1)}, u32[]{:S(2)}) %copy-start.1) | copy-done | bytes 4194328
  60.5 1.6 %copy-done.3 = f32[256,2048]{1,0:T(8,128)S(1)} copy-done((f32[256,2048]{1,0:T(8,128)S(1)}, f32[256,2048]{1,0:T(8,128)}, u32[]{:S(2)}) %copy-start.3) | copy-done | bytes 2097176
  62.1 1.0 %shard_map.98.p_ref = f32[256,2048]{1,0:T(8,128)S(1)} custom-call(bf16[256,2048]{1,0:T(8,128)(2,1)S(1)} %get-tuple-element.48.x_ref, f32[256,2048]{1,0:T(8,128)S(1)} %get-tuple-element.49.dt_ref, bf16[32,256,256]{2,1,0:T(8,128)(2,1)S(1)} %copy-done.1, f32[256,2048]{1,0:T(8,128)S(1)} %copy-done.3, f32[1,2048]{1,0:T(1,128)S(1)} %reshape_reshape.3.skip_ref), custom_call_target="tpu_custom_call" | custom-call | flops 2147483648 | bytes 11534336 | tf_op jit(solution)/shard_map/pallas_call | solution.py:27
  63.2 0.0 collective-permute-done.15.came_ref
  63.2 0.5 copy-done.5
  63.7 1.5 %shard_map.99 = (f32[256,2048]{1,0:T(8,128)S(1)}, f32[8,256]{1,0:T(8,128)S(1)}) custom-call(bf16[128,1024]{1,0:T(8,128)(2,1)S(1)} %get-tuple-element.46.own_ref, bf16[128,1024]{1,0:T(8,128)(2,1)} %collective-permute-done.15.came_ref, bf16[256,128]{1,0:T(8,128)(2,1)S(1)} %copy-done.6, f32[256,2048]{1,0:T(8,128)S(1)} %shard_map.98.p_ref, f32[256,2048]{1,0:T(8,128)S(1)} %copy-done.5), custom_call_target="tpu_custom_call" | custom-call | tf_op jit(solution)/shard_map/pallas_call | solution.py:27
  65.2 1.3 %collective-permute-start.16 = (f32[8,256]{1,0:T(8,128)S(1)}, f32[8,256]{1,0:T(8,128)S(1)}, u32[]{:S(2)}, u32[]{:S(2)}) collective-permute-start(f32[8,256]{1,0:T(8,128)S(1)} %get-tuple-element.54.q0), channel_id=1, source_target_pairs={{0,1},{1,2},{2,3},{3,0},{4,5},{5,6},{6,7},{7,4},{8,9},{9,10},{10,1... | collective-permute-start | bytes 24584 | tf_op jit(solution)/shard_map/ppermute | solution.py:258
  66.6 2.4 %collective-permute-start.17 = (f32[8,256]{1,0:T(8,128)S(1)}, f32[8,256]{1,0:T(8,128)S(1)}, u32[]{:S(2)}, u32[]{:S(2)}) collective-permute-start(f32[8,256]{1,0:T(8,128)S(1)} %get-tuple-element.54.q0), channel_id=1, source_target_pairs={{0,2},{1,3},{2,0},{3,1},{4,6},{5,7},{6,4},{7,5},{8,10},{9,11},{10,... | collective-permute-start | bytes 24584 | tf_op jit(solution)/shard_map/ppermute | solution.py:258
  68.9 1.6 %collective-permute-start.18 = (f32[8,256]{1,0:T(8,128)S(1)}, f32[8,256]{1,0:T(8,128)S(1)}, u32[]{:S(2)}, u32[]{:S(2)}) collective-permute-start(f32[8,256]{1,0:T(8,128)S(1)} %get-tuple-element.54.q0), channel_id=1, source_target_pairs={{0,3},{1,0},{2,1},{3,2},{4,7},{5,4},{6,5},{7,6},{8,11},{9,8},{10,9... | collective-permute-start | bytes 24584 | tf_op jit(solution)/shard_map/ppermute | solution.py:258
  70.5 0.0 collective-permute-done.16.q1
  70.5 1.2 %collective-permute-done.17.q2 = f32[8,256]{1,0:T(8,128)S(1)} collective-permute-done((f32[8,256]{1,0:T(8,128)S(1)}, f32[8,256]{1,0:T(8,128)S(1)}, u32[]{:S(2)}, u32[]{:S(2)}) %collective-permute-start.17) | collective-permute-done | bytes 8224 | tf_op jit(solution)/shard_map/ppermute | solution.py:258
  71.7 0.9 %collective-permute-done.18.q3 = f32[8,256]{1,0:T(8,128)S(1)} collective-permute-done((f32[8,256]{1,0:T(8,128)S(1)}, f32[8,256]{1,0:T(8,128)S(1)}, u32[]{:S(2)}, u32[]{:S(2)}) %collective-permute-start.18) | collective-permute-done | bytes 8224 | tf_op jit(solution)/shard_map/ppermute | solution.py:258
  72.6 1.3 %shard_map.100 = bf16[256,2048]{1,0:T(8,128)(2,1)} custom-call(f32[256,2048]{1,0:T(8,128)S(1)} %get-tuple-element.53.gated_ref, f32[8,256]{1,0:T(8,128)S(1)} %get-tuple-element.54.q0, f32[8,256]{1,0:T(8,128)S(1)} %collective-permute-done.16.q1, f32[8,256]{1,0:T(8,128)S(1)} %collective-permute-done.17.q2, f32[8,256]{1,0:T(8,128)S(1)} %collective-permute-done.18.q3, ...), custom_call_target="tpu_custom_call" | custom-call | tf_op jit(solution)/shard_map/pallas_call | solution.py:27
  (15 shorter events, 0.1 us)
Async XLA Ops:
  0.0 7.4 %copy-start.12 = (f32[256]{0:T(256)S(1)}, f32[256]{0:T(256)}, u32[]{:S(2)}) copy-start(f32[256]{0:T(256)} %param.15) | copy-start | bytes 3076
  0.0 7.4 %copy-start.8 = (bf16[256,2048]{1,0:T(8,128)(2,1)S(1)}, bf16[256,2048]{1,0:T(8,128)(2,1)}, u32[]{:S(2)}) copy-start(bf16[256,2048]{1,0:T(8,128)(2,1)} %gate_ref.1) | copy-start | bytes 3145732
  0.0 7.4 %copy-start.9 = (bf16[256,128]{1,0:T(8,128)(2,1)S(1)}, bf16[256,128]{1,0:T(8,128)(2,1)}, u32[]{:S(2)}) copy-start(bf16[256,128]{1,0:T(8,128)(2,1)} %b_ref.1) | copy-start | bytes 196612
  0.0 7.4 %copy-start.6 = (bf16[256,128]{1,0:T(8,128)(2,1)S(1)}, bf16[256,128]{1,0:T(8,128)(2,1)}, u32[]{:S(2)}) copy-start(bf16[256,128]{1,0:T(8,128)(2,1)} %c_ref.3) | copy-start | bytes 196612
  0.0 7.4 %copy-start.10 = (f32[32,256]{1,0:T(8,128)S(1)}, f32[32,256]{1,0:T(8,128)}, u32[]{:S(2)}) copy-start(f32[32,256]{1,0:T(8,128)} %log_ref.1) | copy-start | bytes 98308
  0.0 7.4 %copy-start.11 = (f32[32,256]{1,0:T(8,128)S(1)}, f32[32,256]{1,0:T(8,128)}, u32[]{:S(2)}) copy-start(f32[32,256]{1,0:T(8,128)} %step_ref.1) | copy-start | bytes 98308
  1.5 11.5 %collective-permute-start = (bf16[64,2048]{1,0:T(8,128)(2,1)S(1)}, bf16[64,2048]{1,0:T(8,128)(2,1)S(1)}, u32[]{:S(2)}, u32[]{:S(2)}) collective-permute-start(bf16[64,2048]{1,0:T(8,128)(2,1)S(1)} %get-tuple-element.56), channel_id=1, source_target_pairs={{0,1},{1,2},{2,3},{3,0},{4,5},{5,6},{6,7},{7,4},{8,9},{9,10},{10,1... | collective-permute-start | bytes 786440 | tf_op jit(solution)/shard_map/ppermute | solution.py:258
  3.1 14.5 %collective-permute-start.1 = (bf16[64,2048]{1,0:T(8,128)(2,1)S(1)}, bf16[64,2048]{1,0:T(8,128)(2,1)S(1)}, u32[]{:S(2)}, u32[]{:S(2)}) collective-permute-start(bf16[64,2048]{1,0:T(8,128)(2,1)S(1)} %get-tuple-element.58), channel_id=1, source_target_pairs={{0,2},{1,3},{2,0},{3,1},{4,6},{5,7},{6,4},{7,5},{8,10},{9,11},{10,... | collective-permute-start | bytes 786440 | tf_op jit(solution)/shard_map/ppermute | solution.py:258
  6.0 11.6 %collective-permute-start.2 = (bf16[64,2048]{1,0:T(8,128)(2,1)S(1)}, bf16[64,2048]{1,0:T(8,128)(2,1)S(1)}, u32[]{:S(2)}, u32[]{:S(2)}) collective-permute-start(bf16[64,2048]{1,0:T(8,128)(2,1)S(1)} %get-tuple-element.55), channel_id=1, source_target_pairs={{0,3},{1,0},{2,1},{3,2},{4,7},{5,4},{6,5},{7,6},{8,11},{9,8},{10,9... | collective-permute-start | bytes 786440 | tf_op jit(solution)/shard_map/ppermute | solution.py:258
  10.9 2.0 %copy-start = (bf16[32,256,256]{2,1,0:T(8,128)(2,1)}, bf16[32,256,256]{2,1,0:T(8,128)(2,1)S(1)}, u32[]{:S(2)}) copy-start(bf16[32,256,256]{2,1,0:T(8,128)(2,1)S(1)} %get-tuple-element.50.w_ref) | copy-start | bytes 12582916
  12.9 16.2 %copy-start.2 = (f32[256,2048]{1,0:T(8,128)}, f32[256,2048]{1,0:T(8,128)S(1)}, u32[]{:S(2)}) copy-start(f32[256,2048]{1,0:T(8,128)S(1)} %get-tuple-element.51.g_ref) | copy-start | bytes 6291460
  12.9 16.2 %copy-start.4 = (f32[256,2048]{1,0:T(8,128)}, f32[256,2048]{1,0:T(8,128)S(1)}, u32[]{:S(2)}) copy-start(f32[256,2048]{1,0:T(8,128)S(1)} %get-tuple-element.52.q_ref) | copy-start | bytes 6291460
  18.3 39.9 %copy-start.13 = (f32[32]{0:T(128)S(1)}, f32[32]{0:T(128)}, u32[]{:S(2)}) copy-start(f32[32]{0:T(128)} %param.16) | copy-start | bytes 388
  18.3 1.7 %collective-permute-start.3 = (bf16[128,1024]{1,0:T(8,128)(2,1)S(1)}, bf16[128,1024]{1,0:T(8,128)(2,1)S(1)}, u32[]{:S(2)}, u32[]{:S(2)}) collective-permute-start(bf16[128,1024]{1,0:T(8,128)(2,1)S(1)} %get-tuple-element.33), channel_id=1, source_target_pairs={{0,4},{4,0},{1,5},{5,1},{2,6},{6,2},{3,7},{7,3},{8,12},{12,8},{9,1... | collective-permute-start | bytes 786440 | tf_op jit(solution)/shard_map/ppermute | solution.py:258
  18.4 1.6 %collective-permute-start.4 = (f32[8,2048]{1,0:T(8,128)S(1)}, f32[8,2048]{1,0:T(8,128)S(1)}, u32[]{:S(2)}, u32[]{:S(2)}) collective-permute-start(f32[8,2048]{1,0:T(8,128)S(1)} %get-tuple-element.34.tot_ref), channel_id=1, source_target_pairs={{0,4},{4,0},{1,5},{5,1},{2,6},{6,2},{3,7},{7,3},{8,12},{12,8},{9,1... | collective-permute-start | bytes 196616 | tf_op jit(solution)/shard_map/ppermute | solution.py:258
  20.3 5.7 %collective-permute-start.5 = (bf16[144,256]{1,0:T(8,128)(2,1)S(1)}, bf16[144,256]{1,0:T(8,128)(2,1)S(1)}, u32[]{:S(2)}, u32[]{:S(2)}) collective-permute-start(bf16[144,256]{1,0:T(8,128)(2,1)S(1)} %get-tuple-element.36), channel_id=1, source_target_pairs={{0,8},{8,16},{16,24},{24,0},{1,9},{9,17},{17,25},{25,1},{2,10},{10... | collective-permute-start | bytes 221192 | tf_op jit(solution)/shard_map/ppermute | solution.py:258
  21.9 6.6 %collective-permute-start.6 = (bf16[144,256]{1,0:T(8,128)(2,1)S(1)}, bf16[144,256]{1,0:T(8,128)(2,1)S(1)}, u32[]{:S(2)}, u32[]{:S(2)}) collective-permute-start(bf16[144,256]{1,0:T(8,128)(2,1)S(1)} %get-tuple-element.37), channel_id=1, source_target_pairs={{0,16},{8,24},{16,0},{24,8},{1,17},{9,25},{17,1},{25,9},{2,18},{10... | collective-permute-start | bytes 221192 | tf_op jit(solution)/shard_map/ppermute | solution.py:258
  24.6 4.4 %collective-permute-start.7 = (bf16[144,256]{1,0:T(8,128)(2,1)S(1)}, bf16[144,256]{1,0:T(8,128)(2,1)S(1)}, u32[]{:S(2)}, u32[]{:S(2)}) collective-permute-start(bf16[144,256]{1,0:T(8,128)(2,1)S(1)} %get-tuple-element.38), channel_id=1, source_target_pairs={{0,24},{8,0},{16,8},{24,16},{1,25},{9,1},{17,9},{25,17},{2,26},{10... | collective-permute-start | bytes 221192 | tf_op jit(solution)/shard_map/ppermute | solution.py:258
  29.1 4.4 %collective-permute-start.8 = (bf16[144,256]{1,0:T(8,128)(2,1)S(1)}, bf16[144,256]{1,0:T(8,128)(2,1)S(1)}, u32[]{:S(2)}, u32[]{:S(2)}) collective-permute-start(bf16[144,256]{1,0:T(8,128)(2,1)S(1)} %get-tuple-element.39.row_ref), channel_id=1, source_target_pairs={{0,32},{32,64},{64,96},{96,128},{128,160},{160,192},{192,224},{224... | collective-permute-start | bytes 221192 | tf_op jit(solution)/shard_map/ppermute | solution.py:258
  33.6 10.1 %collective-permute-start.10 = (bf16[144,256]{1,0:T(8,128)(2,1)S(1)}, bf16[144,256]{1,0:T(8,128)(2,1)S(1)}, u32[]{:S(2)}, u32[]{:S(2)}) collective-permute-start(bf16[144,256]{1,0:T(8,128)(2,1)S(1)} %shard_map.95), channel_id=1, source_target_pairs={{0,128},{32,160},{64,192},{96,224},{128,0},{160,32},{192,64},{224,... | collective-permute-start | bytes 221192 | tf_op jit(solution)/shard_map/ppermute | solution.py:258
  40.0 5.6 %collective-permute-start.11 = (bf16[144,256]{1,0:T(8,128)(2,1)S(1)}, bf16[144,256]{1,0:T(8,128)(2,1)S(1)}, u32[]{:S(2)}, u32[]{:S(2)}) collective-permute-start(bf16[144,256]{1,0:T(8,128)(2,1)S(1)} %shard_map.95), channel_id=1, source_target_pairs={{0,192},{32,224},{64,0},{96,32},{128,64},{160,96},{192,128},{224,1... | collective-permute-start | bytes 221192 | tf_op jit(solution)/shard_map/ppermute | solution.py:258
  41.3 7.3 %collective-permute-start.9 = (bf16[144,256]{1,0:T(8,128)(2,1)S(1)}, bf16[144,256]{1,0:T(8,128)(2,1)S(1)}, u32[]{:S(2)}, u32[]{:S(2)}) collective-permute-start(bf16[144,256]{1,0:T(8,128)(2,1)S(1)} %shard_map.95), channel_id=1, source_target_pairs={{0,64},{32,96},{64,128},{96,160},{128,192},{160,224},{192,0},{224,... | collective-permute-start | bytes 221192 | tf_op jit(solution)/shard_map/ppermute | solution.py:258
  48.7 5.6 %collective-permute-start.12 = (bf16[128,256]{1,0:T(8,128)(2,1)S(1)}, bf16[128,256]{1,0:T(8,128)(2,1)S(1)}, u32[]{:S(2)}, u32[]{:S(2)}) collective-permute-start(bf16[128,256]{1,0:T(8,128)(2,1)S(1)} %get-tuple-element.43), channel_id=1, source_target_pairs={{0,8},{8,16},{16,24},{24,0},{1,9},{9,17},{17,25},{25,1},{2,10},{10... | collective-permute-start | bytes 196616 | tf_op jit(solution)/shard_map/ppermute | solution.py:258
  49.6 6.2 %collective-permute-start.13 = (bf16[128,256]{1,0:T(8,128)(2,1)S(1)}, bf16[128,256]{1,0:T(8,128)(2,1)S(1)}, u32[]{:S(2)}, u32[]{:S(2)}) collective-permute-start(bf16[128,256]{1,0:T(8,128)(2,1)S(1)} %get-tuple-element.44), channel_id=1, source_target_pairs={{0,16},{8,24},{16,0},{24,8},{1,17},{9,25},{17,1},{25,9},{2,18},{10... | collective-permute-start | bytes 196616 | tf_op jit(solution)/shard_map/ppermute | solution.py:258
  52.9 4.3 %collective-permute-start.14 = (bf16[128,256]{1,0:T(8,128)(2,1)S(1)}, bf16[128,256]{1,0:T(8,128)(2,1)S(1)}, u32[]{:S(2)}, u32[]{:S(2)}) collective-permute-start(bf16[128,256]{1,0:T(8,128)(2,1)S(1)} %get-tuple-element.45), channel_id=1, source_target_pairs={{0,24},{8,0},{16,8},{24,16},{1,25},{9,1},{17,9},{25,17},{2,26},{10... | collective-permute-start | bytes 196616 | tf_op jit(solution)/shard_map/ppermute | solution.py:258
  58.2 5.0 %collective-permute-start.15 = (bf16[128,1024]{1,0:T(8,128)(2,1)}, bf16[128,1024]{1,0:T(8,128)(2,1)}, u32[]{:S(2)}, u32[]{:S(2)}) collective-permute-start(bf16[128,1024]{1,0:T(8,128)(2,1)} %get-tuple-element.47), channel_id=1, source_target_pairs={{0,4},{4,0},{1,5},{5,1},{2,6},{6,2},{3,7},{7,3},{8,12},{12,8},{9,1... | collective-permute-start | bytes 786440 | tf_op jit(solution)/shard_map/ppermute | solution.py:258
  58.3 2.2 %copy-start.1 = (bf16[32,256,256]{2,1,0:T(8,128)(2,1)S(1)}, bf16[32,256,256]{2,1,0:T(8,128)(2,1)}, u32[]{:S(2)}) copy-start(bf16[32,256,256]{2,1,0:T(8,128)(2,1)} %copy-done) | copy-start | bytes 12582916
  60.5 1.6 %copy-start.3 = (f32[256,2048]{1,0:T(8,128)S(1)}, f32[256,2048]{1,0:T(8,128)}, u32[]{:S(2)}) copy-start(f32[256,2048]{1,0:T(8,128)} %copy-done.2) | copy-start | bytes 6291460
  62.1 1.6 %copy-start.5 = (f32[256,2048]{1,0:T(8,128)S(1)}, f32[256,2048]{1,0:T(8,128)}, u32[]{:S(2)}) copy-start(f32[256,2048]{1,0:T(8,128)} %copy-done.4) | copy-start | bytes 6291460
  63.7 8.9 %copy-start.7 = (f32[2048]{0:T(1024)S(1)}, f32[2048]{0:T(1024)}, u32[]{:S(2)}) copy-start(f32[2048]{0:T(1024)} %param.17) | copy-start | bytes 24580
  65.2 5.3 %collective-permute-start.16 = (f32[8,256]{1,0:T(8,128)S(1)}, f32[8,256]{1,0:T(8,128)S(1)}, u32[]{:S(2)}, u32[]{:S(2)}) collective-permute-start(f32[8,256]{1,0:T(8,128)S(1)} %get-tuple-element.54.q0), channel_id=1, source_target_pairs={{0,1},{1,2},{2,3},{3,0},{4,5},{5,6},{6,7},{7,4},{8,9},{9,10},{10,1... | collective-permute-start | bytes 24584 | tf_op jit(solution)/shard_map/ppermute | solution.py:258
  66.6 5.2 %collective-permute-start.17 = (f32[8,256]{1,0:T(8,128)S(1)}, f32[8,256]{1,0:T(8,128)S(1)}, u32[]{:S(2)}, u32[]{:S(2)}) collective-permute-start(f32[8,256]{1,0:T(8,128)S(1)} %get-tuple-element.54.q0), channel_id=1, source_target_pairs={{0,2},{1,3},{2,0},{3,1},{4,6},{5,7},{6,4},{7,5},{8,10},{9,11},{10,... | collective-permute-start | bytes 24584 | tf_op jit(solution)/shard_map/ppermute | solution.py:258
  68.9 3.7 %collective-permute-start.18 = (f32[8,256]{1,0:T(8,128)S(1)}, f32[8,256]{1,0:T(8,128)S(1)}, u32[]{:S(2)}, u32[]{:S(2)}) collective-permute-start(f32[8,256]{1,0:T(8,128)S(1)} %get-tuple-element.54.q0), channel_id=1, source_target_pairs={{0,3},{1,0},{2,1},{3,2},{4,7},{5,4},{6,5},{7,6},{8,11},{9,8},{10,9... | collective-permute-start | bytes 24584 | tf_op jit(solution)/shard_map/ppermute | solution.py:258

commit v2 on v1

--- a/solution.py
+++ b/solution.py
@@ -22,19 +22,24 @@
 LOGS = 16
 
 
-def kernel_call(body, outs, *args, scratch=(), flops=0, bytes_accessed=0):
+def kernel_call(body, outs, *args, scratch=(), after=(), flops=0, bytes_accessed=0):
     vmem = pl.BlockSpec(memory_space=pltpu.VMEM)
+    count = len(args)
+
+    def ordered(*refs):
+        body(*refs[:count], *refs[count + len(after):])
+
     return pl.pallas_call(
-        body,
+        ordered,
         out_shape=[jax.ShapeDtypeStruct(s, d) for s, d in outs],
-        in_specs=[vmem] * len(args),
+        in_specs=[vmem] * count + [pl.BlockSpec(memory_space=pl.ANY)] * len(after),
         out_specs=[vmem] * len(outs),
         scratch_shapes=[pltpu.VMEM(s, d) for s, d in scratch],
-        compiler_params=pltpu.CompilerParams(vmem_limit_bytes=40 * 1024 * 1024),
+        compiler_params=pltpu.CompilerParams(vmem_limit_bytes=20 * 1024 * 1024),
         cost_estimate=pl.CostEstimate(
             flops=flops, bytes_accessed=bytes_accessed, transcendentals=0
         ),
-    )(*args)
+    )(*args, *after)
 
 
 def three_terms(v):
@@ -67,8 +72,19 @@
     return message[:STATE, :].astype(F32)
 
 
-def prepare(log_ref, step_ref, imp_ref, b_ref, c_ref, gate_ref,
-            w_ref, dt_ref, dtt_ref, q_ref, g_ref, bt_ref, tot_ref):
+def cut(x_ref, s0, s1, s2, s3, sems):
+    copies = []
+    for k, out in enumerate((s0, s1, s2, s3)):
+        at = pl.multiple_of(place("head", k, 4) * FEATS, FEATS)
+        copies.append(pltpu.make_async_copy(x_ref.at[:, pl.ds(at, FEATS)], out, sems.at[k]))
+    for copy in copies:
+        copy.start()
+    for copy in copies:
+        copy.wait()
+
+
+def prepare(log_ref, step_ref, imp_ref, b_ref, c_ref, gate_ref, skip_ref,
+            w_ref, dt_ref, dtt_ref, q_ref, g_ref, bt_ref, tot_ref, skip_row_ref):
     lane = lax.broadcasted_iota(jnp.int32, (HERE, STRETCH), 1)
     cum = log_ref[...]
     shift = 1
@@ -109,6 +125,9 @@
     logs = columns(cum)
     last = jnp.broadcast_to(logs[STRETCH - 16:, :][15:, :], (16, 128))
     tot_ref[...] = jnp.dot(last, spread, preferred_element_type=F32)[:8]
+    hi, mid, lo = three_terms(jnp.broadcast_to(skip_ref[...], (16, HERE)))
+    skip = jnp.concatenate([hi, mid, lo, jnp.zeros_like(hi)], axis=1).astype(BF16)
+    skip_row_ref[...] = jnp.dot(skip, spread, preferred_element_type=F32)[:8]
     bt_ref[...] = b_ref[...].astype(F32).T.astype(BF16)
 
     scores = lax.dot_general(
@@ -156,7 +175,7 @@
         top += jnp.dot(w_ref[2 * j + 1, :128, :128], two[:128], preferred_element_type=F32)
         low = jnp.dot(w_ref[2 * j, 128:, :], one, preferred_element_type=F32)
         low += jnp.dot(w_ref[2 * j + 1, 128:, :], two, preferred_element_type=F32)
-        skip = skip_ref[:, at]
+        skip = skip_ref[:1, at]
         p_ref[:128, at] = (top + skip * x[:128]) * g_ref[:128, at]
         p_ref[128:, at] = (low + skip * x[128:]) * g_ref[128:, at]
 
@@ -228,19 +247,17 @@
     give_ref[...] = pick(core, second, first).astype(BF16)
 
 
-def gate_all(own_ref, came_ref, c_ref, p_ref, q_ref, gated_ref, sums_ref):
+def gate_all(own_ref, came_ref, c_ref, p_ref, q_ref, gated_ref, sums_ref, states):
     core = lax.axis_index("core")
+    states[:, pl.ds(pl.multiple_of(core * HALF, HALF), HALF)] = own_ref[...]
+    states[:, pl.ds(pl.multiple_of((1 - core) * HALF, HALF), HALF)] = came_ref[...]
     total = jnp.zeros((STRETCH, 128), F32)
-    for half in range(2):
-        for at in range(0, HALF, 256):
-            own, came = own_ref[:, at:at + 256].astype(F32), came_ref[:, at:at + 256].astype(F32)
-            state = (pick(core, own, came) if half == 0 else pick(core, came, own)).astype(BF16)
-            carried = jnp.dot(c_ref[...], state, preferred_element_type=F32)
-            to = half * HALF + at
-            gated = p_ref[:, to:to + 256] + q_ref[:, to:to + 256] * carried
-            gated_ref[:, to:to + 256] = gated
-            square = gated * gated
-            total = total + square[:, :128] + square[:, 128:]
+    for at in range(0, FEATS, 256):
+        carried = jnp.dot(c_ref[...], states[:, at:at + 256], preferred_element_type=F32)
+        gated = p_ref[:, at:at + 256] + q_ref[:, at:at + 256] * carried
+        gated_ref[:, at:at + 256] = gated
+        square = gated * gated
+        total = total + square[:, :128] + square[:, 128:]
     sums_ref[...] = jnp.broadcast_to(jnp.sum(total.T, axis=0, keepdims=True), (8, STRETCH))
 
 
@@ -259,18 +276,23 @@
 
 
 def on_device(inputs, gate, in_b, in_c, log_decay, step_size, importance, skip, norm_gain):
-    y = lax.axis_index("head")
-    pieces = [
-        lax.dynamic_slice(inputs, (0, lax.rem(y + k, 4) * FEATS), (64, FEATS)) for k in range(4)
-    ]
+    pieces = pl.pallas_call(
+        cut,
+        out_shape=[jax.ShapeDtypeStruct((64, FEATS), BF16)] * 4,
+        in_specs=[pl.BlockSpec(memory_space=pl.ANY)],
+        out_specs=[pl.BlockSpec(memory_space=pltpu.VMEM)] * 4,
+        scratch_shapes=[pltpu.SemaphoreType.DMA((4,))],
+        compiler_params=pltpu.CompilerParams(vmem_limit_bytes=4 * 1024 * 1024),
+    )(inputs)
     pieces = [pieces[0]] + [shifted(pieces[k], "head", k, 4) for k in (1, 2, 3)]
 
     big = (STRETCH, FEATS)
-    weights, dt, dtt, q, g, b_t, tot = kernel_call(
+    weights, dt, dtt, q, g, b_t, tot, skip_row = kernel_call(
         prepare,
         [((HERE, STRETCH, STRETCH), BF16), (big, F32), (big, F32), (big, F32), (big, F32),
-         ((STATE, STRETCH), BF16), ((8, FEATS), F32)],
+         ((STATE, STRETCH), BF16), ((8, FEATS), F32), ((8, FEATS), F32)],
         log_decay, step_size, importance.reshape(1, STRETCH), in_b, in_c, gate,
+        skip.reshape(1, HERE),
         flops=4 << 30, bytes_accessed=12 << 20,
     )
     tot_other = shifted(tot, "core", 1, 2)
@@ -279,10 +301,10 @@
         [(big, BF16), ((STATE, HALF), F32), ((STATE, HALF), BF16)],
         *pieces, dtt, b_t,
         scratch=[((STATE, FEATS), F32)],
+        after=[tot_other],
         flops=1 << 28, bytes_accessed=4 << 20,
     )
     came = shifted(send, "core", 1, 2)
-    skip_row = jnp.repeat(skip, HEAD_DIM).reshape(1, FEATS)
     (p,) = kernel_call(
         inside, [(big, F32)], x, dt, weights, g, skip_row, flops=2 << 30, bytes_accessed=11 << 20
     )
@@ -291,6 +313,7 @@
     slices = kernel_call(
         chip_state, [(message, BF16)] * 4, keep, came, tot, tot_other,
         scratch=[((STATE + LOGS, HALF), BF16)],
+        after=[p],
     )
     slices = [slices[0]] + [shifted(slices[k], "x", k, 4) for k in (1, 2, 3)]
     chips, row, state = kernel_call(
@@ -310,7 +333,8 @@
     )
     got = shifted(give, "core", 1, 2)
     gated, sums = kernel_call(
-        gate_all, [(big, F32), ((8, STRETCH), F32)], own, got, in_c, p, q
+        gate_all, [(big, F32), ((8, STRETCH), F32)], own, got, in_c, p, q,
+        scratch=[((STATE, FEATS), BF16)],
     )
     others = [shifted(sums, "head", k, 4) for k in (1, 2, 3)]
     (out,) = kernel_call(

time: 74.4 us -> 70.2 us (0.944)
  starting transfers between devices: 33.6 us -> 32.1 us
  Pallas kernels: 9.68 us -> 8.24 us
  local copies, waits for them, and re-layouts: 7.86 us -> 6.98 us
    ppermute x19, starting transfers between devices: 33.6 us -> 32.1 us  [shifted(): return lax.ppermute(v, axis, [(i, (i + step) % size) for i in range(size)])]
    pallas_call x10 -> x11, Pallas kernels: 9.68 us -> 8.24 us  [the longest x10 8.13 us: kernel_call(): pl.pallas_call(ordered, out_shape=[jax.ShapeDtypeStruct(s, d) for s, d in...]
    dynamic_slice x1 -> x0, local copies, waits for them, and re-layouts: 1.38 us -> none  [on_device(): lax.dynamic_slice(inputs, (0, lax.rem(y + k, 4) * FEATS), (64, FEATS))]
    unnamed x28 -> x20, local copies, waits for them, and re-layouts: 6.32 us -> 6.98 us
  transfers between devices with their start and end apart: 19 -> 19, of which waited for: 13 -> 13; matrix products, arithmetic and copies ran while one was open for 0% -> 0% of each run, Pallas kernels for 6% -> 7%
where the time goes in v2:
time: 70.2 us; the launch traced here: 69.8 us
  starting transfers between devices  32.1 us (46%)
  waiting for transfers between devices  22.4 us (32%)
  Pallas kernels  8.24 us (12%)
  local copies, waits for them, and re-layouts  6.98 us (10%)
    ppermute x19, starting transfers between devices, shifted(): return lax.ppermute(v, axis, [(i, (i + step) % size) for i in range(size)])  32.1 us
    ppermute x19, waiting for transfers between devices, shifted(): return lax.ppermute(v, axis, [(i, (i + step) % size) for i in range(size)])  22.4 us
    pallas_call x10, Pallas kernels, kernel_call(): pl.pallas_call(ordered, out_shape=[jax.ShapeDtypeStruct(s, d) for s, d in...  8.13 us
    unnamed x20, local copies, waits for them, and re-layouts  6.98 us
  transfers between devices with their start and end apart: 19, of which 13 were waited for; matrix products, arithmetic and copies ran while one was open for 0% of the time, Pallas kernels for 7%

profile of v2, /device:TPU:32, one launch (start us, length us, event | category | flops | bytes accessed | tf_op | source)
XLA Modules:
  0.0 69.8 jit_solution(1765147498351034529)
XLA Ops:
  0.0 0.0 copy-start
  0.0 1.2 %copy-done = bf16[64,8192]{1,0:T(8,128)(2,1)S(1)} copy-done((bf16[64,8192]{1,0:T(8,128)(2,1)S(1)}, bf16[64,8192]{1,0:T(8,128)(2,1)}, u32[]{:S(2)}) %copy-start) | copy-done | bytes 1048600
  1.2 0.1 shard_map.91
  1.3 1.7 %collective-permute-start = (bf16[64,2048]{1,0:T(8,128)(2,1)S(1)}, bf16[64,2048]{1,0:T(8,128)(2,1)S(1)}, u32[]{:S(2)}, u32[]{:S(2)}) collective-permute-start(bf16[64,2048]{1,0:T(8,128)(2,1)S(1)} %get-tuple-element.36), channel_id=1, source_target_pairs={{0,1},{1,2},{2,3},{3,0},{4,5},{5,6},{6,7},{7,4},{8,9},{9,10},{10,1... | collective-permute-start | bytes 786440 | tf_op jit(solution)/shard_map/ppermute | solution.py:275
  3.0 2.9 %collective-permute-start.1 = (bf16[64,2048]{1,0:T(8,128)(2,1)S(1)}, bf16[64,2048]{1,0:T(8,128)(2,1)S(1)}, u32[]{:S(2)}, u32[]{:S(2)}) collective-permute-start(bf16[64,2048]{1,0:T(8,128)(2,1)S(1)} %get-tuple-element.37), channel_id=1, source_target_pairs={{0,2},{1,3},{2,0},{3,1},{4,6},{5,7},{6,4},{7,5},{8,10},{9,11},{10,... | collective-permute-start | bytes 786440 | tf_op jit(solution)/shard_map/ppermute | solution.py:275
  5.9 1.3 %collective-permute-start.2 = (bf16[64,2048]{1,0:T(8,128)(2,1)S(1)}, bf16[64,2048]{1,0:T(8,128)(2,1)S(1)}, u32[]{:S(2)}, u32[]{:S(2)}) collective-permute-start(bf16[64,2048]{1,0:T(8,128)(2,1)S(1)} %get-tuple-element.38), channel_id=1, source_target_pairs={{0,3},{1,0},{2,1},{3,2},{4,7},{5,4},{6,5},{7,6},{8,11},{9,8},{10,9... | collective-permute-start | bytes 786440 | tf_op jit(solution)/shard_map/ppermute | solution.py:275
  7.3 0.0 copy-start.1
  7.3 0.8 %copy-done.1 = bf16[256,128]{1,0:T(8,128)(2,1)S(1)} copy-done((bf16[256,128]{1,0:T(8,128)(2,1)S(1)}, bf16[256,128]{1,0:T(8,128)(2,1)}, u32[]{:S(2)}) %copy-start.1) | copy-done | bytes 65560
  8.1 0.0 copy-start.4
  8.1 1.2 %copy-done.4 = bf16[256,2048]{1,0:T(8,128)(2,1)S(1)} copy-done((bf16[256,2048]{1,0:T(8,128)(2,1)S(1)}, bf16[256,2048]{1,0:T(8,128)(2,1)}, u32[]{:S(2)}) %copy-start.4) | copy-done | bytes 1048600
  9.3 0.0 copy-start.5
  9.3 0.8 %copy-done.5 = bf16[256,128]{1,0:T(8,128)(2,1)S(1)} copy-done((bf16[256,128]{1,0:T(8,128)(2,1)S(1)}, bf16[256,128]{1,0:T(8,128)(2,1)}, u32[]{:S(2)}) %copy-start.5) | copy-done | bytes 65560
  10.2 0.0 copy-start.6
  10.2 0.8 %copy-done.6 = f32[32,256]{1,0:T(8,128)S(1)} copy-done((f32[32,256]{1,0:T(8,128)S(1)}, f32[32,256]{1,0:T(8,128)}, u32[]{:S(2)}) %copy-start.6) | copy-done | bytes 32792
  10.9 0.0 copy-start.7
  10.9 0.8 %copy-done.7 = f32[32,256]{1,0:T(8,128)S(1)} copy-done((f32[32,256]{1,0:T(8,128)S(1)}, f32[32,256]{1,0:T(8,128)}, u32[]{:S(2)}) %copy-start.7) | copy-done | bytes 32792
  11.7 0.7 copy-done.8
  12.4 0.7 copy-done.9
  13.0 3.4 %shard_map.92 = (bf16[32,256,256]{2,1,0:T(8,128)(2,1)S(1)}, f32[256,2048]{1,0:T(8,128)S(1)}, f32[256,2048]{1,0:T(8,128)S(1)}, f32[256,2048]{1,0:T(8,128)S(1)}, f...) custom-call(f32[32,256]{1,0:T(8,128)S(1)} %copy-done.6, ...), custom_call_target="tpu_custom_call" | custom-call | flops 4294967296 | bytes 12582912 | tf_op jit(solution)/shard_map/pallas_call | solution.py:32
  16.5 0.1 collective-permute-start.3
  16.6 1.2 %collective-permute-done.3.refs_6_.refs_3_.refs_7_ = f32[8,2048]{1,0:T(8,128)S(1)} collective-permute-done((f32[8,2048]{1,0:T(8,128)S(1)}, f32[8,2048]{1,0:T(8,128)S(1)}, u32[]{:S(2)}, u32[]{:S(2)}) %collective-permute-start.3) | collective-permute-done | bytes 65568 | tf_op jit(solution)/shard_map/ppermute | solution.py:275
  17.8 0.0 collective-permute-done.refs_1_
  17.8 0.0 collective-permute-done.1.refs_2_
  17.8 0.0 collective-permute-done.2.refs_3_
  17.8 0.7 shard_map.93
  18.5 0.2 collective-permute-start.4
  18.8 1.2 %shard_map.94.refs_4_.refs_3_ = f32[256,2048]{1,0:T(8,128)S(1)} custom-call(bf16[256,2048]{1,0:T(8,128)(2,1)S(1)} %get-tuple-element.44.refs_0_, f32[256,2048]{1,0:T(8,128)S(1)} %get-tuple-element.45.refs_1_, bf16[32,256,256]{2,1,0:T(8,128)(2,1)S(1)} %get-tuple-element.46.refs_2_, f32[256,2048]{1,0:T(8,128)S(1)} %get-tuple-element.47.refs_3_, ...), custom_call_target="tpu_custom_call" | custom-call | flops 2147483648 | bytes 11534336 | tf_op jit(solution)/shard_map/pallas_call | solution.py:32
  19.9 0.2 collective-permute-done.4.refs_1_.refs_5_
  20.1 0.3 shard_map.95
  20.4 1.6 %collective-permute-start.5 = (bf16[144,256]{1,0:T(8,128)(2,1)S(1)}, bf16[144,256]{1,0:T(8,128)(2,1)S(1)}, u32[]{:S(2)}, u32[]{:S(2)}) collective-permute-start(bf16[144,256]{1,0:T(8,128)(2,1)S(1)} %get-tuple-element.50), channel_id=1, source_target_pairs={{0,8},{8,16},{16,24},{24,0},{1,9},{9,17},{17,25},{25,1},{2,10},{10... | collective-permute-start | bytes 221192 | tf_op jit(solution)/shard_map/ppermute | solution.py:275
  22.0 2.7 %collective-permute-start.6 = (bf16[144,256]{1,0:T(8,128)(2,1)S(1)}, bf16[144,256]{1,0:T(8,128)(2,1)S(1)}, u32[]{:S(2)}, u32[]{:S(2)}) collective-permute-start(bf16[144,256]{1,0:T(8,128)(2,1)S(1)} %get-tuple-element.51), channel_id=1, source_target_pairs={{0,16},{8,24},{16,0},{24,8},{1,17},{9,25},{17,1},{25,9},{2,18},{10... | collective-permute-start | bytes 221192 | tf_op jit(solution)/shard_map/ppermute | solution.py:275
  24.7 1.4 %collective-permute-start.7 = (bf16[144,256]{1,0:T(8,128)(2,1)S(1)}, bf16[144,256]{1,0:T(8,128)(2,1)S(1)}, u32[]{:S(2)}, u32[]{:S(2)}) collective-permute-start(bf16[144,256]{1,0:T(8,128)(2,1)S(1)} %get-tuple-element.52), channel_id=1, source_target_pairs={{0,24},{8,0},{16,8},{24,16},{1,25},{9,1},{17,9},{25,17},{2,26},{10... | collective-permute-start | bytes 221192 | tf_op jit(solution)/shard_map/ppermute | solution.py:275
  26.1 0.0 collective-permute-done.5.refs_1_
  26.1 2.5 %collective-permute-done.6.refs_2_ = bf16[144,256]{1,0:T(8,128)(2,1)S(1)} collective-permute-done((bf16[144,256]{1,0:T(8,128)(2,1)S(1)}, bf16[144,256]{1,0:T(8,128)(2,1)S(1)}, u32[]{:S(2)}, u32[]{:S(2)}) %collective-permute-start.6) | collective-permute-done | bytes 73760 | tf_op jit(solution)/shard_map/ppermute | solution.py:275
  28.6 0.4 collective-permute-done.7.refs_3_
  29.1 0.1 shard_map.96
  29.2 2.0 %collective-permute-start.8 = (bf16[144,256]{1,0:T(8,128)(2,1)S(1)}, bf16[144,256]{1,0:T(8,128)(2,1)S(1)}, u32[]{:S(2)}, u32[]{:S(2)}) collective-permute-start(bf16[144,256]{1,0:T(8,128)(2,1)S(1)} %get-tuple-element.53.refs_0_), channel_id=1, source_target_pairs={{0,32},{32,64},{64,96},{96,128},{128,160},{160,192},{192,224},{224... | collective-permute-start | bytes 221192 | tf_op jit(solution)/shard_map/ppermute | solution.py:275
  31.2 2.4 %collective-permute-done.8.refs_2_.refs_0_ = bf16[144,256]{1,0:T(8,128)(2,1)S(1)} collective-permute-done((bf16[144,256]{1,0:T(8,128)(2,1)S(1)}, bf16[144,256]{1,0:T(8,128)(2,1)S(1)}, u32[]{:S(2)}, u32[]{:S(2)}) %collective-permute-start.8) | collective-permute-done | bytes 73760 | tf_op jit(solution)/shard_map/ppermute | solution.py:275
  33.6 5.5 %collective-permute-start.11 = (bf16[144,256]{1,0:T(8,128)(2,1)S(1)}, bf16[144,256]{1,0:T(8,128)(2,1)S(1)}, u32[]{:S(2)}, u32[]{:S(2)}) collective-permute-start(bf16[144,256]{1,0:T(8,128)(2,1)S(1)} %shard_map.97), channel_id=1, source_target_pairs={{0,192},{32,224},{64,0},{96,32},{128,64},{160,96},{192,128},{224,1... | collective-permute-start | bytes 221192 | tf_op jit(solution)/shard_map/ppermute | solution.py:275
  39.1 2.2 %collective-permute-start.10 = (bf16[144,256]{1,0:T(8,128)(2,1)S(1)}, bf16[144,256]{1,0:T(8,128)(2,1)S(1)}, u32[]{:S(2)}, u32[]{:S(2)}) collective-permute-start(bf16[144,256]{1,0:T(8,128)(2,1)S(1)} %shard_map.97), channel_id=1, source_target_pairs={{0,128},{32,160},{64,192},{96,224},{128,0},{160,32},{192,64},{224,... | collective-permute-start | bytes 221192 | tf_op jit(solution)/shard_map/ppermute | solution.py:275
  41.3 1.6 %collective-permute-start.9 = (bf16[144,256]{1,0:T(8,128)(2,1)S(1)}, bf16[144,256]{1,0:T(8,128)(2,1)S(1)}, u32[]{:S(2)}, u32[]{:S(2)}) collective-permute-start(bf16[144,256]{1,0:T(8,128)(2,1)S(1)} %shard_map.97), channel_id=1, source_target_pairs={{0,64},{32,96},{64,128},{96,160},{128,192},{160,224},{192,0},{224,... | collective-permute-start | bytes 221192 | tf_op jit(solution)/shard_map/ppermute | solution.py:275
  42.9 0.0 collective-permute-done.11.refs_3_
  43.0 4.7 %collective-permute-done.10.refs_2_ = bf16[144,256]{1,0:T(8,128)(2,1)S(1)} collective-permute-done((bf16[144,256]{1,0:T(8,128)(2,1)S(1)}, bf16[144,256]{1,0:T(8,128)(2,1)S(1)}, u32[]{:S(2)}, u32[]{:S(2)}) %collective-permute-start.10) | collective-permute-done | bytes 73760 | tf_op jit(solution)/shard_map/ppermute | solution.py:275
  47.7 1.0 %collective-permute-done.9.refs_1_ = bf16[144,256]{1,0:T(8,128)(2,1)S(1)} collective-permute-done((bf16[144,256]{1,0:T(8,128)(2,1)S(1)}, bf16[144,256]{1,0:T(8,128)(2,1)S(1)}, u32[]{:S(2)}, u32[]{:S(2)}) %collective-permute-start.9) | collective-permute-done | bytes 73760 | tf_op jit(solution)/shard_map/ppermute | solution.py:275
  48.7 0.2 shard_map.98
  48.9 1.7 %collective-permute-start.12 = (bf16[128,256]{1,0:T(8,128)(2,1)S(1)}, bf16[128,256]{1,0:T(8,128)(2,1)S(1)}, u32[]{:S(2)}, u32[]{:S(2)}) collective-permute-start(bf16[128,256]{1,0:T(8,128)(2,1)S(1)} %get-tuple-element.57), channel_id=1, source_target_pairs={{0,8},{8,16},{16,24},{24,0},{1,9},{9,17},{17,25},{25,1},{2,10},{10... | collective-permute-start | bytes 196616 | tf_op jit(solution)/shard_map/ppermute | solution.py:275
  50.5 3.2 %collective-permute-start.13 = (bf16[128,256]{1,0:T(8,128)(2,1)S(1)}, bf16[128,256]{1,0:T(8,128)(2,1)S(1)}, u32[]{:S(2)}, u32[]{:S(2)}) collective-permute-start(bf16[128,256]{1,0:T(8,128)(2,1)S(1)} %get-tuple-element.58), channel_id=1, source_target_pairs={{0,16},{8,24},{16,0},{24,8},{1,17},{9,25},{17,1},{25,9},{2,18},{10... | collective-permute-start | bytes 196616 | tf_op jit(solution)/shard_map/ppermute | solution.py:275
  53.7 0.1 collective-permute-start.14
  53.9 0.7 collective-permute-done.12.refs_1_
  54.5 2.2 %collective-permute-done.13.refs_2_ = bf16[128,256]{1,0:T(8,128)(2,1)S(1)} collective-permute-done((bf16[128,256]{1,0:T(8,128)(2,1)S(1)}, bf16[128,256]{1,0:T(8,128)(2,1)S(1)}, u32[]{:S(2)}, u32[]{:S(2)}) %collective-permute-start.13) | collective-permute-done | bytes 65568 | tf_op jit(solution)/shard_map/ppermute | solution.py:275
  56.7 1.3 %collective-permute-done.14.refs_3_ = bf16[128,256]{1,0:T(8,128)(2,1)S(1)} collective-permute-done((bf16[128,256]{1,0:T(8,128)(2,1)S(1)}, bf16[128,256]{1,0:T(8,128)(2,1)S(1)}, u32[]{:S(2)}, u32[]{:S(2)}) %collective-permute-start.14) | collective-permute-done | bytes 65568 | tf_op jit(solution)/shard_map/ppermute | solution.py:275
  58.0 0.3 shard_map.99
  58.3 0.1 collective-permute-start.15
  58.4 1.5 %collective-permute-done.15.refs_1_ = bf16[128,1024]{1,0:T(8,128)(2,1)S(1)} collective-permute-done((bf16[128,1024]{1,0:T(8,128)(2,1)S(1)}, bf16[128,1024]{1,0:T(8,128)(2,1)S(1)}, u32[]{:S(2)}, u32[]{:S(2)}) %collective-permute-start.15) | collective-permute-done | bytes 262176 | tf_op jit(solution)/shard_map/ppermute | solution.py:275
  59.9 0.0 copy-done.2
  60.0 0.6 shard_map.100
  60.6 2.0 %collective-permute-start.18 = (f32[8,256]{1,0:T(8,128)S(1)}, f32[8,256]{1,0:T(8,128)S(1)}, u32[]{:S(2)}, u32[]{:S(2)}) collective-permute-start(f32[8,256]{1,0:T(8,128)S(1)} %get-tuple-element.64.refs_1_), channel_id=1, source_target_pairs={{0,3},{1,0},{2,1},{3,2},{4,7},{5,4},{6,5},{7,6},{8,11},{9,8},{10,9... | collective-permute-start | bytes 24584 | tf_op jit(solution)/shard_map/ppermute | solution.py:275
  62.5 1.1 %collective-permute-start.17 = (f32[8,256]{1,0:T(8,128)S(1)}, f32[8,256]{1,0:T(8,128)S(1)}, u32[]{:S(2)}, u32[]{:S(2)}) collective-permute-start(f32[8,256]{1,0:T(8,128)S(1)} %get-tuple-element.64.refs_1_), channel_id=1, source_target_pairs={{0,2},{1,3},{2,0},{3,1},{4,6},{5,7},{6,4},{7,5},{8,10},{9,11},{10,... | collective-permute-start | bytes 24584 | tf_op jit(solution)/shard_map/ppermute | solution.py:275
  63.7 0.7 collective-permute-start.16
  64.4 0.0 collective-permute-done.18.refs_4_
  64.4 3.3 %collective-permute-done.17.refs_3_ = f32[8,256]{1,0:T(8,128)S(1)} collective-permute-done((f32[8,256]{1,0:T(8,128)S(1)}, f32[8,256]{1,0:T(8,128)S(1)}, u32[]{:S(2)}, u32[]{:S(2)}) %collective-permute-start.17) | collective-permute-done | bytes 8224 | tf_op jit(solution)/shard_map/ppermute | solution.py:275
  67.7 0.8 %collective-permute-done.16.refs_2_ = f32[8,256]{1,0:T(8,128)S(1)} collective-permute-done((f32[8,256]{1,0:T(8,128)S(1)}, f32[8,256]{1,0:T(8,128)S(1)}, u32[]{:S(2)}, u32[]{:S(2)}) %collective-permute-start.16) | collective-permute-done | bytes 8224 | tf_op jit(solution)/shard_map/ppermute | solution.py:275
  68.5 0.0 copy-done.3
  68.5 1.3 %shard_map.101 = bf16[256,2048]{1,0:T(8,128)(2,1)} custom-call(f32[256,2048]{1,0:T(8,128)S(1)} %get-tuple-element.63.refs_0_, f32[8,256]{1,0:T(8,128)S(1)} %get-tuple-element.64.refs_1_, f32[8,256]{1,0:T(8,128)S(1)} %collective-permute-done.16.refs_2_, f32[8,256]{1,0:T(8,128)S(1)} %collective-permute-done.17.refs_3_, ...), custom_call_target="tpu_custom_call" | custom-call | tf_op jit(solution)/shard_map/pallas_call | solution.py:32
  (5 shorter events, 0.0 us)
Async XLA Ops:
  0.0 1.2 %copy-start = (bf16[64,8192]{1,0:T(8,128)(2,1)S(1)}, bf16[64,8192]{1,0:T(8,128)(2,1)}, u32[]{:S(2)}) copy-start(bf16[64,8192]{1,0:T(8,128)(2,1)} %x_ref.1) | copy-start | bytes 3145732
  1.3 16.5 %collective-permute-start = (bf16[64,2048]{1,0:T(8,128)(2,1)S(1)}, bf16[64,2048]{1,0:T(8,128)(2,1)S(1)}, u32[]{:S(2)}, u32[]{:S(2)}) collective-permute-start(bf16[64,2048]{1,0:T(8,128)(2,1)S(1)} %get-tuple-element.36), channel_id=1, source_target_pairs={{0,1},{1,2},{2,3},{3,0},{4,5},{5,6},{6,7},{7,4},{8,9},{9,10},{10,1... | collective-permute-start | bytes 786440 | tf_op jit(solution)/shard_map/ppermute | solution.py:275
  3.0 14.8 %collective-permute-start.1 = (bf16[64,2048]{1,0:T(8,128)(2,1)S(1)}, bf16[64,2048]{1,0:T(8,128)(2,1)S(1)}, u32[]{:S(2)}, u32[]{:S(2)}) collective-permute-start(bf16[64,2048]{1,0:T(8,128)(2,1)S(1)} %get-tuple-element.37), channel_id=1, source_target_pairs={{0,2},{1,3},{2,0},{3,1},{4,6},{5,7},{6,4},{7,5},{8,10},{9,11},{10,... | collective-permute-start | bytes 786440 | tf_op jit(solution)/shard_map/ppermute | solution.py:275
  5.9 11.9 %collective-permute-start.2 = (bf16[64,2048]{1,0:T(8,128)(2,1)S(1)}, bf16[64,2048]{1,0:T(8,128)(2,1)S(1)}, u32[]{:S(2)}, u32[]{:S(2)}) collective-permute-start(bf16[64,2048]{1,0:T(8,128)(2,1)S(1)} %get-tuple-element.38), channel_id=1, source_target_pairs={{0,3},{1,0},{2,1},{3,2},{4,7},{5,4},{6,5},{7,6},{8,11},{9,8},{10,9... | collective-permute-start | bytes 786440 | tf_op jit(solution)/shard_map/ppermute | solution.py:275
  7.3 0.8 %copy-start.1 = (bf16[256,128]{1,0:T(8,128)(2,1)S(1)}, bf16[256,128]{1,0:T(8,128)(2,1)}, u32[]{:S(2)}) copy-start(bf16[256,128]{1,0:T(8,128)(2,1)} %refs_2_.1) | copy-start | bytes 196612
  8.1 1.2 %copy-start.4 = (bf16[256,2048]{1,0:T(8,128)(2,1)S(1)}, bf16[256,2048]{1,0:T(8,128)(2,1)}, u32[]{:S(2)}) copy-start(bf16[256,2048]{1,0:T(8,128)(2,1)} %refs_5_.1) | copy-start | bytes 3145732
  9.3 0.8 %copy-start.5 = (bf16[256,128]{1,0:T(8,128)(2,1)S(1)}, bf16[256,128]{1,0:T(8,128)(2,1)}, u32[]{:S(2)}) copy-start(bf16[256,128]{1,0:T(8,128)(2,1)} %refs_3_.1) | copy-start | bytes 196612
  10.2 0.8 %copy-start.6 = (f32[32,256]{1,0:T(8,128)S(1)}, f32[32,256]{1,0:T(8,128)}, u32[]{:S(2)}) copy-start(f32[32,256]{1,0:T(8,128)} %refs_0_.1) | copy-start | bytes 98308
  10.9 0.8 %copy-start.7 = (f32[32,256]{1,0:T(8,128)S(1)}, f32[32,256]{1,0:T(8,128)}, u32[]{:S(2)}) copy-start(f32[32,256]{1,0:T(8,128)} %refs_1_.1) | copy-start | bytes 98308
  11.7 0.7 copy-start.8
  12.4 0.7 copy-start.9
  16.5 1.3 %collective-permute-start.3 = (f32[8,2048]{1,0:T(8,128)S(1)}, f32[8,2048]{1,0:T(8,128)S(1)}, u32[]{:S(2)}, u32[]{:S(2)}) collective-permute-start(f32[8,2048]{1,0:T(8,128)S(1)} %get-tuple-element.41.refs_2_.refs_6_), channel_id=1, source_target_pairs={{0,4},{4,0},{1,5},{5,1},{2,6},{6,2},{3,7},{7,3},{8,12},{12,8},{9,1... | collective-permute-start | bytes 196616 | tf_op jit(solution)/shard_map/ppermute | solution.py:275
  18.5 1.6 %collective-permute-start.4 = (bf16[128,1024]{1,0:T(8,128)(2,1)S(1)}, bf16[128,1024]{1,0:T(8,128)(2,1)S(1)}, u32[]{:S(2)}, u32[]{:S(2)}) collective-permute-start(bf16[128,1024]{1,0:T(8,128)(2,1)S(1)} %get-tuple-element.43), channel_id=1, source_target_pairs={{0,4},{4,0},{1,5},{5,1},{2,6},{6,2},{3,7},{7,3},{8,12},{12,8},{9,1... | collective-permute-start | bytes 786440 | tf_op jit(solution)/shard_map/ppermute | solution.py:275
  20.1 39.8 %copy-start.2 = (bf16[256,128]{1,0:T(8,128)(2,1)S(1)}, bf16[256,128]{1,0:T(8,128)(2,1)}, u32[]{:S(2)}) copy-start(bf16[256,128]{1,0:T(8,128)(2,1)} %refs_2_.1) | copy-start | bytes 196612
  20.4 5.7 %collective-permute-start.5 = (bf16[144,256]{1,0:T(8,128)(2,1)S(1)}, bf16[144,256]{1,0:T(8,128)(2,1)S(1)}, u32[]{:S(2)}, u32[]{:S(2)}) collective-permute-start(bf16[144,256]{1,0:T(8,128)(2,1)S(1)} %get-tuple-element.50), channel_id=1, source_target_pairs={{0,8},{8,16},{16,24},{24,0},{1,9},{9,17},{17,25},{25,1},{2,10},{10... | collective-permute-start | bytes 221192 | tf_op jit(solution)/shard_map/ppermute | solution.py:275
  22.0 6.6 %collective-permute-start.6 = (bf16[144,256]{1,0:T(8,128)(2,1)S(1)}, bf16[144,256]{1,0:T(8,128)(2,1)S(1)}, u32[]{:S(2)}, u32[]{:S(2)}) collective-permute-start(bf16[144,256]{1,0:T(8,128)(2,1)S(1)} %get-tuple-element.51), channel_id=1, source_target_pairs={{0,16},{8,24},{16,0},{24,8},{1,17},{9,25},{17,1},{25,9},{2,18},{10... | collective-permute-start | bytes 221192 | tf_op jit(solution)/shard_map/ppermute | solution.py:275
  24.7 4.4 %collective-permute-start.7 = (bf16[144,256]{1,0:T(8,128)(2,1)S(1)}, bf16[144,256]{1,0:T(8,128)(2,1)S(1)}, u32[]{:S(2)}, u32[]{:S(2)}) collective-permute-start(bf16[144,256]{1,0:T(8,128)(2,1)S(1)} %get-tuple-element.52), channel_id=1, source_target_pairs={{0,24},{8,0},{16,8},{24,16},{1,25},{9,1},{17,9},{25,17},{2,26},{10... | collective-permute-start | bytes 221192 | tf_op jit(solution)/shard_map/ppermute | solution.py:275
  29.2 4.4 %collective-permute-start.8 = (bf16[144,256]{1,0:T(8,128)(2,1)S(1)}, bf16[144,256]{1,0:T(8,128)(2,1)S(1)}, u32[]{:S(2)}, u32[]{:S(2)}) collective-permute-start(bf16[144,256]{1,0:T(8,128)(2,1)S(1)} %get-tuple-element.53.refs_0_), channel_id=1, source_target_pairs={{0,32},{32,64},{64,96},{96,128},{128,160},{160,192},{192,224},{224... | collective-permute-start | bytes 221192 | tf_op jit(solution)/shard_map/ppermute | solution.py:275
  33.6 9.3 %collective-permute-start.11 = (bf16[144,256]{1,0:T(8,128)(2,1)S(1)}, bf16[144,256]{1,0:T(8,128)(2,1)S(1)}, u32[]{:S(2)}, u32[]{:S(2)}) collective-permute-start(bf16[144,256]{1,0:T(8,128)(2,1)S(1)} %shard_map.97), channel_id=1, source_target_pairs={{0,192},{32,224},{64,0},{96,32},{128,64},{160,96},{192,128},{224,1... | collective-permute-start | bytes 221192 | tf_op jit(solution)/shard_map/ppermute | solution.py:275
  39.1 8.5 %collective-permute-start.10 = (bf16[144,256]{1,0:T(8,128)(2,1)S(1)}, bf16[144,256]{1,0:T(8,128)(2,1)S(1)}, u32[]{:S(2)}, u32[]{:S(2)}) collective-permute-start(bf16[144,256]{1,0:T(8,128)(2,1)S(1)} %shard_map.97), channel_id=1, source_target_pairs={{0,128},{32,160},{64,192},{96,224},{128,0},{160,32},{192,64},{224,... | collective-permute-start | bytes 221192 | tf_op jit(solution)/shard_map/ppermute | solution.py:275
  41.3 7.3 %collective-permute-start.9 = (bf16[144,256]{1,0:T(8,128)(2,1)S(1)}, bf16[144,256]{1,0:T(8,128)(2,1)S(1)}, u32[]{:S(2)}, u32[]{:S(2)}) collective-permute-start(bf16[144,256]{1,0:T(8,128)(2,1)S(1)} %shard_map.97), channel_id=1, source_target_pairs={{0,64},{32,96},{64,128},{96,160},{128,192},{160,224},{192,0},{224,... | collective-permute-start | bytes 221192 | tf_op jit(solution)/shard_map/ppermute | solution.py:275
  48.9 5.7 %collective-permute-start.12 = (bf16[128,256]{1,0:T(8,128)(2,1)S(1)}, bf16[128,256]{1,0:T(8,128)(2,1)S(1)}, u32[]{:S(2)}, u32[]{:S(2)}) collective-permute-start(bf16[128,256]{1,0:T(8,128)(2,1)S(1)} %get-tuple-element.57), channel_id=1, source_target_pairs={{0,8},{8,16},{16,24},{24,0},{1,9},{9,17},{17,25},{25,1},{2,10},{10... | collective-permute-start | bytes 196616 | tf_op jit(solution)/shard_map/ppermute | solution.py:275
  50.5 6.2 %collective-permute-start.13 = (bf16[128,256]{1,0:T(8,128)(2,1)S(1)}, bf16[128,256]{1,0:T(8,128)(2,1)S(1)}, u32[]{:S(2)}, u32[]{:S(2)}) collective-permute-start(bf16[128,256]{1,0:T(8,128)(2,1)S(1)} %get-tuple-element.58), channel_id=1, source_target_pairs={{0,16},{8,24},{16,0},{24,8},{1,17},{9,25},{17,1},{25,9},{2,18},{10... | collective-permute-start | bytes 196616 | tf_op jit(solution)/shard_map/ppermute | solution.py:275
  53.7 4.3 %collective-permute-start.14 = (bf16[128,256]{1,0:T(8,128)(2,1)S(1)}, bf16[128,256]{1,0:T(8,128)(2,1)S(1)}, u32[]{:S(2)}, u32[]{:S(2)}) collective-permute-start(bf16[128,256]{1,0:T(8,128)(2,1)S(1)} %get-tuple-element.59), channel_id=1, source_target_pairs={{0,24},{8,0},{16,8},{24,16},{1,25},{9,1},{17,9},{25,17},{2,26},{10... | collective-permute-start | bytes 196616 | tf_op jit(solution)/shard_map/ppermute | solution.py:275
  58.3 1.6 %collective-permute-start.15 = (bf16[128,1024]{1,0:T(8,128)(2,1)S(1)}, bf16[128,1024]{1,0:T(8,128)(2,1)S(1)}, u32[]{:S(2)}, u32[]{:S(2)}) collective-permute-start(bf16[128,1024]{1,0:T(8,128)(2,1)S(1)} %get-tuple-element.61), channel_id=1, source_target_pairs={{0,4},{4,0},{1,5},{5,1},{2,6},{6,2},{3,7},{7,3},{8,12},{12,8},{9,1... | collective-permute-start | bytes 786440 | tf_op jit(solution)/shard_map/ppermute | solution.py:275
  59.9 8.6 %copy-start.3 = (f32[2048]{0:T(1024)S(1)}, f32[2048]{0:T(1024)}, u32[]{:S(2)}) copy-start(f32[2048]{0:T(1024)} %param.17) | copy-start | bytes 24580
  60.6 3.8 %collective-permute-start.18 = (f32[8,256]{1,0:T(8,128)S(1)}, f32[8,256]{1,0:T(8,128)S(1)}, u32[]{:S(2)}, u32[]{:S(2)}) collective-permute-start(f32[8,256]{1,0:T(8,128)S(1)} %get-tuple-element.64.refs_1_), channel_id=1, source_target_pairs={{0,3},{1,0},{2,1},{3,2},{4,7},{5,4},{6,5},{7,6},{8,11},{9,8},{10,9... | collective-permute-start | bytes 24584 | tf_op jit(solution)/shard_map/ppermute | solution.py:275
  62.5 5.2 %collective-permute-start.17 = (f32[8,256]{1,0:T(8,128)S(1)}, f32[8,256]{1,0:T(8,128)S(1)}, u32[]{:S(2)}, u32[]{:S(2)}) collective-permute-start(f32[8,256]{1,0:T(8,128)S(1)} %get-tuple-element.64.refs_1_), channel_id=1, source_target_pairs={{0,2},{1,3},{2,0},{3,1},{4,6},{5,7},{6,4},{7,5},{8,10},{9,11},{10,... | collective-permute-start | bytes 24584 | tf_op jit(solution)/shard_map/ppermute | solution.py:275
  63.7 4.9 %collective-permute-start.16 = (f32[8,256]{1,0:T(8,128)S(1)}, f32[8,256]{1,0:T(8,128)S(1)}, u32[]{:S(2)}, u32[]{:S(2)}) collective-permute-start(f32[8,256]{1,0:T(8,128)S(1)} %get-tuple-element.64.refs_1_), channel_id=1, source_target_pairs={{0,1},{1,2},{2,3},{3,0},{4,5},{5,6},{6,7},{7,4},{8,9},{9,10},{10,1... | collective-permute-start | bytes 24584 | tf_op jit(solution)/shard_map/ppermute | solution.py:275

commit v3 on v2

--- a/solution.py
+++ b/solution.py
@@ -19,11 +19,13 @@
 FEATS = HERE * HEAD_DIM
 HALF = FEATS // 2
 PART = HALF // 4
+STEPS = (0, 1, 3, 2)
 LOGS = 16
 
 
-def kernel_call(body, outs, *args, scratch=(), after=(), flops=0, bytes_accessed=0):
-    vmem = pl.BlockSpec(memory_space=pltpu.VMEM)
+def kernel_call(body, outs, *args, scratch=(), after=(), flops=0, bytes_accessed=0,
+                hbm_in=False, hbm_out=False, copies=0):
+    vmem, hbm = pl.BlockSpec(memory_space=pltpu.VMEM), pl.BlockSpec(memory_space=pltpu.HBM)
     count = len(args)
 
     def ordered(*refs):
@@ -32,9 +34,11 @@
     return pl.pallas_call(
         ordered,
         out_shape=[jax.ShapeDtypeStruct(s, d) for s, d in outs],
-        in_specs=[vmem] * count + [pl.BlockSpec(memory_space=pl.ANY)] * len(after),
-        out_specs=[vmem] * len(outs),
-        scratch_shapes=[pltpu.VMEM(s, d) for s, d in scratch],
+        in_specs=[hbm if hbm_in else vmem] * count
+        + [pl.BlockSpec(memory_space=pl.ANY)] * len(after),
+        out_specs=[hbm if hbm_out else vmem] * len(outs),
+        scratch_shapes=[pltpu.VMEM(s, d) for s, d in scratch]
+        + ([pltpu.SemaphoreType.DMA((copies,))] if copies else []),
         compiler_params=pltpu.CompilerParams(vmem_limit_bytes=20 * 1024 * 1024),
         cost_estimate=pl.CostEstimate(
             flops=flops, bytes_accessed=bytes_accessed, transcendentals=0
@@ -72,18 +76,7 @@
     return message[:STATE, :].astype(F32)
 
 
-def cut(x_ref, s0, s1, s2, s3, sems):
-    copies = []
-    for k, out in enumerate((s0, s1, s2, s3)):
-        at = pl.multiple_of(place("head", k, 4) * FEATS, FEATS)
-        copies.append(pltpu.make_async_copy(x_ref.at[:, pl.ds(at, FEATS)], out, sems.at[k]))
-    for copy in copies:
-        copy.start()
-    for copy in copies:
-        copy.wait()
-
-
-def prepare(log_ref, step_ref, imp_ref, b_ref, c_ref, gate_ref, skip_ref,
+def prepare(log_ref, step_ref, imp_ref, skip_ref, b_ref, c_ref, gate_ref,
             w_ref, dt_ref, dtt_ref, q_ref, g_ref, bt_ref, tot_ref, skip_row_ref):
     lane = lax.broadcasted_iota(jnp.int32, (HERE, STRETCH), 1)
     cum = log_ref[...]
@@ -194,12 +187,12 @@
         jnp.exp(log1) * pick(core, keep, came) + pick(core, came, keep)
     ).astype(BF16)
     message[STATE:, :] = log_block(log0 + log1)
-    for k, out in enumerate((s0, s1, s2, s3)):
+    for k, out in zip(STEPS, (s0, s1, s2, s3)):
         out[...] = message[:, pl.ds(pl.multiple_of(place("x", k, 4) * PART, PART), PART)]
 
 
 def row_state(m0, m1, m2, m3, all_ref, row_ref, state_ref):
-    for k, piece in enumerate((m0, m1, m2, m3)):
+    for k, piece in zip(STEPS, (m0, m1, m2, m3)):
         all_ref[place("x", -k, 4)] = piece[...]
     state = state_of(all_ref[0])
     logs = logs_of(all_ref[0])
@@ -212,31 +205,33 @@
     row_ref[STATE:, :] = log_block(logs)
 
 
-def window(row_ref, state_ref, before_ref, out_ref):
+def window(row_ref, state_ref, before_ref, after_ref, out_ref):
     z = lax.axis_index("z")
-    log = logs_of(row_ref[...])
+    log, log_after = logs_of(row_ref[...]), logs_of(after_ref[...])
     before = state_of(before_ref[...])
-    before = pick(jnp.minimum(z, 1), jnp.zeros_like(before), before)
-    out_ref[:STATE, :] = (jnp.exp(log) * before + state_ref[...]).astype(BF16)
-    out_ref[STATE:, :] = log_block(log + logs_of(before_ref[...]))
-
-
-def enter(before_ref, p2, p4, p6, all_ref, e0, e1, e2, e3, every):
+    before = pick(z, jnp.zeros_like(before), before)
+    state = jnp.exp(log_after) * (jnp.exp(log) * before + state_ref[...])
+    state = pick(7 - z, jnp.zeros_like(state), state) + state_of(after_ref[...])
+    out_ref[:STATE, :] = state.astype(BF16)
+    out_ref[STATE:, :] = log_block(log + log_after + logs_of(before_ref[...]))
+
+
+def enter(before_ref, w3, w6, all_ref, e0, e1, e2, e3, every):
     z = lax.axis_index("z")
     state = jnp.zeros((STATE, PART), F32)
-    for gap, piece in ((6, p6), (4, p4), (2, p2), (1, before_ref)):
-        there = pick(lax.div(z, gap), jnp.zeros_like(state), state_of(piece[...]))
+    for least, piece in ((5, w6), (2, w3), (1, before_ref)):
+        there = pick(lax.div(z, least), jnp.zeros_like(state), state_of(piece[...]))
         state = jnp.exp(logs_of(piece[...])) * state + there
     for x in range(4):
         every[x] = state.astype(BF16)
         if x < 3:
             state = jnp.exp(logs_of(all_ref[x])) * state + state_of(all_ref[x])
-    for k, out in enumerate((e0, e1, e2, e3)):
+    for k, out in zip(STEPS, (e0, e1, e2, e3)):
         out[...] = every[place("x", k, 4)]
 
 
 def core_states(f0, f1, f2, f3, keep_ref, came_ref, tot_ref, tot_other_ref, own_ref, give_ref, chip):
-    for k, piece in enumerate((f0, f1, f2, f3)):
+    for k, piece in zip(STEPS, (f0, f1, f2, f3)):
         chip[:, pl.ds(pl.multiple_of(place("x", -k, 4) * PART, PART), PART)] = piece[...]
     core = lax.axis_index("core")
     log0, _ = halves(core, tot_ref, tot_other_ref)
@@ -261,38 +256,46 @@
     sums_ref[...] = jnp.broadcast_to(jnp.sum(total.T, axis=0, keepdims=True), (8, STRETCH))
 
 
-def normalize(gated_ref, q0, q1, q2, q3, gain_ref, out_ref):
+def normalize(gated_ref, q0, q1, q2, q3, gain_ref, out_hbm, out_ref, sems):
     total = q0[:1, :] + q1[:1, :] + q2[:1, :] + q3[:1, :]
     scale = lax.rsqrt(total / (HEADS * HEAD_DIM) + epsilon)
     scale = jnp.broadcast_to(scale, (128, STRETCH)).T
-    for at in range(0, FEATS, 128):
-        out_ref[:, at:at + 128] = (
-            gated_ref[:, at:at + 128] * scale * gain_ref[:, at:at + 128]
-        ).astype(BF16)
+    copies = []
+    for k in range(4):
+        rows = slice(k * 64, k * 64 + 64)
+        for at in range(0, FEATS, 128):
+            out_ref[rows, at:at + 128] = (
+                gated_ref[rows, at:at + 128] * scale[rows] * gain_ref[:, at:at + 128]
+            ).astype(BF16)
+        copy = pltpu.make_async_copy(out_ref.at[rows], out_hbm.at[rows], sems.at[k])
+        copy.start()
+        copies.append(copy)
+    for copy in copies:
+        copy.wait()
 
 
 def shifted(v, axis, step, size):
     return lax.ppermute(v, axis, [(i, (i + step) % size) for i in range(size)])
 
 
+def triple(pieces, axis, steps):
+    return [shifted(piece, axis, k, 4) for k, piece in zip(steps, pieces[1:])]
+
+
 def on_device(inputs, gate, in_b, in_c, log_decay, step_size, importance, skip, norm_gain):
-    pieces = pl.pallas_call(
-        cut,
-        out_shape=[jax.ShapeDtypeStruct((64, FEATS), BF16)] * 4,
-        in_specs=[pl.BlockSpec(memory_space=pl.ANY)],
-        out_specs=[pl.BlockSpec(memory_space=pltpu.VMEM)] * 4,
-        scratch_shapes=[pltpu.SemaphoreType.DMA((4,))],
-        compiler_params=pltpu.CompilerParams(vmem_limit_bytes=4 * 1024 * 1024),
-    )(inputs)
-    pieces = [pieces[0]] + [shifted(pieces[k], "head", k, 4) for k in (1, 2, 3)]
+    y = lax.axis_index("head")
+    pieces = [
+        lax.dynamic_slice(inputs, (0, lax.rem(y + k, 4) * FEATS), (64, FEATS)) for k in range(4)
+    ]
+    pieces = [pieces[0]] + triple(pieces, "head", (1, 2, 3))
 
     big = (STRETCH, FEATS)
     weights, dt, dtt, q, g, b_t, tot, skip_row = kernel_call(
         prepare,
         [((HERE, STRETCH, STRETCH), BF16), (big, F32), (big, F32), (big, F32), (big, F32),
          ((STATE, STRETCH), BF16), ((8, FEATS), F32), ((8, FEATS), F32)],
-        log_decay, step_size, importance.reshape(1, STRETCH), in_b, in_c, gate,
-        skip.reshape(1, HERE),
+        log_decay, step_size, importance.reshape(1, STRETCH), skip.reshape(1, HERE),
+        in_b, in_c, gate,
         flops=4 << 30, bytes_accessed=12 << 20,
     )
     tot_other = shifted(tot, "core", 1, 2)
@@ -315,18 +318,19 @@
         scratch=[((STATE + LOGS, HALF), BF16)],
         after=[p],
     )
-    slices = [slices[0]] + [shifted(slices[k], "x", k, 4) for k in (1, 2, 3)]
+    slices = [slices[0]] + triple(slices, "x", STEPS[1:])
     chips, row, state = kernel_call(
         row_state, [((4,) + message, BF16), (message, BF16), ((STATE, PART), F32)], *slices
     )
     before = shifted(row, "z", 1, 8)
-    (pair,) = kernel_call(window, [(message, BF16)], row, state, before)
-    back = [shifted(pair, "z", k, 8) for k in (2, 4, 6)]
+    after = shifted(row, "z", 7, 8)
+    (three,) = kernel_call(window, [(message, BF16)], row, state, before, after)
+    back = [shifted(three, "z", 3, 8), shifted(three, "z", 6, 8)]
     enters = kernel_call(
         enter, [((STATE, PART), BF16)] * 4, before, *back, chips,
         scratch=[((4, STATE, PART), BF16)],
     )
-    enters = [enters[0]] + [shifted(enters[k], "x", k, 4) for k in (1, 2, 3)]
+    enters = [enters[0]] + triple(enters, "x", STEPS[1:])
     own, give = kernel_call(
         core_states, [((STATE, HALF), BF16)] * 2, *enters, keep, came, tot, tot_other,
         scratch=[((STATE, HALF), BF16)],
@@ -336,9 +340,10 @@
         gate_all, [(big, F32), ((8, STRETCH), F32)], own, got, in_c, p, q,
         scratch=[((STATE, FEATS), BF16)],
     )
-    others = [shifted(sums, "head", k, 4) for k in (1, 2, 3)]
+    others = triple([sums] * 4, "head", (2, 3, 1))
     (out,) = kernel_call(
-        normalize, [(big, BF16)], gated, sums, *others, norm_gain.reshape(1, FEATS)
+        normalize, [(big, BF16)], gated, sums, *others, norm_gain.reshape(1, FEATS),
+        scratch=[(big, BF16)], hbm_out=True, copies=4,
     )
     return out
 

time: 70.2 us -> 72.9 us (1.038)
  waiting for transfers between devices: 22.4 us -> 39.2 us
  starting transfers between devices: 32.1 us -> 23.6 us
  local copies, waits for them, and re-layouts: 6.98 us -> 1.41 us
    ppermute x19, waiting for transfers between devices: 22.4 us -> 39.2 us  [shifted(): return lax.ppermute(v, axis, [(i, (i + step) % size) for i in range(size)])]
    ppermute x19, starting transfers between devices: 32.1 us -> 23.6 us  [shifted(): return lax.ppermute(v, axis, [(i, (i + step) % size) for i in range(size)])]
    unnamed x20 -> x16, local copies, waits for them, and re-layouts: 6.98 us -> 0.03 us
    dynamic_slice x0 -> x1, local copies, waits for them, and re-layouts: none -> 1.38 us  [on_device(): lax.dynamic_slice(inputs, (0, lax.rem(y + k, 4) * FEATS), (64, FEATS))]
  transfers between devices with their start and end apart: 19 -> 19, of which waited for: 13 -> 16; matrix products, arithmetic and copies ran while one was open for 0% -> 0% of each run, Pallas kernels for 7% -> 6%
where the time goes in v3:
time: 72.9 us; the launch traced here: 72.6 us
  waiting for transfers between devices  39.2 us (54%)
  starting transfers between devices  23.6 us (32%)
  Pallas kernels  8.02 us (11%)
  local copies, waits for them, and re-layouts  1.41 us (2%)
    ppermute x19, waiting for transfers between devices, shifted(): return lax.ppermute(v, axis, [(i, (i + step) % size) for i in range(size)])  39.2 us
    ppermute x19, starting transfers between devices, shifted(): return lax.ppermute(v, axis, [(i, (i + step) % size) for i in range(size)])  23.6 us
    pallas_call x10, Pallas kernels, kernel_call(): pl.pallas_call(ordered, out_shape=[jax.ShapeDtypeStruct(s, d) for s, d in...  8.02 us
  transfers between devices with their start and end apart: 19, of which 16 were waited for; matrix products, arithmetic and copies ran while one was open for 0% of the time, Pallas kernels for 6%

profile of v3, /device:TPU:32, one launch (start us, length us, event | category | flops | bytes accessed | tf_op | source)
XLA Modules:
  0.0 72.6 jit_solution(14744738788625589840)
XLA Ops:
  0.0 0.0 copy-start.7
  0.0 0.0 copy-start.6
  0.0 0.0 copy-start.5
  0.0 0.0 copy-start.4
  0.0 0.0 copy-start.3
  0.0 0.0 copy-start.2
  0.1 1.4 %constant_dynamic-slice_fusion = (bf16[64,2048]{1,0:T(8,128)(2,1)S(1)}, bf16[64,2048]{1,0:T(8,128)(2,1)S(1)}, bf16[64,2048]{1,0:T(8,128)(2,1)S(1)}, bf16[64,2048]{1,0:T(8,128)(2,1)S(1)}) fusion(bf16[64,8192]{1,0:T(8,128)(2,1)} %param.9, s32[]{:T(128)S(6)} %select_n.15, s32[]{:T(128)S(6)} %select_n.13, s32[]{:T(128)S(6)} %select_n.12, s32[]{:T(128)S(6)} %select_n.14), kind=kLoop, calls=%fused_computation | loop fusion | bytes 2097168 | tf_op jit(solution)/shard_map/dynamic_slice | solution.py:288
  1.5 3.1 %collective-permute-start.2 = (bf16[64,2048]{1,0:T(8,128)(2,1)S(1)}, bf16[64,2048]{1,0:T(8,128)(2,1)S(1)}, u32[]{:S(2)}, u32[]{:S(2)}) collective-permute-start(bf16[64,2048]{1,0:T(8,128)(2,1)S(1)} %get-tuple-element.57), channel_id=1, source_target_pairs={{0,3},{1,0},{2,1},{3,2},{4,7},{5,4},{6,5},{7,6},{8,11},{9,8},{10,9... | collective-permute-start | bytes 786440 | tf_op jit(solution)/shard_map/ppermute | solution.py:278
  4.6 0.0 collective-permute-start
  4.6 2.2 %collective-permute-start.1 = (bf16[64,2048]{1,0:T(8,128)(2,1)S(1)}, bf16[64,2048]{1,0:T(8,128)(2,1)S(1)}, u32[]{:S(2)}, u32[]{:S(2)}) collective-permute-start(bf16[64,2048]{1,0:T(8,128)(2,1)S(1)} %get-tuple-element.60), channel_id=1, source_target_pairs={{0,2},{1,3},{2,0},{3,1},{4,6},{5,7},{6,4},{7,5},{8,10},{9,11},{10,... | collective-permute-start | bytes 786440 | tf_op jit(solution)/shard_map/ppermute | solution.py:278
  6.8 0.0 copy-done
  6.8 0.0 copy-done.7
  6.8 0.0 copy-done.6
  6.8 0.0 copy-done.5
  6.8 0.0 copy-done.4
  6.8 0.0 copy-done.3
  6.8 0.0 copy-done.2
  6.8 3.4 %shard_map.91 = (bf16[32,256,256]{2,1,0:T(8,128)(2,1)S(1)}, f32[256,2048]{1,0:T(8,128)S(1)}, f32[256,2048]{1,0:T(8,128)S(1)}, f32[256,2048]{1,0:T(8,128)S(1)}, f...) custom-call(f32[32,256]{1,0:T(8,128)S(1)} %copy-done.4, ...), custom_call_target="tpu_custom_call" | custom-call | flops 4294967296 | bytes 12582912 | tf_op jit(solution)/shard_map/pallas_call | solution.py:34
  10.2 0.1 collective-permute-start.3
  10.3 1.2 %collective-permute-done.3.refs_6_.refs_3_.refs_7_ = f32[8,2048]{1,0:T(8,128)S(1)} collective-permute-done((f32[8,2048]{1,0:T(8,128)S(1)}, f32[8,2048]{1,0:T(8,128)S(1)}, u32[]{:S(2)}, u32[]{:S(2)}) %collective-permute-start.3) | collective-permute-done | bytes 65568 | tf_op jit(solution)/shard_map/ppermute | solution.py:278
  11.6 4.1 %collective-permute-done.2.refs_3_ = bf16[64,2048]{1,0:T(8,128)(2,1)S(1)} collective-permute-done((bf16[64,2048]{1,0:T(8,128)(2,1)S(1)}, bf16[64,2048]{1,0:T(8,128)(2,1)S(1)}, u32[]{:S(2)}, u32[]{:S(2)}) %collective-permute-start.2) | collective-permute-done | bytes 262176 | tf_op jit(solution)/shard_map/ppermute | solution.py:278
  15.7 3.4 %collective-permute-done.refs_1_ = bf16[64,2048]{1,0:T(8,128)(2,1)S(1)} collective-permute-done((bf16[64,2048]{1,0:T(8,128)(2,1)S(1)}, bf16[64,2048]{1,0:T(8,128)(2,1)S(1)}, u32[]{:S(2)}, u32[]{:S(2)}) %collective-permute-start) | collective-permute-done | bytes 262176 | tf_op jit(solution)/shard_map/ppermute | solution.py:278
  19.1 0.0 collective-permute-done.1.refs_2_
  19.2 0.7 shard_map.92
  19.8 0.1 collective-permute-start.4
  19.9 1.2 %shard_map.93.refs_4_.refs_3_ = f32[256,2048]{1,0:T(8,128)S(1)} custom-call(bf16[256,2048]{1,0:T(8,128)(2,1)S(1)} %get-tuple-element.36.refs_0_, f32[256,2048]{1,0:T(8,128)S(1)} %get-tuple-element.37.refs_1_, bf16[32,256,256]{2,1,0:T(8,128)(2,1)S(1)} %get-tuple-element.38.refs_2_, f32[256,2048]{1,0:T(8,128)S(1)} %get-tuple-element.39.refs_3_, ...), custom_call_target="tpu_custom_call" | custom-call | flops 2147483648 | bytes 11534336 | tf_op jit(solution)/shard_map/pallas_call | solution.py:34
  21.1 0.3 collective-permute-done.4.refs_1_.refs_5_
  21.5 0.3 shard_map.94
  21.7 1.6 %collective-permute-start.5 = (bf16[144,256]{1,0:T(8,128)(2,1)S(1)}, bf16[144,256]{1,0:T(8,128)(2,1)S(1)}, u32[]{:S(2)}, u32[]{:S(2)}) collective-permute-start(bf16[144,256]{1,0:T(8,128)(2,1)S(1)} %get-tuple-element.42), channel_id=1, source_target_pairs={{0,8},{8,16},{16,24},{24,0},{1,9},{9,17},{17,25},{25,1},{2,10},{10... | collective-permute-start | bytes 221192 | tf_op jit(solution)/shard_map/ppermute | solution.py:278
  23.3 1.7 %collective-permute-start.6 = (bf16[144,256]{1,0:T(8,128)(2,1)S(1)}, bf16[144,256]{1,0:T(8,128)(2,1)S(1)}, u32[]{:S(2)}, u32[]{:S(2)}) collective-permute-start(bf16[144,256]{1,0:T(8,128)(2,1)S(1)} %get-tuple-element.43), channel_id=1, source_target_pairs={{0,24},{8,0},{16,8},{24,16},{1,25},{9,1},{17,9},{25,17},{2,26},{10... | collective-permute-start | bytes 221192 | tf_op jit(solution)/shard_map/ppermute | solution.py:278
  25.1 1.8 %collective-permute-start.7 = (bf16[144,256]{1,0:T(8,128)(2,1)S(1)}, bf16[144,256]{1,0:T(8,128)(2,1)S(1)}, u32[]{:S(2)}, u32[]{:S(2)}) collective-permute-start(bf16[144,256]{1,0:T(8,128)(2,1)S(1)} %get-tuple-element.44), channel_id=1, source_target_pairs={{0,16},{8,24},{16,0},{24,8},{1,17},{9,25},{17,1},{25,9},{2,18},{10... | collective-permute-start | bytes 221192 | tf_op jit(solution)/shard_map/ppermute | solution.py:278
  26.9 0.5 collective-permute-done.5.refs_1_
  27.4 0.4 collective-permute-done.6.refs_2_
  27.7 3.2 %collective-permute-done.7.refs_3_ = bf16[144,256]{1,0:T(8,128)(2,1)S(1)} collective-permute-done((bf16[144,256]{1,0:T(8,128)(2,1)S(1)}, bf16[144,256]{1,0:T(8,128)(2,1)S(1)}, u32[]{:S(2)}, u32[]{:S(2)}) %collective-permute-start.7) | collective-permute-done | bytes 73760 | tf_op jit(solution)/shard_map/ppermute | solution.py:278
  30.9 0.1 shard_map.95
  31.0 0.2 collective-permute-start.9
  31.2 1.9 %collective-permute-start.8 = (bf16[144,256]{1,0:T(8,128)(2,1)S(1)}, bf16[144,256]{1,0:T(8,128)(2,1)S(1)}, u32[]{:S(2)}, u32[]{:S(2)}) collective-permute-start(bf16[144,256]{1,0:T(8,128)(2,1)S(1)} %get-tuple-element.45.refs_0_), channel_id=1, source_target_pairs={{0,32},{32,64},{64,96},{96,128},{128,160},{160,192},{192,224},{224... | collective-permute-start | bytes 221192 | tf_op jit(solution)/shard_map/ppermute | solution.py:278
  33.1 2.3 %collective-permute-done.9.refs_3_ = bf16[144,256]{1,0:T(8,128)(2,1)S(1)} collective-permute-done((bf16[144,256]{1,0:T(8,128)(2,1)S(1)}, bf16[144,256]{1,0:T(8,128)(2,1)S(1)}, u32[]{:S(2)}, u32[]{:S(2)}) %collective-permute-start.9) | collective-permute-done | bytes 73760 | tf_op jit(solution)/shard_map/ppermute | solution.py:278
  35.4 3.9 %collective-permute-done.8.refs_2_.refs_0_ = bf16[144,256]{1,0:T(8,128)(2,1)S(1)} collective-permute-done((bf16[144,256]{1,0:T(8,128)(2,1)S(1)}, bf16[144,256]{1,0:T(8,128)(2,1)S(1)}, u32[]{:S(2)}, u32[]{:S(2)}) %collective-permute-start.8) | collective-permute-done | bytes 73760 | tf_op jit(solution)/shard_map/ppermute | solution.py:278
  39.4 0.1 shard_map.96
  39.5 2.9 %collective-permute-start.11 = (bf16[144,256]{1,0:T(8,128)(2,1)S(1)}, bf16[144,256]{1,0:T(8,128)(2,1)S(1)}, u32[]{:S(2)}, u32[]{:S(2)}) collective-permute-start(bf16[144,256]{1,0:T(8,128)(2,1)S(1)} %shard_map.96), channel_id=1, source_target_pairs={{0,192},{32,224},{64,0},{96,32},{128,64},{160,96},{192,128},{224,1... | collective-permute-start | bytes 221192 | tf_op jit(solution)/shard_map/ppermute | solution.py:278
  42.4 0.6 collective-permute-start.10
  43.0 2.7 %collective-permute-done.11.refs_2_ = bf16[144,256]{1,0:T(8,128)(2,1)S(1)} collective-permute-done((bf16[144,256]{1,0:T(8,128)(2,1)S(1)}, bf16[144,256]{1,0:T(8,128)(2,1)S(1)}, u32[]{:S(2)}, u32[]{:S(2)}) %collective-permute-start.11) | collective-permute-done | bytes 73760 | tf_op jit(solution)/shard_map/ppermute | solution.py:278
  45.8 5.2 %collective-permute-done.10.refs_1_ = bf16[144,256]{1,0:T(8,128)(2,1)S(1)} collective-permute-done((bf16[144,256]{1,0:T(8,128)(2,1)S(1)}, bf16[144,256]{1,0:T(8,128)(2,1)S(1)}, u32[]{:S(2)}, u32[]{:S(2)}) %collective-permute-start.10) | collective-permute-done | bytes 73760 | tf_op jit(solution)/shard_map/ppermute | solution.py:278
  50.9 0.2 shard_map.97
  51.1 0.4 collective-permute-start.12
  51.5 2.9 %collective-permute-start.13 = (bf16[128,256]{1,0:T(8,128)(2,1)S(1)}, bf16[128,256]{1,0:T(8,128)(2,1)S(1)}, u32[]{:S(2)}, u32[]{:S(2)}) collective-permute-start(bf16[128,256]{1,0:T(8,128)(2,1)S(1)} %get-tuple-element.50), channel_id=1, source_target_pairs={{0,24},{8,0},{16,8},{24,16},{1,25},{9,1},{17,9},{25,17},{2,26},{10... | collective-permute-start | bytes 196616 | tf_op jit(solution)/shard_map/ppermute | solution.py:278
  54.4 0.6 collective-permute-start.14
  55.0 1.6 %collective-permute-done.12.refs_1_ = bf16[128,256]{1,0:T(8,128)(2,1)S(1)} collective-permute-done((bf16[128,256]{1,0:T(8,128)(2,1)S(1)}, bf16[128,256]{1,0:T(8,128)(2,1)S(1)}, u32[]{:S(2)}, u32[]{:S(2)}) %collective-permute-start.12) | collective-permute-done | bytes 65568 | tf_op jit(solution)/shard_map/ppermute | solution.py:278
  56.6 0.0 collective-permute-done.13.refs_2_
  56.6 3.5 %collective-permute-done.14.refs_3_ = bf16[128,256]{1,0:T(8,128)(2,1)S(1)} collective-permute-done((bf16[128,256]{1,0:T(8,128)(2,1)S(1)}, bf16[128,256]{1,0:T(8,128)(2,1)S(1)}, u32[]{:S(2)}, u32[]{:S(2)}) %collective-permute-start.14) | collective-permute-done | bytes 65568 | tf_op jit(solution)/shard_map/ppermute | solution.py:278
  60.2 0.3 shard_map.98
  60.5 0.1 collective-permute-start.15
  60.6 1.5 %collective-permute-done.15.refs_1_ = bf16[128,1024]{1,0:T(8,128)(2,1)S(1)} collective-permute-done((bf16[128,1024]{1,0:T(8,128)(2,1)S(1)}, bf16[128,1024]{1,0:T(8,128)(2,1)S(1)}, u32[]{:S(2)}, u32[]{:S(2)}) %collective-permute-start.15) | collective-permute-done | bytes 262176 | tf_op jit(solution)/shard_map/ppermute | solution.py:278
  62.1 0.0 copy-start.1
  62.1 0.6 shard_map.99
  62.7 0.1 collective-permute-start.18
  62.8 3.2 %collective-permute-start.17 = (f32[8,256]{1,0:T(8,128)S(1)}, f32[8,256]{1,0:T(8,128)S(1)}, u32[]{:S(2)}, u32[]{:S(2)}) collective-permute-start(f32[8,256]{1,0:T(8,128)S(1)} %get-tuple-element.56.refs_1_), channel_id=1, source_target_pairs={{0,3},{1,0},{2,1},{3,2},{4,7},{5,4},{6,5},{7,6},{8,11},{9,8},{10,9... | collective-permute-start | bytes 24584 | tf_op jit(solution)/shard_map/ppermute | solution.py:278
  66.0 0.0 collective-permute-start.16
  66.0 1.6 %collective-permute-done.18.refs_4_ = f32[8,256]{1,0:T(8,128)S(1)} collective-permute-done((f32[8,256]{1,0:T(8,128)S(1)}, f32[8,256]{1,0:T(8,128)S(1)}, u32[]{:S(2)}, u32[]{:S(2)}) %collective-permute-start.18) | collective-permute-done | bytes 8224 | tf_op jit(solution)/shard_map/ppermute | solution.py:278
  67.7 0.0 collective-permute-done.17.refs_3_
  67.7 3.5 %collective-permute-done.16.refs_2_ = f32[8,256]{1,0:T(8,128)S(1)} collective-permute-done((f32[8,256]{1,0:T(8,128)S(1)}, f32[8,256]{1,0:T(8,128)S(1)}, u32[]{:S(2)}, u32[]{:S(2)}) %collective-permute-start.16) | collective-permute-done | bytes 8224 | tf_op jit(solution)/shard_map/ppermute | solution.py:278
  71.2 0.0 copy-done.1
  71.2 1.2 %shard_map.100 = bf16[256,2048]{1,0:T(8,128)(2,1)} custom-call(f32[256,2048]{1,0:T(8,128)S(1)} %get-tuple-element.55.refs_0_, f32[8,256]{1,0:T(8,128)S(1)} %get-tuple-element.56.refs_1_, f32[8,256]{1,0:T(8,128)S(1)} %collective-permute-done.16.refs_2_, f32[8,256]{1,0:T(8,128)S(1)} %collective-permute-done.17.refs_3_, ...), custom_call_target="tpu_custom_call" | custom-call | tf_op jit(solution)/shard_map/pallas_call | solution.py:34
  (1 shorter events, 0.0 us)
Async XLA Ops:
  0.0 6.8 %copy-start = (bf16[256,128]{1,0:T(8,128)(2,1)S(1)}, bf16[256,128]{1,0:T(8,128)(2,1)}, u32[]{:S(2)}) copy-start(bf16[256,128]{1,0:T(8,128)(2,1)} %refs_2_.1) | copy-start | bytes 196612
  0.0 6.8 %copy-start.7 = (f32[32]{0:T(128)S(1)}, f32[32]{0:T(128)}, u32[]{:S(2)}) copy-start(f32[32]{0:T(128)} %param.16) | copy-start | bytes 388
  0.0 6.8 %copy-start.6 = (f32[256]{0:T(256)S(1)}, f32[256]{0:T(256)}, u32[]{:S(2)}) copy-start(f32[256]{0:T(256)} %param.15) | copy-start | bytes 3076
  0.0 6.8 %copy-start.5 = (f32[32,256]{1,0:T(8,128)S(1)}, f32[32,256]{1,0:T(8,128)}, u32[]{:S(2)}) copy-start(f32[32,256]{1,0:T(8,128)} %refs_1_.1) | copy-start | bytes 98308
  0.0 6.8 %copy-start.4 = (f32[32,256]{1,0:T(8,128)S(1)}, f32[32,256]{1,0:T(8,128)}, u32[]{:S(2)}) copy-start(f32[32,256]{1,0:T(8,128)} %refs_0_.1) | copy-start | bytes 98308
  0.0 6.8 %copy-start.3 = (bf16[256,128]{1,0:T(8,128)(2,1)S(1)}, bf16[256,128]{1,0:T(8,128)(2,1)}, u32[]{:S(2)}) copy-start(bf16[256,128]{1,0:T(8,128)(2,1)} %refs_4_.1) | copy-start | bytes 196612
  0.0 6.8 %copy-start.2 = (bf16[256,2048]{1,0:T(8,128)(2,1)S(1)}, bf16[256,2048]{1,0:T(8,128)(2,1)}, u32[]{:S(2)}) copy-start(bf16[256,2048]{1,0:T(8,128)(2,1)} %refs_6_.1) | copy-start | bytes 3145732
  1.5 14.3 %collective-permute-start.2 = (bf16[64,2048]{1,0:T(8,128)(2,1)S(1)}, bf16[64,2048]{1,0:T(8,128)(2,1)S(1)}, u32[]{:S(2)}, u32[]{:S(2)}) collective-permute-start(bf16[64,2048]{1,0:T(8,128)(2,1)S(1)} %get-tuple-element.57), channel_id=1, source_target_pairs={{0,3},{1,0},{2,1},{3,2},{4,7},{5,4},{6,5},{7,6},{8,11},{9,8},{10,9... | collective-permute-start | bytes 786440 | tf_op jit(solution)/shard_map/ppermute | solution.py:278
  4.6 14.6 %collective-permute-start = (bf16[64,2048]{1,0:T(8,128)(2,1)S(1)}, bf16[64,2048]{1,0:T(8,128)(2,1)S(1)}, u32[]{:S(2)}, u32[]{:S(2)}) collective-permute-start(bf16[64,2048]{1,0:T(8,128)(2,1)S(1)} %get-tuple-element.58), channel_id=1, source_target_pairs={{0,1},{1,2},{2,3},{3,0},{4,5},{5,6},{6,7},{7,4},{8,9},{9,10},{10,1... | collective-permute-start | bytes 786440 | tf_op jit(solution)/shard_map/ppermute | solution.py:278
  4.6 14.6 %collective-permute-start.1 = (bf16[64,2048]{1,0:T(8,128)(2,1)S(1)}, bf16[64,2048]{1,0:T(8,128)(2,1)S(1)}, u32[]{:S(2)}, u32[]{:S(2)}) collective-permute-start(bf16[64,2048]{1,0:T(8,128)(2,1)S(1)} %get-tuple-element.60), channel_id=1, source_target_pairs={{0,2},{1,3},{2,0},{3,1},{4,6},{5,7},{6,4},{7,5},{8,10},{9,11},{10,... | collective-permute-start | bytes 786440 | tf_op jit(solution)/shard_map/ppermute | solution.py:278
  10.2 1.3 %collective-permute-start.3 = (f32[8,2048]{1,0:T(8,128)S(1)}, f32[8,2048]{1,0:T(8,128)S(1)}, u32[]{:S(2)}, u32[]{:S(2)}) collective-permute-start(f32[8,2048]{1,0:T(8,128)S(1)} %get-tuple-element.33.refs_2_.refs_6_), channel_id=1, source_target_pairs={{0,4},{4,0},{1,5},{5,1},{2,6},{6,2},{3,7},{7,3},{8,12},{12,8},{9,1... | collective-permute-start | bytes 196616 | tf_op jit(solution)/shard_map/ppermute | solution.py:278
  19.8 1.6 %collective-permute-start.4 = (bf16[128,1024]{1,0:T(8,128)(2,1)S(1)}, bf16[128,1024]{1,0:T(8,128)(2,1)S(1)}, u32[]{:S(2)}, u32[]{:S(2)}) collective-permute-start(bf16[128,1024]{1,0:T(8,128)(2,1)S(1)} %get-tuple-element.35), channel_id=1, source_target_pairs={{0,4},{4,0},{1,5},{5,1},{2,6},{6,2},{3,7},{7,3},{8,12},{12,8},{9,1... | collective-permute-start | bytes 786440 | tf_op jit(solution)/shard_map/ppermute | solution.py:278
  21.7 5.6 %collective-permute-start.5 = (bf16[144,256]{1,0:T(8,128)(2,1)S(1)}, bf16[144,256]{1,0:T(8,128)(2,1)S(1)}, u32[]{:S(2)}, u32[]{:S(2)}) collective-permute-start(bf16[144,256]{1,0:T(8,128)(2,1)S(1)} %get-tuple-element.42), channel_id=1, source_target_pairs={{0,8},{8,16},{16,24},{24,0},{1,9},{9,17},{17,25},{25,1},{2,10},{10... | collective-permute-start | bytes 221192 | tf_op jit(solution)/shard_map/ppermute | solution.py:278
  23.3 4.4 %collective-permute-start.6 = (bf16[144,256]{1,0:T(8,128)(2,1)S(1)}, bf16[144,256]{1,0:T(8,128)(2,1)S(1)}, u32[]{:S(2)}, u32[]{:S(2)}) collective-permute-start(bf16[144,256]{1,0:T(8,128)(2,1)S(1)} %get-tuple-element.43), channel_id=1, source_target_pairs={{0,24},{8,0},{16,8},{24,16},{1,25},{9,1},{17,9},{25,17},{2,26},{10... | collective-permute-start | bytes 221192 | tf_op jit(solution)/shard_map/ppermute | solution.py:278
  25.1 5.9 %collective-permute-start.7 = (bf16[144,256]{1,0:T(8,128)(2,1)S(1)}, bf16[144,256]{1,0:T(8,128)(2,1)S(1)}, u32[]{:S(2)}, u32[]{:S(2)}) collective-permute-start(bf16[144,256]{1,0:T(8,128)(2,1)S(1)} %get-tuple-element.44), channel_id=1, source_target_pairs={{0,16},{8,24},{16,0},{24,8},{1,17},{9,25},{17,1},{25,9},{2,18},{10... | collective-permute-start | bytes 221192 | tf_op jit(solution)/shard_map/ppermute | solution.py:278
  31.0 4.4 %collective-permute-start.9 = (bf16[144,256]{1,0:T(8,128)(2,1)S(1)}, bf16[144,256]{1,0:T(8,128)(2,1)S(1)}, u32[]{:S(2)}, u32[]{:S(2)}) collective-permute-start(bf16[144,256]{1,0:T(8,128)(2,1)S(1)} %get-tuple-element.45.refs_0_), channel_id=1, source_target_pairs={{0,224},{32,0},{64,32},{96,64},{128,96},{160,128},{192,160},{224,1... | collective-permute-start | bytes 221192 | tf_op jit(solution)/shard_map/ppermute | solution.py:278
  31.2 8.2 %collective-permute-start.8 = (bf16[144,256]{1,0:T(8,128)(2,1)S(1)}, bf16[144,256]{1,0:T(8,128)(2,1)S(1)}, u32[]{:S(2)}, u32[]{:S(2)}) collective-permute-start(bf16[144,256]{1,0:T(8,128)(2,1)S(1)} %get-tuple-element.45.refs_0_), channel_id=1, source_target_pairs={{0,32},{32,64},{64,96},{96,128},{128,160},{160,192},{192,224},{224... | collective-permute-start | bytes 221192 | tf_op jit(solution)/shard_map/ppermute | solution.py:278
  39.5 6.3 %collective-permute-start.11 = (bf16[144,256]{1,0:T(8,128)(2,1)S(1)}, bf16[144,256]{1,0:T(8,128)(2,1)S(1)}, u32[]{:S(2)}, u32[]{:S(2)}) collective-permute-start(bf16[144,256]{1,0:T(8,128)(2,1)S(1)} %shard_map.96), channel_id=1, source_target_pairs={{0,192},{32,224},{64,0},{96,32},{128,64},{160,96},{192,128},{224,1... | collective-permute-start | bytes 221192 | tf_op jit(solution)/shard_map/ppermute | solution.py:278
  42.4 8.5 %collective-permute-start.10 = (bf16[144,256]{1,0:T(8,128)(2,1)S(1)}, bf16[144,256]{1,0:T(8,128)(2,1)S(1)}, u32[]{:S(2)}, u32[]{:S(2)}) collective-permute-start(bf16[144,256]{1,0:T(8,128)(2,1)S(1)} %shard_map.96), channel_id=1, source_target_pairs={{0,96},{32,128},{64,160},{96,192},{128,224},{160,0},{192,32},{224,... | collective-permute-start | bytes 221192 | tf_op jit(solution)/shard_map/ppermute | solution.py:278
  51.1 5.6 %collective-permute-start.12 = (bf16[128,256]{1,0:T(8,128)(2,1)S(1)}, bf16[128,256]{1,0:T(8,128)(2,1)S(1)}, u32[]{:S(2)}, u32[]{:S(2)}) collective-permute-start(bf16[128,256]{1,0:T(8,128)(2,1)S(1)} %get-tuple-element.49), channel_id=1, source_target_pairs={{0,8},{8,16},{16,24},{24,0},{1,9},{9,17},{17,25},{25,1},{2,10},{10... | collective-permute-start | bytes 196616 | tf_op jit(solution)/shard_map/ppermute | solution.py:278
  51.5 5.1 %collective-permute-start.13 = (bf16[128,256]{1,0:T(8,128)(2,1)S(1)}, bf16[128,256]{1,0:T(8,128)(2,1)S(1)}, u32[]{:S(2)}, u32[]{:S(2)}) collective-permute-start(bf16[128,256]{1,0:T(8,128)(2,1)S(1)} %get-tuple-element.50), channel_id=1, source_target_pairs={{0,24},{8,0},{16,8},{24,16},{1,25},{9,1},{17,9},{25,17},{2,26},{10... | collective-permute-start | bytes 196616 | tf_op jit(solution)/shard_map/ppermute | solution.py:278
  54.4 5.8 %collective-permute-start.14 = (bf16[128,256]{1,0:T(8,128)(2,1)S(1)}, bf16[128,256]{1,0:T(8,128)(2,1)S(1)}, u32[]{:S(2)}, u32[]{:S(2)}) collective-permute-start(bf16[128,256]{1,0:T(8,128)(2,1)S(1)} %get-tuple-element.51), channel_id=1, source_target_pairs={{0,16},{8,24},{16,0},{24,8},{1,17},{9,25},{17,1},{25,9},{2,18},{10... | collective-permute-start | bytes 196616 | tf_op jit(solution)/shard_map/ppermute | solution.py:278
  60.5 1.6 %collective-permute-start.15 = (bf16[128,1024]{1,0:T(8,128)(2,1)S(1)}, bf16[128,1024]{1,0:T(8,128)(2,1)S(1)}, u32[]{:S(2)}, u32[]{:S(2)}) collective-permute-start(bf16[128,1024]{1,0:T(8,128)(2,1)S(1)} %get-tuple-element.53), channel_id=1, source_target_pairs={{0,4},{4,0},{1,5},{5,1},{2,6},{6,2},{3,7},{7,3},{8,12},{12,8},{9,1... | collective-permute-start | bytes 786440 | tf_op jit(solution)/shard_map/ppermute | solution.py:278
  62.1 9.1 %copy-start.1 = (f32[2048]{0:T(1024)S(1)}, f32[2048]{0:T(1024)}, u32[]{:S(2)}) copy-start(f32[2048]{0:T(1024)} %param.17) | copy-start | bytes 24580
  62.7 4.9 %collective-permute-start.18 = (f32[8,256]{1,0:T(8,128)S(1)}, f32[8,256]{1,0:T(8,128)S(1)}, u32[]{:S(2)}, u32[]{:S(2)}) collective-permute-start(f32[8,256]{1,0:T(8,128)S(1)} %get-tuple-element.56.refs_1_), channel_id=1, source_target_pairs={{0,1},{1,2},{2,3},{3,0},{4,5},{5,6},{6,7},{7,4},{8,9},{9,10},{10,1... | collective-permute-start | bytes 24584 | tf_op jit(solution)/shard_map/ppermute | solution.py:278
  62.8 4.9 %collective-permute-start.17 = (f32[8,256]{1,0:T(8,128)S(1)}, f32[8,256]{1,0:T(8,128)S(1)}, u32[]{:S(2)}, u32[]{:S(2)}) collective-permute-start(f32[8,256]{1,0:T(8,128)S(1)} %get-tuple-element.56.refs_1_), channel_id=1, source_target_pairs={{0,3},{1,0},{2,1},{3,2},{4,7},{5,4},{6,5},{7,6},{8,11},{9,8},{10,9... | collective-permute-start | bytes 24584 | tf_op jit(solution)/shard_map/ppermute | solution.py:278
  66.0 5.2 %collective-permute-start.16 = (f32[8,256]{1,0:T(8,128)S(1)}, f32[8,256]{1,0:T(8,128)S(1)}, u32[]{:S(2)}, u32[]{:S(2)}) collective-permute-start(f32[8,256]{1,0:T(8,128)S(1)} %get-tuple-element.56.refs_1_), channel_id=1, source_target_pairs={{0,2},{1,3},{2,0},{3,1},{4,6},{5,7},{6,4},{7,5},{8,10},{9,11},{10,... | collective-permute-start | bytes 24584 | tf_op jit(solution)/shard_map/ppermute | solution.py:278

commit v4 on v3

--- a/solution.py
+++ b/solution.py
@@ -19,7 +19,8 @@
 FEATS = HERE * HEAD_DIM
 HALF = FEATS // 2
 PART = HALF // 4
-STEPS = (0, 1, 3, 2)
+ROUND_Y = (0, 2, 3, 1)
+ROUND_X = (0, 1, 2, 3)
 LOGS = 16
 
 
@@ -145,7 +146,7 @@
 
 
 def end_state(x0, x1, x2, x3, dtt_ref, bt_ref, x_ref, keep_ref, send_ref, local):
-    for k, piece in enumerate((x0, x1, x2, x3)):
+    for k, piece in zip(ROUND_Y, (x0, x1, x2, x3)):
         at = pl.multiple_of(place("head", -k, 4) * 64, 64)
         x_ref[pl.ds(at, 64), :] = piece[...]
     for at in range(0, FEATS, 256):
@@ -187,12 +188,12 @@
         jnp.exp(log1) * pick(core, keep, came) + pick(core, came, keep)
     ).astype(BF16)
     message[STATE:, :] = log_block(log0 + log1)
-    for k, out in zip(STEPS, (s0, s1, s2, s3)):
+    for k, out in zip(ROUND_X, (s0, s1, s2, s3)):
         out[...] = message[:, pl.ds(pl.multiple_of(place("x", k, 4) * PART, PART), PART)]
 
 
-def row_state(m0, m1, m2, m3, all_ref, row_ref, state_ref):
-    for k, piece in zip(STEPS, (m0, m1, m2, m3)):
+def row_state(m0, m1, m2, m3, all_ref, row_ref):
+    for k, piece in zip(ROUND_X, (m0, m1, m2, m3)):
         all_ref[place("x", -k, 4)] = piece[...]
     state = state_of(all_ref[0])
     logs = logs_of(all_ref[0])
@@ -200,38 +201,38 @@
         log = logs_of(all_ref[x])
         state = jnp.exp(log) * state + state_of(all_ref[x])
         logs = logs + log
-    state_ref[...] = state
     row_ref[:STATE, :] = state.astype(BF16)
     row_ref[STATE:, :] = log_block(logs)
 
 
-def window(row_ref, state_ref, before_ref, after_ref, out_ref):
-    z = lax.axis_index("z")
-    log, log_after = logs_of(row_ref[...]), logs_of(after_ref[...])
-    before = state_of(before_ref[...])
-    before = pick(z, jnp.zeros_like(before), before)
-    state = jnp.exp(log_after) * (jnp.exp(log) * before + state_ref[...])
-    state = pick(7 - z, jnp.zeros_like(state), state) + state_of(after_ref[...])
-    out_ref[:STATE, :] = state.astype(BF16)
-    out_ref[STATE:, :] = log_block(log + log_after + logs_of(before_ref[...]))
-
-
-def enter(before_ref, w3, w6, all_ref, e0, e1, e2, e3, every):
-    z = lax.axis_index("z")
-    state = jnp.zeros((STATE, PART), F32)
-    for least, piece in ((5, w6), (2, w3), (1, before_ref)):
-        there = pick(lax.div(z, least), jnp.zeros_like(state), state_of(piece[...]))
-        state = jnp.exp(logs_of(piece[...])) * state + there
+def four_rows(r0, r1, r2, r3, inner_ref, logs_ref, total_ref, rows):
+    for k, piece in enumerate((r0, r1, r2, r3)):
+        rows[lax.rem(lax.axis_index("z") + 4 - k, 4)] = piece[...]
+    me = lax.rem(lax.axis_index("z"), 4)
+    state, logs = state_of(rows[0]), logs_of(rows[0])
+    inner, before = jnp.zeros_like(state), jnp.zeros_like(logs)
+    for z in range(1, 4):
+        inner, before = pick(me - z, state, inner), pick(me - z, logs, before)
+        log = logs_of(rows[z])
+        state = jnp.exp(log) * state + state_of(rows[z])
+        logs = logs + log
+    inner_ref[...] = inner
+    logs_ref[...] = jnp.broadcast_to(before, (8, PART))
+    total_ref[...] = state.astype(BF16)
+
+
+def enter(inner_ref, logs_ref, far_ref, all_ref, e0, e1, e2, e3, every):
+    state = jnp.exp(logs_ref[:1, :]) * pick(lax.div(lax.axis_index("z"), 4), jnp.zeros((STATE, PART), F32), far_ref[...].astype(F32)) + inner_ref[...]
     for x in range(4):
         every[x] = state.astype(BF16)
         if x < 3:
             state = jnp.exp(logs_of(all_ref[x])) * state + state_of(all_ref[x])
-    for k, out in zip(STEPS, (e0, e1, e2, e3)):
+    for k, out in zip(ROUND_X, (e0, e1, e2, e3)):
         out[...] = every[place("x", k, 4)]
 
 
 def core_states(f0, f1, f2, f3, keep_ref, came_ref, tot_ref, tot_other_ref, own_ref, give_ref, chip):
-    for k, piece in zip(STEPS, (f0, f1, f2, f3)):
+    for k, piece in zip(ROUND_X, (f0, f1, f2, f3)):
         chip[:, pl.ds(pl.multiple_of(place("x", -k, 4) * PART, PART), PART)] = piece[...]
     core = lax.axis_index("core")
     log0, _ = halves(core, tot_ref, tot_other_ref)
@@ -285,9 +286,9 @@
 def on_device(inputs, gate, in_b, in_c, log_decay, step_size, importance, skip, norm_gain):
     y = lax.axis_index("head")
     pieces = [
-        lax.dynamic_slice(inputs, (0, lax.rem(y + k, 4) * FEATS), (64, FEATS)) for k in range(4)
+        lax.dynamic_slice(inputs, (0, lax.rem(y + k, 4) * FEATS), (64, FEATS)) for k in ROUND_Y
     ]
-    pieces = [pieces[0]] + triple(pieces, "head", (1, 2, 3))
+    pieces = [pieces[0]] + triple(pieces, "head", ROUND_Y[1:])
 
     big = (STRETCH, FEATS)
     weights, dt, dtt, q, g, b_t, tot, skip_row = kernel_call(
@@ -318,19 +319,23 @@
         scratch=[((STATE + LOGS, HALF), BF16)],
         after=[p],
     )
-    slices = [slices[0]] + triple(slices, "x", STEPS[1:])
-    chips, row, state = kernel_call(
-        row_state, [((4,) + message, BF16), (message, BF16), ((STATE, PART), F32)], *slices
-    )
-    before = shifted(row, "z", 1, 8)
-    after = shifted(row, "z", 7, 8)
-    (three,) = kernel_call(window, [(message, BF16)], row, state, before, after)
-    back = [shifted(three, "z", 3, 8), shifted(three, "z", 6, 8)]
+    slices = [slices[0]] + triple(slices, "x", ROUND_X[1:])
+    chips, row = kernel_call(
+        row_state, [((4,) + message, BF16), (message, BF16)], *slices
+    )
+    near = [
+        lax.ppermute(row, "z", [(i, i // 4 * 4 + (i + k) % 4) for i in range(8)]) for k in (1, 2, 3)
+    ]
+    inner, logs, total = kernel_call(
+        four_rows, [((STATE, PART), F32), ((8, PART), F32), ((STATE, PART), BF16)], row, *near,
+        scratch=[((4,) + message, BF16)],
+    )
+    far = lax.ppermute(total, "z", [(i, 7 - i) for i in range(8)])
     enters = kernel_call(
-        enter, [((STATE, PART), BF16)] * 4, before, *back, chips,
+        enter, [((STATE, PART), BF16)] * 4, inner, logs, far, chips,
         scratch=[((4, STATE, PART), BF16)],
     )
-    enters = [enters[0]] + triple(enters, "x", STEPS[1:])
+    enters = [enters[0]] + triple(enters, "x", ROUND_X[1:])
     own, give = kernel_call(
         core_states, [((STATE, HALF), BF16)] * 2, *enters, keep, came, tot, tot_other,
         scratch=[((STATE, HALF), BF16)],
@@ -340,7 +345,7 @@
         gate_all, [(big, F32), ((8, STRETCH), F32)], own, got, in_c, p, q,
         scratch=[((STATE, FEATS), BF16)],
     )
-    others = triple([sums] * 4, "head", (2, 3, 1))
+    others = triple([sums] * 4, "head", (1, 2, 3))
     (out,) = kernel_call(
         normalize, [(big, BF16)], gated, sums, *others, norm_gain.reshape(1, FEATS),
         scratch=[(big, BF16)], hbm_out=True, copies=4,

time: 72.9 us -> 67.1 us (0.920)
  waiting for transfers between devices: 39.2 us -> 23.7 us
  starting transfers between devices: 23.6 us -> 33.3 us
    ppermute x19 -> x15, waiting for transfers between devices: 39.2 us -> 18.6 us  [shifted(): return lax.ppermute(v, axis, [(i, (i + step) % size) for i in range(size)])]
    ppermute x0 -> x4, starting transfers between devices: none -> 12.2 us  [the longest x3 6.27 us: on_device(): lax.ppermute(row, 'z', [(i, i // 4 * 4 + (i + k) % 4) for i in range(8)])]
    ppermute x0 -> x4, waiting for transfers between devices: none -> 5.06 us  [the longest x3 2.81 us: on_device(): lax.ppermute(row, 'z', [(i, i // 4 * 4 + (i + k) % 4) for i in range(8)])]
    ppermute x19 -> x15, starting transfers between devices: 23.6 us -> 21 us  [shifted(): return lax.ppermute(v, axis, [(i, (i + step) % size) for i in range(size)])]
  transfers between devices with their start and end apart: 19 -> 19, of which waited for: 16 -> 14; matrix products, arithmetic and copies ran while one was open for 0% -> 0% of each run, Pallas kernels for 6% -> 7%
where the time goes in v4:
time: 67.1 us; the launch traced here: 66.7 us
  starting transfers between devices  33.3 us (50%)
  waiting for transfers between devices  23.7 us (35%)
  Pallas kernels  8.01 us (12%)
  local copies, waits for them, and re-layouts  1.41 us (2%)
    ppermute x15, starting transfers between devices, shifted(): return lax.ppermute(v, axis, [(i, (i + step) % size) for i in range(size)])  21 us
    ppermute x15, waiting for transfers between devices, shifted(): return lax.ppermute(v, axis, [(i, (i + step) % size) for i in range(size)])  18.6 us
    pallas_call x10, Pallas kernels, kernel_call(): pl.pallas_call(ordered, out_shape=[jax.ShapeDtypeStruct(s, d) for s, d in...  8.01 us
    ppermute x3, starting transfers between devices, on_device(): lax.ppermute(row, 'z', [(i, i // 4 * 4 + (i + k) % 4) for i in range(8)])  6.27 us
    ppermute x1, starting transfers between devices, on_device(): far = lax.ppermute(total, 'z', [(i, 7 - i) for i in range(8)])  5.94 us
    ppermute x3, waiting for transfers between devices, on_device(): lax.ppermute(row, 'z', [(i, i // 4 * 4 + (i + k) % 4) for i in range(8)])  2.81 us
    ppermute x1, waiting for transfers between devices, on_device(): far = lax.ppermute(total, 'z', [(i, 7 - i) for i in range(8)])  2.25 us
    dynamic_slice x1, local copies, waits for them, and re-layouts, on_device(): lax.dynamic_slice(inputs, (0, lax.rem(y + k, 4) * FEATS), (64, FEATS))  1.38 us
  transfers between devices with their start and end apart: 19, of which 14 were waited for; matrix products, arithmetic and copies ran while one was open for 0% of the time, Pallas kernels for 7%

profile of v4, /device:TPU:32, one launch (start us, length us, event | category | flops | bytes accessed | tf_op | source)
XLA Modules:
  0.0 66.7 jit_solution(13469496804586574756)
XLA Ops:
  0.0 0.0 copy-start
  0.0 0.0 copy-start.7
  0.0 0.0 copy-start.6
  0.0 0.0 copy-start.5
  0.0 0.0 copy-start.4
  0.0 0.0 copy-start.3
  0.0 0.0 copy-start.2
  0.1 1.4 %constant_dynamic-slice_fusion = (bf16[64,2048]{1,0:T(8,128)(2,1)S(1)}, bf16[64,2048]{1,0:T(8,128)(2,1)S(1)}, bf16[64,2048]{1,0:T(8,128)(2,1)S(1)}, bf16[64,2048]{1,0:T(8,128)(2,1)S(1)}) fusion(bf16[64,8192]{1,0:T(8,128)(2,1)} %param.9, s32[]{:T(128)S(6)} %select_n.15, s32[]{:T(128)S(6)} %select_n.13, s32[]{:T(128)S(6)} %select_n.12, s32[]{:T(128)S(6)} %select_n.14), kind=kLoop, calls=%fused_computation | loop fusion | bytes 2097168 | tf_op jit(solution)/shard_map/dynamic_slice | solution.py:289
  1.5 1.7 %collective-permute-start.2 = (bf16[64,2048]{1,0:T(8,128)(2,1)S(1)}, bf16[64,2048]{1,0:T(8,128)(2,1)S(1)}, u32[]{:S(2)}, u32[]{:S(2)}) collective-permute-start(bf16[64,2048]{1,0:T(8,128)(2,1)S(1)} %get-tuple-element.61), channel_id=1, source_target_pairs={{0,1},{1,2},{2,3},{3,0},{4,5},{5,6},{6,7},{7,4},{8,9},{9,10},{10,1... | collective-permute-start | bytes 786440 | tf_op jit(solution)/shard_map/ppermute | solution.py:279
  3.1 2.9 %collective-permute-start = (bf16[64,2048]{1,0:T(8,128)(2,1)S(1)}, bf16[64,2048]{1,0:T(8,128)(2,1)S(1)}, u32[]{:S(2)}, u32[]{:S(2)}) collective-permute-start(bf16[64,2048]{1,0:T(8,128)(2,1)S(1)} %get-tuple-element.62), channel_id=1, source_target_pairs={{0,2},{1,3},{2,0},{3,1},{4,6},{5,7},{6,4},{7,5},{8,10},{9,11},{10,... | collective-permute-start | bytes 786440 | tf_op jit(solution)/shard_map/ppermute | solution.py:279
  6.0 1.3 %collective-permute-start.1 = (bf16[64,2048]{1,0:T(8,128)(2,1)S(1)}, bf16[64,2048]{1,0:T(8,128)(2,1)S(1)}, u32[]{:S(2)}, u32[]{:S(2)}) collective-permute-start(bf16[64,2048]{1,0:T(8,128)(2,1)S(1)} %get-tuple-element.64), channel_id=1, source_target_pairs={{0,3},{1,0},{2,1},{3,2},{4,7},{5,4},{6,5},{7,6},{8,11},{9,8},{10,9... | collective-permute-start | bytes 786440 | tf_op jit(solution)/shard_map/ppermute | solution.py:279
  7.4 0.0 copy-done
  7.4 0.0 copy-done.7
  7.4 0.0 copy-done.6
  7.4 0.0 copy-done.5
  7.4 0.0 copy-done.4
  7.4 0.0 copy-done.3
  7.4 0.0 copy-done.2
  7.4 3.4 %shard_map.91 = (bf16[32,256,256]{2,1,0:T(8,128)(2,1)S(1)}, f32[256,2048]{1,0:T(8,128)S(1)}, f32[256,2048]{1,0:T(8,128)S(1)}, f32[256,2048]{1,0:T(8,128)S(1)}, f...) custom-call(f32[32,256]{1,0:T(8,128)S(1)} %copy-done.4, ...), custom_call_target="tpu_custom_call" | custom-call | flops 4294967296 | bytes 12582912 | tf_op jit(solution)/shard_map/pallas_call | solution.py:35
  10.9 0.1 collective-permute-start.3
  11.0 1.2 %collective-permute-done.3.refs_6_.refs_3_.refs_7_ = f32[8,2048]{1,0:T(8,128)S(1)} collective-permute-done((f32[8,2048]{1,0:T(8,128)S(1)}, f32[8,2048]{1,0:T(8,128)S(1)}, u32[]{:S(2)}, u32[]{:S(2)}) %collective-permute-start.3) | collective-permute-done | bytes 65568 | tf_op jit(solution)/shard_map/ppermute | solution.py:279
  12.2 0.0 collective-permute-done.2.refs_3_
  12.2 5.5 %collective-permute-done.refs_1_ = bf16[64,2048]{1,0:T(8,128)(2,1)S(1)} collective-permute-done((bf16[64,2048]{1,0:T(8,128)(2,1)S(1)}, bf16[64,2048]{1,0:T(8,128)(2,1)S(1)}, u32[]{:S(2)}, u32[]{:S(2)}) %collective-permute-start) | collective-permute-done | bytes 262176 | tf_op jit(solution)/shard_map/ppermute | solution.py:279
  17.7 0.0 collective-permute-done.1.refs_2_
  17.7 0.7 shard_map.92
  18.3 0.1 collective-permute-start.4
  18.4 1.2 %shard_map.93.refs_4_.refs_3_ = f32[256,2048]{1,0:T(8,128)S(1)} custom-call(bf16[256,2048]{1,0:T(8,128)(2,1)S(1)} %get-tuple-element.38.refs_0_, f32[256,2048]{1,0:T(8,128)S(1)} %get-tuple-element.39.refs_1_, bf16[32,256,256]{2,1,0:T(8,128)(2,1)S(1)} %get-tuple-element.40.refs_2_, f32[256,2048]{1,0:T(8,128)S(1)} %get-tuple-element.41.refs_3_, ...), custom_call_target="tpu_custom_call" | custom-call | flops 2147483648 | bytes 11534336 | tf_op jit(solution)/shard_map/pallas_call | solution.py:35
  19.6 0.3 collective-permute-done.4.refs_1_.refs_5_
  19.9 0.3 shard_map.94
  20.2 1.6 %collective-permute-start.5 = (bf16[144,256]{1,0:T(8,128)(2,1)S(1)}, bf16[144,256]{1,0:T(8,128)(2,1)S(1)}, u32[]{:S(2)}, u32[]{:S(2)}) collective-permute-start(bf16[144,256]{1,0:T(8,128)(2,1)S(1)} %get-tuple-element.44), channel_id=1, source_target_pairs={{0,8},{8,16},{16,24},{24,0},{1,9},{9,17},{17,25},{25,1},{2,10},{10... | collective-permute-start | bytes 221192 | tf_op jit(solution)/shard_map/ppermute | solution.py:279
  21.8 2.7 %collective-permute-start.6 = (bf16[144,256]{1,0:T(8,128)(2,1)S(1)}, bf16[144,256]{1,0:T(8,128)(2,1)S(1)}, u32[]{:S(2)}, u32[]{:S(2)}) collective-permute-start(bf16[144,256]{1,0:T(8,128)(2,1)S(1)} %get-tuple-element.45), channel_id=1, source_target_pairs={{0,16},{8,24},{16,0},{24,8},{1,17},{9,25},{17,1},{25,9},{2,18},{10... | collective-permute-start | bytes 221192 | tf_op jit(solution)/shard_map/ppermute | solution.py:279
  24.5 1.4 %collective-permute-start.7 = (bf16[144,256]{1,0:T(8,128)(2,1)S(1)}, bf16[144,256]{1,0:T(8,128)(2,1)S(1)}, u32[]{:S(2)}, u32[]{:S(2)}) collective-permute-start(bf16[144,256]{1,0:T(8,128)(2,1)S(1)} %get-tuple-element.46), channel_id=1, source_target_pairs={{0,24},{8,0},{16,8},{24,16},{1,25},{9,1},{17,9},{25,17},{2,26},{10... | collective-permute-start | bytes 221192 | tf_op jit(solution)/shard_map/ppermute | solution.py:279
  26.0 0.0 collective-permute-done.5.refs_1_
  26.0 2.5 %collective-permute-done.6.refs_2_ = bf16[144,256]{1,0:T(8,128)(2,1)S(1)} collective-permute-done((bf16[144,256]{1,0:T(8,128)(2,1)S(1)}, bf16[144,256]{1,0:T(8,128)(2,1)S(1)}, u32[]{:S(2)}, u32[]{:S(2)}) %collective-permute-start.6) | collective-permute-done | bytes 73760 | tf_op jit(solution)/shard_map/ppermute | solution.py:279
  28.4 0.4 collective-permute-done.7.refs_3_
  28.9 0.1 shard_map.95
  29.0 0.2 collective-permute-start.10
  29.2 3.3 %collective-permute-start.9 = (bf16[144,256]{1,0:T(8,128)(2,1)S(1)}, bf16[144,256]{1,0:T(8,128)(2,1)S(1)}, u32[]{:S(2)}, u32[]{:S(2)}) collective-permute-start(bf16[144,256]{1,0:T(8,128)(2,1)S(1)} %get-tuple-element.47.refs_0_), channel_id=1, source_target_pairs={{0,64},{32,96},{64,0},{96,32},{128,192},{160,224},{192,128},{224,1... | collective-permute-start | bytes 221192 | tf_op jit(solution)/shard_map/ppermute | solution.py:327
  32.4 2.8 %collective-permute-start.8 = (bf16[144,256]{1,0:T(8,128)(2,1)S(1)}, bf16[144,256]{1,0:T(8,128)(2,1)S(1)}, u32[]{:S(2)}, u32[]{:S(2)}) collective-permute-start(bf16[144,256]{1,0:T(8,128)(2,1)S(1)} %get-tuple-element.47.refs_0_), channel_id=1, source_target_pairs={{0,32},{32,64},{64,96},{96,0},{128,160},{160,192},{192,224},{224,1... | collective-permute-start | bytes 221192 | tf_op jit(solution)/shard_map/ppermute | solution.py:327
  35.3 0.0 collective-permute-done.10.refs_3_
  35.3 1.6 %collective-permute-done.9.refs_2_ = bf16[144,256]{1,0:T(8,128)(2,1)S(1)} collective-permute-done((bf16[144,256]{1,0:T(8,128)(2,1)S(1)}, bf16[144,256]{1,0:T(8,128)(2,1)S(1)}, u32[]{:S(2)}, u32[]{:S(2)}) %collective-permute-start.9) | collective-permute-done | bytes 73760 | tf_op jit(solution)/shard_map/ppermute | solution.py:327
  36.9 1.2 %collective-permute-done.8.refs_1_ = bf16[144,256]{1,0:T(8,128)(2,1)S(1)} collective-permute-done((bf16[144,256]{1,0:T(8,128)(2,1)S(1)}, bf16[144,256]{1,0:T(8,128)(2,1)S(1)}, u32[]{:S(2)}, u32[]{:S(2)}) %collective-permute-start.8) | collective-permute-done | bytes 73760 | tf_op jit(solution)/shard_map/ppermute | solution.py:327
  38.1 0.1 shard_map.96
  38.2 5.9 %collective-permute-start.11 = (bf16[128,256]{1,0:T(8,128)(2,1)S(1)}, bf16[128,256]{1,0:T(8,128)(2,1)S(1)}, u32[]{:S(2)}, u32[]{:S(2)}) collective-permute-start(bf16[128,256]{1,0:T(8,128)(2,1)S(1)} %get-tuple-element.50), channel_id=1, source_target_pairs={{0,224},{32,192},{64,160},{96,128},{128,96},{160,64},{192,32},{224... | collective-permute-start | bytes 196616 | tf_op jit(solution)/shard_map/ppermute | solution.py:333
  44.1 2.2 %collective-permute-done.11.refs_2_ = bf16[128,256]{1,0:T(8,128)(2,1)S(1)} collective-permute-done((bf16[128,256]{1,0:T(8,128)(2,1)S(1)}, bf16[128,256]{1,0:T(8,128)(2,1)S(1)}, u32[]{:S(2)}, u32[]{:S(2)}) %collective-permute-start.11) | collective-permute-done | bytes 65568 | tf_op jit(solution)/shard_map/ppermute | solution.py:333
  46.4 0.1 shard_map.97
  46.5 0.4 collective-permute-start.12
  46.9 3.4 %collective-permute-start.13 = (bf16[128,256]{1,0:T(8,128)(2,1)S(1)}, bf16[128,256]{1,0:T(8,128)(2,1)S(1)}, u32[]{:S(2)}, u32[]{:S(2)}) collective-permute-start(bf16[128,256]{1,0:T(8,128)(2,1)S(1)} %get-tuple-element.54), channel_id=1, source_target_pairs={{0,16},{8,24},{16,0},{24,8},{1,17},{9,25},{17,1},{25,9},{2,18},{10... | collective-permute-start | bytes 196616 | tf_op jit(solution)/shard_map/ppermute | solution.py:279
  50.2 1.3 %collective-permute-start.14 = (bf16[128,256]{1,0:T(8,128)(2,1)S(1)}, bf16[128,256]{1,0:T(8,128)(2,1)S(1)}, u32[]{:S(2)}, u32[]{:S(2)}) collective-permute-start(bf16[128,256]{1,0:T(8,128)(2,1)S(1)} %get-tuple-element.55), channel_id=1, source_target_pairs={{0,24},{8,0},{16,8},{24,16},{1,25},{9,1},{17,9},{25,17},{2,26},{10... | collective-permute-start | bytes 196616 | tf_op jit(solution)/shard_map/ppermute | solution.py:279
  51.6 0.5 collective-permute-done.12.refs_1_
  52.1 1.1 %collective-permute-done.13.refs_2_ = bf16[128,256]{1,0:T(8,128)(2,1)S(1)} collective-permute-done((bf16[128,256]{1,0:T(8,128)(2,1)S(1)}, bf16[128,256]{1,0:T(8,128)(2,1)S(1)}, u32[]{:S(2)}, u32[]{:S(2)}) %collective-permute-start.13) | collective-permute-done | bytes 65568 | tf_op jit(solution)/shard_map/ppermute | solution.py:279
  53.2 1.3 %collective-permute-done.14.refs_3_ = bf16[128,256]{1,0:T(8,128)(2,1)S(1)} collective-permute-done((bf16[128,256]{1,0:T(8,128)(2,1)S(1)}, bf16[128,256]{1,0:T(8,128)(2,1)S(1)}, u32[]{:S(2)}, u32[]{:S(2)}) %collective-permute-start.14) | collective-permute-done | bytes 65568 | tf_op jit(solution)/shard_map/ppermute | solution.py:279
  54.5 0.3 shard_map.98
  54.8 0.1 collective-permute-start.15
  54.9 1.5 %collective-permute-done.15.refs_1_ = bf16[128,1024]{1,0:T(8,128)(2,1)S(1)} collective-permute-done((bf16[128,1024]{1,0:T(8,128)(2,1)S(1)}, bf16[128,1024]{1,0:T(8,128)(2,1)S(1)}, u32[]{:S(2)}, u32[]{:S(2)}) %collective-permute-start.15) | collective-permute-done | bytes 262176 | tf_op jit(solution)/shard_map/ppermute | solution.py:279
  56.5 0.6 shard_map.99
  57.1 2.2 %collective-permute-start.18 = (f32[8,256]{1,0:T(8,128)S(1)}, f32[8,256]{1,0:T(8,128)S(1)}, u32[]{:S(2)}, u32[]{:S(2)}) collective-permute-start(f32[8,256]{1,0:T(8,128)S(1)} %get-tuple-element.60.refs_1_), channel_id=1, source_target_pairs={{0,3},{1,0},{2,1},{3,2},{4,7},{5,4},{6,5},{7,6},{8,11},{9,8},{10,9... | collective-permute-start | bytes 24584 | tf_op jit(solution)/shard_map/ppermute | solution.py:279
  59.3 1.2 %collective-permute-start.17 = (f32[8,256]{1,0:T(8,128)S(1)}, f32[8,256]{1,0:T(8,128)S(1)}, u32[]{:S(2)}, u32[]{:S(2)}) collective-permute-start(f32[8,256]{1,0:T(8,128)S(1)} %get-tuple-element.60.refs_1_), channel_id=1, source_target_pairs={{0,2},{1,3},{2,0},{3,1},{4,6},{5,7},{6,4},{7,5},{8,10},{9,11},{10,... | collective-permute-start | bytes 24584 | tf_op jit(solution)/shard_map/ppermute | solution.py:279
  60.5 0.7 %collective-permute-start.16 = (f32[8,256]{1,0:T(8,128)S(1)}, f32[8,256]{1,0:T(8,128)S(1)}, u32[]{:S(2)}, u32[]{:S(2)}) collective-permute-start(f32[8,256]{1,0:T(8,128)S(1)} %get-tuple-element.60.refs_1_), channel_id=1, source_target_pairs={{0,1},{1,2},{2,3},{3,0},{4,5},{5,6},{6,7},{7,4},{8,9},{9,10},{10,1... | collective-permute-start | bytes 24584 | tf_op jit(solution)/shard_map/ppermute | solution.py:279
  61.1 0.0 collective-permute-done.18.refs_4_
  61.1 3.3 %collective-permute-done.17.refs_3_ = f32[8,256]{1,0:T(8,128)S(1)} collective-permute-done((f32[8,256]{1,0:T(8,128)S(1)}, f32[8,256]{1,0:T(8,128)S(1)}, u32[]{:S(2)}, u32[]{:S(2)}) %collective-permute-start.17) | collective-permute-done | bytes 8224 | tf_op jit(solution)/shard_map/ppermute | solution.py:279
  64.5 0.9 %collective-permute-done.16.refs_2_ = f32[8,256]{1,0:T(8,128)S(1)} collective-permute-done((f32[8,256]{1,0:T(8,128)S(1)}, f32[8,256]{1,0:T(8,128)S(1)}, u32[]{:S(2)}, u32[]{:S(2)}) %collective-permute-start.16) | collective-permute-done | bytes 8224 | tf_op jit(solution)/shard_map/ppermute | solution.py:279
  65.3 0.0 copy-done.1
  65.3 1.2 %shard_map.100 = bf16[256,2048]{1,0:T(8,128)(2,1)} custom-call(f32[256,2048]{1,0:T(8,128)S(1)} %get-tuple-element.59.refs_0_, f32[8,256]{1,0:T(8,128)S(1)} %get-tuple-element.60.refs_1_, f32[8,256]{1,0:T(8,128)S(1)} %collective-permute-done.16.refs_2_, f32[8,256]{1,0:T(8,128)S(1)} %collective-permute-done.17.refs_3_, ...), custom_call_target="tpu_custom_call" | custom-call | tf_op jit(solution)/shard_map/pallas_call | solution.py:35
  (1 shorter events, 0.0 us)
Async XLA Ops:
  0.0 7.4 %copy-start = (bf16[256,128]{1,0:T(8,128)(2,1)S(1)}, bf16[256,128]{1,0:T(8,128)(2,1)}, u32[]{:S(2)}) copy-start(bf16[256,128]{1,0:T(8,128)(2,1)} %refs_2_.1) | copy-start | bytes 196612
  0.0 7.4 %copy-start.7 = (f32[32]{0:T(128)S(1)}, f32[32]{0:T(128)}, u32[]{:S(2)}) copy-start(f32[32]{0:T(128)} %param.16) | copy-start | bytes 388
  0.0 7.4 %copy-start.6 = (f32[256]{0:T(256)S(1)}, f32[256]{0:T(256)}, u32[]{:S(2)}) copy-start(f32[256]{0:T(256)} %param.15) | copy-start | bytes 3076
  0.0 7.4 %copy-start.5 = (f32[32,256]{1,0:T(8,128)S(1)}, f32[32,256]{1,0:T(8,128)}, u32[]{:S(2)}) copy-start(f32[32,256]{1,0:T(8,128)} %refs_1_.1) | copy-start | bytes 98308
  0.0 7.4 %copy-start.4 = (f32[32,256]{1,0:T(8,128)S(1)}, f32[32,256]{1,0:T(8,128)}, u32[]{:S(2)}) copy-start(f32[32,256]{1,0:T(8,128)} %refs_0_.1) | copy-start | bytes 98308
  0.0 7.4 %copy-start.3 = (bf16[256,128]{1,0:T(8,128)(2,1)S(1)}, bf16[256,128]{1,0:T(8,128)(2,1)}, u32[]{:S(2)}) copy-start(bf16[256,128]{1,0:T(8,128)(2,1)} %refs_4_.1) | copy-start | bytes 196612
  0.0 7.4 %copy-start.2 = (bf16[256,2048]{1,0:T(8,128)(2,1)S(1)}, bf16[256,2048]{1,0:T(8,128)(2,1)}, u32[]{:S(2)}) copy-start(bf16[256,2048]{1,0:T(8,128)(2,1)} %refs_6_.1) | copy-start | bytes 3145732
  1.5 10.7 %collective-permute-start.2 = (bf16[64,2048]{1,0:T(8,128)(2,1)S(1)}, bf16[64,2048]{1,0:T(8,128)(2,1)S(1)}, u32[]{:S(2)}, u32[]{:S(2)}) collective-permute-start(bf16[64,2048]{1,0:T(8,128)(2,1)S(1)} %get-tuple-element.61), channel_id=1, source_target_pairs={{0,1},{1,2},{2,3},{3,0},{4,5},{5,6},{6,7},{7,4},{8,9},{9,10},{10,1... | collective-permute-start | bytes 786440 | tf_op jit(solution)/shard_map/ppermute | solution.py:279
  3.1 14.5 %collective-permute-start = (bf16[64,2048]{1,0:T(8,128)(2,1)S(1)}, bf16[64,2048]{1,0:T(8,128)(2,1)S(1)}, u32[]{:S(2)}, u32[]{:S(2)}) collective-permute-start(bf16[64,2048]{1,0:T(8,128)(2,1)S(1)} %get-tuple-element.62), channel_id=1, source_target_pairs={{0,2},{1,3},{2,0},{3,1},{4,6},{5,7},{6,4},{7,5},{8,10},{9,11},{10,... | collective-permute-start | bytes 786440 | tf_op jit(solution)/shard_map/ppermute | solution.py:279
  6.0 11.6 %collective-permute-start.1 = (bf16[64,2048]{1,0:T(8,128)(2,1)S(1)}, bf16[64,2048]{1,0:T(8,128)(2,1)S(1)}, u32[]{:S(2)}, u32[]{:S(2)}) collective-permute-start(bf16[64,2048]{1,0:T(8,128)(2,1)S(1)} %get-tuple-element.64), channel_id=1, source_target_pairs={{0,3},{1,0},{2,1},{3,2},{4,7},{5,4},{6,5},{7,6},{8,11},{9,8},{10,9... | collective-permute-start | bytes 786440 | tf_op jit(solution)/shard_map/ppermute | solution.py:279
  10.9 1.3 %collective-permute-start.3 = (f32[8,2048]{1,0:T(8,128)S(1)}, f32[8,2048]{1,0:T(8,128)S(1)}, u32[]{:S(2)}, u32[]{:S(2)}) collective-permute-start(f32[8,2048]{1,0:T(8,128)S(1)} %get-tuple-element.35.refs_2_.refs_6_), channel_id=1, source_target_pairs={{0,4},{4,0},{1,5},{5,1},{2,6},{6,2},{3,7},{7,3},{8,12},{12,8},{9,1... | collective-permute-start | bytes 196616 | tf_op jit(solution)/shard_map/ppermute | solution.py:279
  18.3 1.6 %collective-permute-start.4 = (bf16[128,1024]{1,0:T(8,128)(2,1)S(1)}, bf16[128,1024]{1,0:T(8,128)(2,1)S(1)}, u32[]{:S(2)}, u32[]{:S(2)}) collective-permute-start(bf16[128,1024]{1,0:T(8,128)(2,1)S(1)} %get-tuple-element.37), channel_id=1, source_target_pairs={{0,4},{4,0},{1,5},{5,1},{2,6},{6,2},{3,7},{7,3},{8,12},{12,8},{9,1... | collective-permute-start | bytes 786440 | tf_op jit(solution)/shard_map/ppermute | solution.py:279
  20.2 5.7 %collective-permute-start.5 = (bf16[144,256]{1,0:T(8,128)(2,1)S(1)}, bf16[144,256]{1,0:T(8,128)(2,1)S(1)}, u32[]{:S(2)}, u32[]{:S(2)}) collective-permute-start(bf16[144,256]{1,0:T(8,128)(2,1)S(1)} %get-tuple-element.44), channel_id=1, source_target_pairs={{0,8},{8,16},{16,24},{24,0},{1,9},{9,17},{17,25},{25,1},{2,10},{10... | collective-permute-start | bytes 221192 | tf_op jit(solution)/shard_map/ppermute | solution.py:279
  21.8 6.6 %collective-permute-start.6 = (bf16[144,256]{1,0:T(8,128)(2,1)S(1)}, bf16[144,256]{1,0:T(8,128)(2,1)S(1)}, u32[]{:S(2)}, u32[]{:S(2)}) collective-permute-start(bf16[144,256]{1,0:T(8,128)(2,1)S(1)} %get-tuple-element.45), channel_id=1, source_target_pairs={{0,16},{8,24},{16,0},{24,8},{1,17},{9,25},{17,1},{25,9},{2,18},{10... | collective-permute-start | bytes 221192 | tf_op jit(solution)/shard_map/ppermute | solution.py:279
  24.5 4.4 %collective-permute-start.7 = (bf16[144,256]{1,0:T(8,128)(2,1)S(1)}, bf16[144,256]{1,0:T(8,128)(2,1)S(1)}, u32[]{:S(2)}, u32[]{:S(2)}) collective-permute-start(bf16[144,256]{1,0:T(8,128)(2,1)S(1)} %get-tuple-element.46), channel_id=1, source_target_pairs={{0,24},{8,0},{16,8},{24,16},{1,25},{9,1},{17,9},{25,17},{2,26},{10... | collective-permute-start | bytes 221192 | tf_op jit(solution)/shard_map/ppermute | solution.py:279
  29.0 6.3 %collective-permute-start.10 = (bf16[144,256]{1,0:T(8,128)(2,1)S(1)}, bf16[144,256]{1,0:T(8,128)(2,1)S(1)}, u32[]{:S(2)}, u32[]{:S(2)}) collective-permute-start(bf16[144,256]{1,0:T(8,128)(2,1)S(1)} %get-tuple-element.47.refs_0_), channel_id=1, source_target_pairs={{0,96},{32,0},{64,32},{96,64},{128,224},{160,128},{192,160},{224,1... | collective-permute-start | bytes 221192 | tf_op jit(solution)/shard_map/ppermute | solution.py:327
  29.2 7.7 %collective-permute-start.9 = (bf16[144,256]{1,0:T(8,128)(2,1)S(1)}, bf16[144,256]{1,0:T(8,128)(2,1)S(1)}, u32[]{:S(2)}, u32[]{:S(2)}) collective-permute-start(bf16[144,256]{1,0:T(8,128)(2,1)S(1)} %get-tuple-element.47.refs_0_), channel_id=1, source_target_pairs={{0,64},{32,96},{64,0},{96,32},{128,192},{160,224},{192,128},{224,1... | collective-permute-start | bytes 221192 | tf_op jit(solution)/shard_map/ppermute | solution.py:327
  32.4 5.6 %collective-permute-start.8 = (bf16[144,256]{1,0:T(8,128)(2,1)S(1)}, bf16[144,256]{1,0:T(8,128)(2,1)S(1)}, u32[]{:S(2)}, u32[]{:S(2)}) collective-permute-start(bf16[144,256]{1,0:T(8,128)(2,1)S(1)} %get-tuple-element.47.refs_0_), channel_id=1, source_target_pairs={{0,32},{32,64},{64,96},{96,0},{128,160},{160,192},{192,224},{224,1... | collective-permute-start | bytes 221192 | tf_op jit(solution)/shard_map/ppermute | solution.py:327
  38.2 8.2 %collective-permute-start.11 = (bf16[128,256]{1,0:T(8,128)(2,1)S(1)}, bf16[128,256]{1,0:T(8,128)(2,1)S(1)}, u32[]{:S(2)}, u32[]{:S(2)}) collective-permute-start(bf16[128,256]{1,0:T(8,128)(2,1)S(1)} %get-tuple-element.50), channel_id=1, source_target_pairs={{0,224},{32,192},{64,160},{96,128},{128,96},{160,64},{192,32},{224... | collective-permute-start | bytes 196616 | tf_op jit(solution)/shard_map/ppermute | solution.py:333
  46.5 5.6 %collective-permute-start.12 = (bf16[128,256]{1,0:T(8,128)(2,1)S(1)}, bf16[128,256]{1,0:T(8,128)(2,1)S(1)}, u32[]{:S(2)}, u32[]{:S(2)}) collective-permute-start(bf16[128,256]{1,0:T(8,128)(2,1)S(1)} %get-tuple-element.53), channel_id=1, source_target_pairs={{0,8},{8,16},{16,24},{24,0},{1,9},{9,17},{17,25},{25,1},{2,10},{10... | collective-permute-start | bytes 196616 | tf_op jit(solution)/shard_map/ppermute | solution.py:279
  46.9 6.3 %collective-permute-start.13 = (bf16[128,256]{1,0:T(8,128)(2,1)S(1)}, bf16[128,256]{1,0:T(8,128)(2,1)S(1)}, u32[]{:S(2)}, u32[]{:S(2)}) collective-permute-start(bf16[128,256]{1,0:T(8,128)(2,1)S(1)} %get-tuple-element.54), channel_id=1, source_target_pairs={{0,16},{8,24},{16,0},{24,8},{1,17},{9,25},{17,1},{25,9},{2,18},{10... | collective-permute-start | bytes 196616 | tf_op jit(solution)/shard_map/ppermute | solution.py:279
  50.2 4.3 %collective-permute-start.14 = (bf16[128,256]{1,0:T(8,128)(2,1)S(1)}, bf16[128,256]{1,0:T(8,128)(2,1)S(1)}, u32[]{:S(2)}, u32[]{:S(2)}) collective-permute-start(bf16[128,256]{1,0:T(8,128)(2,1)S(1)} %get-tuple-element.55), channel_id=1, source_target_pairs={{0,24},{8,0},{16,8},{24,16},{1,25},{9,1},{17,9},{25,17},{2,26},{10... | collective-permute-start | bytes 196616 | tf_op jit(solution)/shard_map/ppermute | solution.py:279
  54.8 1.6 %collective-permute-start.15 = (bf16[128,1024]{1,0:T(8,128)(2,1)S(1)}, bf16[128,1024]{1,0:T(8,128)(2,1)S(1)}, u32[]{:S(2)}, u32[]{:S(2)}) collective-permute-start(bf16[128,1024]{1,0:T(8,128)(2,1)S(1)} %get-tuple-element.57), channel_id=1, source_target_pairs={{0,4},{4,0},{1,5},{5,1},{2,6},{6,2},{3,7},{7,3},{8,12},{12,8},{9,1... | collective-permute-start | bytes 786440 | tf_op jit(solution)/shard_map/ppermute | solution.py:279
  56.5 8.9 %copy-start.1 = (f32[2048]{0:T(1024)S(1)}, f32[2048]{0:T(1024)}, u32[]{:S(2)}) copy-start(f32[2048]{0:T(1024)} %param.17) | copy-start | bytes 24580
  57.1 4.1 %collective-permute-start.18 = (f32[8,256]{1,0:T(8,128)S(1)}, f32[8,256]{1,0:T(8,128)S(1)}, u32[]{:S(2)}, u32[]{:S(2)}) collective-permute-start(f32[8,256]{1,0:T(8,128)S(1)} %get-tuple-element.60.refs_1_), channel_id=1, source_target_pairs={{0,3},{1,0},{2,1},{3,2},{4,7},{5,4},{6,5},{7,6},{8,11},{9,8},{10,9... | collective-permute-start | bytes 24584 | tf_op jit(solution)/shard_map/ppermute | solution.py:279
  59.3 5.2 %collective-permute-start.17 = (f32[8,256]{1,0:T(8,128)S(1)}, f32[8,256]{1,0:T(8,128)S(1)}, u32[]{:S(2)}, u32[]{:S(2)}) collective-permute-start(f32[8,256]{1,0:T(8,128)S(1)} %get-tuple-element.60.refs_1_), channel_id=1, source_target_pairs={{0,2},{1,3},{2,0},{3,1},{4,6},{5,7},{6,4},{7,5},{8,10},{9,11},{10,... | collective-permute-start | bytes 24584 | tf_op jit(solution)/shard_map/ppermute | solution.py:279
  60.5 4.9 %collective-permute-start.16 = (f32[8,256]{1,0:T(8,128)S(1)}, f32[8,256]{1,0:T(8,128)S(1)}, u32[]{:S(2)}, u32[]{:S(2)}) collective-permute-start(f32[8,256]{1,0:T(8,128)S(1)} %get-tuple-element.60.refs_1_), channel_id=1, source_target_pairs={{0,1},{1,2},{2,3},{3,0},{4,5},{5,6},{6,7},{7,4},{8,9},{9,10},{10,1... | collective-permute-start | bytes 24584 | tf_op jit(solution)/shard_map/ppermute | solution.py:279

commit v5 on v4

--- a/solution.py
+++ b/solution.py
@@ -145,8 +145,11 @@
         ).astype(BF16)
 
 
-def end_state(x0, x1, x2, x3, dtt_ref, bt_ref, x_ref, keep_ref, send_ref, local):
-    for k, piece in zip(ROUND_Y, (x0, x1, x2, x3)):
+def end_state(all_ref, x1, x2, x3, dtt_ref, bt_ref, x_ref, keep_ref, send_ref, local):
+    y = lax.axis_index("head")
+    own = pl.ds(pl.multiple_of(y * FEATS, FEATS), FEATS)
+    x_ref[pl.ds(pl.multiple_of(y * 64, 64), 64), :] = all_ref[:, own]
+    for k, piece in zip(ROUND_Y[1:], (x1, x2, x3)):
         at = pl.multiple_of(place("head", -k, 4) * 64, 64)
         x_ref[pl.ds(at, 64), :] = piece[...]
     for at in range(0, FEATS, 256):
@@ -286,9 +289,9 @@
 def on_device(inputs, gate, in_b, in_c, log_decay, step_size, importance, skip, norm_gain):
     y = lax.axis_index("head")
     pieces = [
-        lax.dynamic_slice(inputs, (0, lax.rem(y + k, 4) * FEATS), (64, FEATS)) for k in ROUND_Y
+        lax.dynamic_slice(inputs, (0, lax.rem(y + k, 4) * FEATS), (64, FEATS)) for k in ROUND_Y[1:]
     ]
-    pieces = [pieces[0]] + triple(pieces, "head", ROUND_Y[1:])
+    pieces = triple([inputs] + pieces, "head", ROUND_Y[1:])
 
     big = (STRETCH, FEATS)
     weights, dt, dtt, q, g, b_t, tot, skip_row = kernel_call(
@@ -303,25 +306,25 @@
     x, keep, send = kernel_call(
         end_state,
         [(big, BF16), ((STATE, HALF), F32), ((STATE, HALF), BF16)],
-        *pieces, dtt, b_t,
+        inputs, *pieces, dtt, b_t,
         scratch=[((STATE, FEATS), F32)],
         after=[tot_other],
         flops=1 << 28, bytes_accessed=4 << 20,
     )
     came = shifted(send, "core", 1, 2)
-    (p,) = kernel_call(
-        inside, [(big, F32)], x, dt, weights, g, skip_row, flops=2 << 30, bytes_accessed=11 << 20
-    )
 
     message = (STATE + LOGS, PART)
     slices = kernel_call(
         chip_state, [(message, BF16)] * 4, keep, came, tot, tot_other,
         scratch=[((STATE + LOGS, HALF), BF16)],
-        after=[p],
+    )
+    (p,) = kernel_call(
+        inside, [(big, F32)], x, dt, weights, g, skip_row, after=[slices[0]],
+        flops=2 << 30, bytes_accessed=11 << 20,
     )
     slices = [slices[0]] + triple(slices, "x", ROUND_X[1:])
     chips, row = kernel_call(
-        row_state, [((4,) + message, BF16), (message, BF16)], *slices
+        row_state, [((4,) + message, BF16), (message, BF16)], *slices, after=[p]
     )
     near = [
         lax.ppermute(row, "z", [(i, i // 4 * 4 + (i + k) % 4) for i in range(8)]) for k in (1, 2, 3)

time: 67.1 us -> 66.7 us (level)
  local copies, waits for them, and re-layouts: 1.41 us -> 6.92 us
  waiting for transfers between devices: 23.7 us -> 19.1 us
  starting transfers between devices: 33.3 us -> 31.9 us
    unnamed x16 -> x20, local copies, waits for them, and re-layouts: 0.03 us -> 5.76 us
    ppermute x15, waiting for transfers between devices: 18.6 us -> 14.2 us  [shifted(): return lax.ppermute(v, axis, [(i, (i + step) % size) for i in range(size)])]
    ppermute x15, starting transfers between devices: 21 us -> 19.7 us  [shifted(): return lax.ppermute(v, axis, [(i, (i + step) % size) for i in range(size)])]
  transfers between devices with their start and end apart: 19 -> 19, of which waited for: 14 -> 15; matrix products, arithmetic and copies ran while one was open for 0% -> 0% of each run, Pallas kernels for 7% -> 7%
where the time goes in v5:
time: 66.7 us; the launch traced here: 66.2 us
  starting transfers between devices  31.9 us (48%)
  waiting for transfers between devices  19.1 us (29%)
  Pallas kernels  7.94 us (12%)
  local copies, waits for them, and re-layouts  6.92 us (10%)
    ppermute x15, starting transfers between devices, shifted(): return lax.ppermute(v, axis, [(i, (i + step) % size) for i in range(size)])  19.7 us
    ppermute x15, waiting for transfers between devices, shifted(): return lax.ppermute(v, axis, [(i, (i + step) % size) for i in range(size)])  14.2 us
    pallas_call x10, Pallas kernels, kernel_call(): pl.pallas_call(ordered, out_shape=[jax.ShapeDtypeStruct(s, d) for s, d in...  7.94 us
    ppermute x3, starting transfers between devices, on_device(): lax.ppermute(row, 'z', [(i, i // 4 * 4 + (i + k) % 4) for i in range(8)])  6.27 us
    ppermute x1, starting transfers between devices, on_device(): far = lax.ppermute(total, 'z', [(i, 7 - i) for i in range(8)])  5.95 us
    unnamed x20, local copies, waits for them, and re-layouts  5.76 us
    ppermute x3, waiting for transfers between devices, on_device(): lax.ppermute(row, 'z', [(i, i // 4 * 4 + (i + k) % 4) for i in range(8)])  2.64 us
    ppermute x1, waiting for transfers between devices, on_device(): far = lax.ppermute(total, 'z', [(i, 7 - i) for i in range(8)])  2.25 us
  transfers between devices with their start and end apart: 19, of which 15 were waited for; matrix products, arithmetic and copies ran while one was open for 0% of the time, Pallas kernels for 7%

profile of v5, /device:TPU:32, one launch (start us, length us, event | category | flops | bytes accessed | tf_op | source)
XLA Modules:
  0.0 66.2 jit_solution(16755074558025743165)
XLA Ops:
  0.0 1.2 %constant_dynamic-slice_fusion = (bf16[64,2048]{1,0:T(8,128)(2,1)S(1)}, bf16[64,2048]{1,0:T(8,128)(2,1)S(1)}, bf16[64,2048]{1,0:T(8,128)(2,1)S(1)}) fusion(bf16[64,8192]{1,0:T(8,128)(2,1)} %refs_0_.3, s32[]{:T(128)S(6)} %select_n.11, s32[]{:T(128)S(6)} %select_n.10, s32[]{:T(128)S(6)} %select_n.9), kind=kLoop, calls=%fused_computation | loop fusion | bytes 1572876 | tf_op jit(solution)/shard_map/dynamic_slice | solution.py:292
  1.2 1.7 %collective-permute-start.2 = (bf16[64,2048]{1,0:T(8,128)(2,1)S(1)}, bf16[64,2048]{1,0:T(8,128)(2,1)S(1)}, u32[]{:S(2)}, u32[]{:S(2)}) collective-permute-start(bf16[64,2048]{1,0:T(8,128)(2,1)S(1)} %get-tuple-element.61), channel_id=1, source_target_pairs={{0,1},{1,2},{2,3},{3,0},{4,5},{5,6},{6,7},{7,4},{8,9},{9,10},{10,1... | collective-permute-start | bytes 786440 | tf_op jit(solution)/shard_map/ppermute | solution.py:282
  2.8 1.7 %collective-permute-start.1 = (bf16[64,2048]{1,0:T(8,128)(2,1)S(1)}, bf16[64,2048]{1,0:T(8,128)(2,1)S(1)}, u32[]{:S(2)}, u32[]{:S(2)}) collective-permute-start(bf16[64,2048]{1,0:T(8,128)(2,1)S(1)} %get-tuple-element.62), channel_id=1, source_target_pairs={{0,3},{1,0},{2,1},{3,2},{4,7},{5,4},{6,5},{7,6},{8,11},{9,8},{10,9... | collective-permute-start | bytes 786440 | tf_op jit(solution)/shard_map/ppermute | solution.py:282
  4.5 2.0 %collective-permute-start = (bf16[64,2048]{1,0:T(8,128)(2,1)S(1)}, bf16[64,2048]{1,0:T(8,128)(2,1)S(1)}, u32[]{:S(2)}, u32[]{:S(2)}) collective-permute-start(bf16[64,2048]{1,0:T(8,128)(2,1)S(1)} %get-tuple-element.63), channel_id=1, source_target_pairs={{0,2},{1,3},{2,0},{3,1},{4,6},{5,7},{6,4},{7,5},{8,10},{9,11},{10,... | collective-permute-start | bytes 786440 | tf_op jit(solution)/shard_map/ppermute | solution.py:282
  6.5 0.0 copy-start.1
  6.5 0.8 %copy-done.1 = bf16[256,128]{1,0:T(8,128)(2,1)S(1)} copy-done((bf16[256,128]{1,0:T(8,128)(2,1)S(1)}, bf16[256,128]{1,0:T(8,128)(2,1)}, u32[]{:S(2)}) %copy-start.1) | copy-done | bytes 65560
  7.3 0.0 copy-start.4
  7.3 1.2 %copy-done.4 = bf16[256,2048]{1,0:T(8,128)(2,1)S(1)} copy-done((bf16[256,2048]{1,0:T(8,128)(2,1)S(1)}, bf16[256,2048]{1,0:T(8,128)(2,1)}, u32[]{:S(2)}) %copy-start.4) | copy-done | bytes 1048600
  8.5 0.0 copy-start.5
  8.5 0.8 %copy-done.5 = bf16[256,128]{1,0:T(8,128)(2,1)S(1)} copy-done((bf16[256,128]{1,0:T(8,128)(2,1)S(1)}, bf16[256,128]{1,0:T(8,128)(2,1)}, u32[]{:S(2)}) %copy-start.5) | copy-done | bytes 65560
  9.4 0.0 copy-start.6
  9.4 0.8 %copy-done.6 = f32[32,256]{1,0:T(8,128)S(1)} copy-done((f32[32,256]{1,0:T(8,128)S(1)}, f32[32,256]{1,0:T(8,128)}, u32[]{:S(2)}) %copy-start.6) | copy-done | bytes 32792
  10.1 0.8 %copy-done.7 = f32[32,256]{1,0:T(8,128)S(1)} copy-done((f32[32,256]{1,0:T(8,128)S(1)}, f32[32,256]{1,0:T(8,128)}, u32[]{:S(2)}) %copy-start.7) | copy-done | bytes 32792
  10.9 0.7 %copy-done.8 = f32[256]{0:T(256)S(1)} copy-done((f32[256]{0:T(256)S(1)}, f32[256]{0:T(256)}, u32[]{:S(2)}) %copy-start.8) | copy-done | bytes 1048
  11.6 0.7 copy-done.9
  12.2 3.4 %shard_map.91 = (bf16[32,256,256]{2,1,0:T(8,128)(2,1)S(1)}, f32[256,2048]{1,0:T(8,128)S(1)}, f32[256,2048]{1,0:T(8,128)S(1)}, f32[256,2048]{1,0:T(8,128)S(1)}, f...) custom-call(f32[32,256]{1,0:T(8,128)S(1)} %copy-done.6, ...), custom_call_target="tpu_custom_call" | custom-call | flops 4294967296 | bytes 12582912 | tf_op jit(solution)/shard_map/pallas_call | solution.py:35
  15.7 0.1 collective-permute-start.3
  15.8 1.2 %collective-permute-done.3.refs_6_.refs_3_.refs_7_ = f32[8,2048]{1,0:T(8,128)S(1)} collective-permute-done((f32[8,2048]{1,0:T(8,128)S(1)}, f32[8,2048]{1,0:T(8,128)S(1)}, u32[]{:S(2)}, u32[]{:S(2)}) %collective-permute-start.3) | collective-permute-done | bytes 65568 | tf_op jit(solution)/shard_map/ppermute | solution.py:282
  17.0 0.0 collective-permute-done.2.refs_3_
  17.0 0.0 collective-permute-done.1.refs_2_
  17.0 0.3 collective-permute-done.refs_1_
  17.4 0.0 copy-done
  17.4 0.6 shard_map.92
  18.0 0.1 collective-permute-start.4
  18.1 1.5 %collective-permute-done.4.refs_1_.refs_5_ = bf16[128,1024]{1,0:T(8,128)(2,1)S(1)} collective-permute-done((bf16[128,1024]{1,0:T(8,128)(2,1)S(1)}, bf16[128,1024]{1,0:T(8,128)(2,1)S(1)}, u32[]{:S(2)}, u32[]{:S(2)}) %collective-permute-start.4) | collective-permute-done | bytes 262176 | tf_op jit(solution)/shard_map/ppermute | solution.py:282
  19.6 0.3 shard_map.93
  19.9 1.6 %collective-permute-start.5 = (bf16[144,256]{1,0:T(8,128)(2,1)S(1)}, bf16[144,256]{1,0:T(8,128)(2,1)S(1)}, u32[]{:S(2)}, u32[]{:S(2)}) collective-permute-start(bf16[144,256]{1,0:T(8,128)(2,1)S(1)} %get-tuple-element.39), channel_id=1, source_target_pairs={{0,8},{8,16},{16,24},{24,0},{1,9},{9,17},{17,25},{25,1},{2,10},{10... | collective-permute-start | bytes 221192 | tf_op jit(solution)/shard_map/ppermute | solution.py:282
  21.5 2.7 %collective-permute-start.6 = (bf16[144,256]{1,0:T(8,128)(2,1)S(1)}, bf16[144,256]{1,0:T(8,128)(2,1)S(1)}, u32[]{:S(2)}, u32[]{:S(2)}) collective-permute-start(bf16[144,256]{1,0:T(8,128)(2,1)S(1)} %get-tuple-element.40), channel_id=1, source_target_pairs={{0,16},{8,24},{16,0},{24,8},{1,17},{9,25},{17,1},{25,9},{2,18},{10... | collective-permute-start | bytes 221192 | tf_op jit(solution)/shard_map/ppermute | solution.py:282
  24.2 1.4 %collective-permute-start.7 = (bf16[144,256]{1,0:T(8,128)(2,1)S(1)}, bf16[144,256]{1,0:T(8,128)(2,1)S(1)}, u32[]{:S(2)}, u32[]{:S(2)}) collective-permute-start(bf16[144,256]{1,0:T(8,128)(2,1)S(1)} %get-tuple-element.41), channel_id=1, source_target_pairs={{0,24},{8,0},{16,8},{24,16},{1,25},{9,1},{17,9},{25,17},{2,26},{10... | collective-permute-start | bytes 221192 | tf_op jit(solution)/shard_map/ppermute | solution.py:282
  25.6 1.2 %shard_map.94.refs_4_.refs_3_ = f32[256,2048]{1,0:T(8,128)S(1)} custom-call(bf16[256,2048]{1,0:T(8,128)(2,1)S(1)} %get-tuple-element.42.refs_0_, f32[256,2048]{1,0:T(8,128)S(1)} %get-tuple-element.43.refs_1_, bf16[32,256,256]{2,1,0:T(8,128)(2,1)S(1)} %get-tuple-element.44.refs_2_, f32[256,2048]{1,0:T(8,128)S(1)} %get-tuple-element.45.refs_3_, ...), custom_call_target="tpu_custom_call" | custom-call | flops 2147483648 | bytes 11534336 | tf_op jit(solution)/shard_map/pallas_call | solution.py:35
  26.8 0.0 copy-start.2
  26.8 0.0 collective-permute-done.5.refs_1_
  26.9 1.2 %collective-permute-done.6.refs_2_ = bf16[144,256]{1,0:T(8,128)(2,1)S(1)} collective-permute-done((bf16[144,256]{1,0:T(8,128)(2,1)S(1)}, bf16[144,256]{1,0:T(8,128)(2,1)S(1)}, u32[]{:S(2)}, u32[]{:S(2)}) %collective-permute-start.6) | collective-permute-done | bytes 73760 | tf_op jit(solution)/shard_map/ppermute | solution.py:282
  28.1 0.5 collective-permute-done.7.refs_3_
  28.6 0.1 shard_map.95
  28.7 0.2 collective-permute-start.10
  28.9 3.3 %collective-permute-start.9 = (bf16[144,256]{1,0:T(8,128)(2,1)S(1)}, bf16[144,256]{1,0:T(8,128)(2,1)S(1)}, u32[]{:S(2)}, u32[]{:S(2)}) collective-permute-start(bf16[144,256]{1,0:T(8,128)(2,1)S(1)} %get-tuple-element.47.refs_0_), channel_id=1, source_target_pairs={{0,64},{32,96},{64,0},{96,32},{128,192},{160,224},{192,128},{224,1... | collective-permute-start | bytes 221192 | tf_op jit(solution)/shard_map/ppermute | solution.py:330
  32.1 2.8 %collective-permute-start.8 = (bf16[144,256]{1,0:T(8,128)(2,1)S(1)}, bf16[144,256]{1,0:T(8,128)(2,1)S(1)}, u32[]{:S(2)}, u32[]{:S(2)}) collective-permute-start(bf16[144,256]{1,0:T(8,128)(2,1)S(1)} %get-tuple-element.47.refs_0_), channel_id=1, source_target_pairs={{0,32},{32,64},{64,96},{96,0},{128,160},{160,192},{192,224},{224,1... | collective-permute-start | bytes 221192 | tf_op jit(solution)/shard_map/ppermute | solution.py:330
  34.9 0.0 collective-permute-done.10.refs_3_
  34.9 1.4 %collective-permute-done.9.refs_2_ = bf16[144,256]{1,0:T(8,128)(2,1)S(1)} collective-permute-done((bf16[144,256]{1,0:T(8,128)(2,1)S(1)}, bf16[144,256]{1,0:T(8,128)(2,1)S(1)}, u32[]{:S(2)}, u32[]{:S(2)}) %collective-permute-start.9) | collective-permute-done | bytes 73760 | tf_op jit(solution)/shard_map/ppermute | solution.py:330
  36.4 1.2 %collective-permute-done.8.refs_1_ = bf16[144,256]{1,0:T(8,128)(2,1)S(1)} collective-permute-done((bf16[144,256]{1,0:T(8,128)(2,1)S(1)}, bf16[144,256]{1,0:T(8,128)(2,1)S(1)}, u32[]{:S(2)}, u32[]{:S(2)}) %collective-permute-start.8) | collective-permute-done | bytes 73760 | tf_op jit(solution)/shard_map/ppermute | solution.py:330
  37.6 0.1 shard_map.96
  37.7 5.9 %collective-permute-start.11 = (bf16[128,256]{1,0:T(8,128)(2,1)S(1)}, bf16[128,256]{1,0:T(8,128)(2,1)S(1)}, u32[]{:S(2)}, u32[]{:S(2)}) collective-permute-start(bf16[128,256]{1,0:T(8,128)(2,1)S(1)} %get-tuple-element.50), channel_id=1, source_target_pairs={{0,224},{32,192},{64,160},{96,128},{128,96},{160,64},{192,32},{224... | collective-permute-start | bytes 196616 | tf_op jit(solution)/shard_map/ppermute | solution.py:336
  43.6 2.2 %collective-permute-done.11.refs_2_ = bf16[128,256]{1,0:T(8,128)(2,1)S(1)} collective-permute-done((bf16[128,256]{1,0:T(8,128)(2,1)S(1)}, bf16[128,256]{1,0:T(8,128)(2,1)S(1)}, u32[]{:S(2)}, u32[]{:S(2)}) %collective-permute-start.11) | collective-permute-done | bytes 65568 | tf_op jit(solution)/shard_map/ppermute | solution.py:336
  45.9 0.1 shard_map.97
  46.0 0.5 collective-permute-start.12
  46.5 3.4 %collective-permute-start.13 = (bf16[128,256]{1,0:T(8,128)(2,1)S(1)}, bf16[128,256]{1,0:T(8,128)(2,1)S(1)}, u32[]{:S(2)}, u32[]{:S(2)}) collective-permute-start(bf16[128,256]{1,0:T(8,128)(2,1)S(1)} %get-tuple-element.54), channel_id=1, source_target_pairs={{0,16},{8,24},{16,0},{24,8},{1,17},{9,25},{17,1},{25,9},{2,18},{10... | collective-permute-start | bytes 196616 | tf_op jit(solution)/shard_map/ppermute | solution.py:282
  49.9 1.2 %collective-permute-start.14 = (bf16[128,256]{1,0:T(8,128)(2,1)S(1)}, bf16[128,256]{1,0:T(8,128)(2,1)S(1)}, u32[]{:S(2)}, u32[]{:S(2)}) collective-permute-start(bf16[128,256]{1,0:T(8,128)(2,1)S(1)} %get-tuple-element.55), channel_id=1, source_target_pairs={{0,24},{8,0},{16,8},{24,16},{1,25},{9,1},{17,9},{25,17},{2,26},{10... | collective-permute-start | bytes 196616 | tf_op jit(solution)/shard_map/ppermute | solution.py:282
  51.1 0.4 collective-permute-done.12.refs_1_
  51.6 1.3 %collective-permute-done.13.refs_2_ = bf16[128,256]{1,0:T(8,128)(2,1)S(1)} collective-permute-done((bf16[128,256]{1,0:T(8,128)(2,1)S(1)}, bf16[128,256]{1,0:T(8,128)(2,1)S(1)}, u32[]{:S(2)}, u32[]{:S(2)}) %collective-permute-start.13) | collective-permute-done | bytes 65568 | tf_op jit(solution)/shard_map/ppermute | solution.py:282
  52.9 1.3 %collective-permute-done.14.refs_3_ = bf16[128,256]{1,0:T(8,128)(2,1)S(1)} collective-permute-done((bf16[128,256]{1,0:T(8,128)(2,1)S(1)}, bf16[128,256]{1,0:T(8,128)(2,1)S(1)}, u32[]{:S(2)}, u32[]{:S(2)}) %collective-permute-start.14) | collective-permute-done | bytes 65568 | tf_op jit(solution)/shard_map/ppermute | solution.py:282
  54.2 0.3 shard_map.98
  54.5 0.1 collective-permute-start.15
  54.6 1.5 %collective-permute-done.15.refs_1_ = bf16[128,1024]{1,0:T(8,128)(2,1)S(1)} collective-permute-done((bf16[128,1024]{1,0:T(8,128)(2,1)S(1)}, bf16[128,1024]{1,0:T(8,128)(2,1)S(1)}, u32[]{:S(2)}, u32[]{:S(2)}) %collective-permute-start.15) | collective-permute-done | bytes 262176 | tf_op jit(solution)/shard_map/ppermute | solution.py:282
  56.1 0.0 copy-done.2
  56.1 0.6 shard_map.99
  56.7 1.9 %collective-permute-start.18 = (f32[8,256]{1,0:T(8,128)S(1)}, f32[8,256]{1,0:T(8,128)S(1)}, u32[]{:S(2)}, u32[]{:S(2)}) collective-permute-start(f32[8,256]{1,0:T(8,128)S(1)} %get-tuple-element.60.refs_1_), channel_id=1, source_target_pairs={{0,3},{1,0},{2,1},{3,2},{4,7},{5,4},{6,5},{7,6},{8,11},{9,8},{10,9... | collective-permute-start | bytes 24584 | tf_op jit(solution)/shard_map/ppermute | solution.py:282
  58.6 1.4 %collective-permute-start.17 = (f32[8,256]{1,0:T(8,128)S(1)}, f32[8,256]{1,0:T(8,128)S(1)}, u32[]{:S(2)}, u32[]{:S(2)}) collective-permute-start(f32[8,256]{1,0:T(8,128)S(1)} %get-tuple-element.60.refs_1_), channel_id=1, source_target_pairs={{0,2},{1,3},{2,0},{3,1},{4,6},{5,7},{6,4},{7,5},{8,10},{9,11},{10,... | collective-permute-start | bytes 24584 | tf_op jit(solution)/shard_map/ppermute | solution.py:282
  60.0 0.0 collective-permute-start.16
  60.0 0.5 collective-permute-done.18.refs_4_
  60.5 3.3 %collective-permute-done.17.refs_3_ = f32[8,256]{1,0:T(8,128)S(1)} collective-permute-done((f32[8,256]{1,0:T(8,128)S(1)}, f32[8,256]{1,0:T(8,128)S(1)}, u32[]{:S(2)}, u32[]{:S(2)}) %collective-permute-start.17) | collective-permute-done | bytes 8224 | tf_op jit(solution)/shard_map/ppermute | solution.py:282
  63.8 1.1 %collective-permute-done.16.refs_2_ = f32[8,256]{1,0:T(8,128)S(1)} collective-permute-done((f32[8,256]{1,0:T(8,128)S(1)}, f32[8,256]{1,0:T(8,128)S(1)}, u32[]{:S(2)}, u32[]{:S(2)}) %collective-permute-start.16) | collective-permute-done | bytes 8224 | tf_op jit(solution)/shard_map/ppermute | solution.py:282
  64.9 0.0 copy-done.3
  64.9 1.2 %shard_map.100 = bf16[256,2048]{1,0:T(8,128)(2,1)} custom-call(f32[256,2048]{1,0:T(8,128)S(1)} %get-tuple-element.59.refs_0_, f32[8,256]{1,0:T(8,128)S(1)} %get-tuple-element.60.refs_1_, f32[8,256]{1,0:T(8,128)S(1)} %collective-permute-done.16.refs_2_, f32[8,256]{1,0:T(8,128)S(1)} %collective-permute-done.17.refs_3_, ...), custom_call_target="tpu_custom_call" | custom-call | tf_op jit(solution)/shard_map/pallas_call | solution.py:35
  (5 shorter events, 0.0 us)
Async XLA Ops:
  1.2 15.9 %collective-permute-start.2 = (bf16[64,2048]{1,0:T(8,128)(2,1)S(1)}, bf16[64,2048]{1,0:T(8,128)(2,1)S(1)}, u32[]{:S(2)}, u32[]{:S(2)}) collective-permute-start(bf16[64,2048]{1,0:T(8,128)(2,1)S(1)} %get-tuple-element.61), channel_id=1, source_target_pairs={{0,1},{1,2},{2,3},{3,0},{4,5},{5,6},{6,7},{7,4},{8,9},{9,10},{10,1... | collective-permute-start | bytes 786440 | tf_op jit(solution)/shard_map/ppermute | solution.py:282
  2.8 14.2 %collective-permute-start.1 = (bf16[64,2048]{1,0:T(8,128)(2,1)S(1)}, bf16[64,2048]{1,0:T(8,128)(2,1)S(1)}, u32[]{:S(2)}, u32[]{:S(2)}) collective-permute-start(bf16[64,2048]{1,0:T(8,128)(2,1)S(1)} %get-tuple-element.62), channel_id=1, source_target_pairs={{0,3},{1,0},{2,1},{3,2},{4,7},{5,4},{6,5},{7,6},{8,11},{9,8},{10,9... | collective-permute-start | bytes 786440 | tf_op jit(solution)/shard_map/ppermute | solution.py:282
  4.5 12.9 %collective-permute-start = (bf16[64,2048]{1,0:T(8,128)(2,1)S(1)}, bf16[64,2048]{1,0:T(8,128)(2,1)S(1)}, u32[]{:S(2)}, u32[]{:S(2)}) collective-permute-start(bf16[64,2048]{1,0:T(8,128)(2,1)S(1)} %get-tuple-element.63), channel_id=1, source_target_pairs={{0,2},{1,3},{2,0},{3,1},{4,6},{5,7},{6,4},{7,5},{8,10},{9,11},{10,... | collective-permute-start | bytes 786440 | tf_op jit(solution)/shard_map/ppermute | solution.py:282
  6.5 0.8 %copy-start.1 = (bf16[256,128]{1,0:T(8,128)(2,1)S(1)}, bf16[256,128]{1,0:T(8,128)(2,1)}, u32[]{:S(2)}) copy-start(bf16[256,128]{1,0:T(8,128)(2,1)} %refs_2_.1) | copy-start | bytes 196612
  7.3 1.2 %copy-start.4 = (bf16[256,2048]{1,0:T(8,128)(2,1)S(1)}, bf16[256,2048]{1,0:T(8,128)(2,1)}, u32[]{:S(2)}) copy-start(bf16[256,2048]{1,0:T(8,128)(2,1)} %refs_6_.1) | copy-start | bytes 3145732
  8.5 0.8 %copy-start.5 = (bf16[256,128]{1,0:T(8,128)(2,1)S(1)}, bf16[256,128]{1,0:T(8,128)(2,1)}, u32[]{:S(2)}) copy-start(bf16[256,128]{1,0:T(8,128)(2,1)} %refs_4_.1) | copy-start | bytes 196612
  9.4 0.8 %copy-start.6 = (f32[32,256]{1,0:T(8,128)S(1)}, f32[32,256]{1,0:T(8,128)}, u32[]{:S(2)}) copy-start(f32[32,256]{1,0:T(8,128)} %refs_0_.2) | copy-start | bytes 98308
  10.1 0.8 %copy-start.7 = (f32[32,256]{1,0:T(8,128)S(1)}, f32[32,256]{1,0:T(8,128)}, u32[]{:S(2)}) copy-start(f32[32,256]{1,0:T(8,128)} %refs_1_.1) | copy-start | bytes 98308
  10.9 0.7 %copy-start.8 = (f32[256]{0:T(256)S(1)}, f32[256]{0:T(256)}, u32[]{:S(2)}) copy-start(f32[256]{0:T(256)} %param.15) | copy-start | bytes 3076
  11.6 0.7 copy-start.9
  12.2 5.1 %copy-start = (bf16[64,8192]{1,0:T(8,128)(2,1)S(1)}, bf16[64,8192]{1,0:T(8,128)(2,1)}, u32[]{:S(2)}) copy-start(bf16[64,8192]{1,0:T(8,128)(2,1)} %refs_0_.3) | copy-start | bytes 3145732
  15.7 1.3 %collective-permute-start.3 = (f32[8,2048]{1,0:T(8,128)S(1)}, f32[8,2048]{1,0:T(8,128)S(1)}, u32[]{:S(2)}, u32[]{:S(2)}) collective-permute-start(f32[8,2048]{1,0:T(8,128)S(1)} %get-tuple-element.35.refs_2_.refs_6_), channel_id=1, source_target_pairs={{0,4},{4,0},{1,5},{5,1},{2,6},{6,2},{3,7},{7,3},{8,12},{12,8},{9,1... | collective-permute-start | bytes 196616 | tf_op jit(solution)/shard_map/ppermute | solution.py:282
  18.0 1.6 %collective-permute-start.4 = (bf16[128,1024]{1,0:T(8,128)(2,1)S(1)}, bf16[128,1024]{1,0:T(8,128)(2,1)S(1)}, u32[]{:S(2)}, u32[]{:S(2)}) collective-permute-start(bf16[128,1024]{1,0:T(8,128)(2,1)S(1)} %get-tuple-element.37), channel_id=1, source_target_pairs={{0,4},{4,0},{1,5},{5,1},{2,6},{6,2},{3,7},{7,3},{8,12},{12,8},{9,1... | collective-permute-start | bytes 786440 | tf_op jit(solution)/shard_map/ppermute | solution.py:282
  19.9 6.9 %collective-permute-start.5 = (bf16[144,256]{1,0:T(8,128)(2,1)S(1)}, bf16[144,256]{1,0:T(8,128)(2,1)S(1)}, u32[]{:S(2)}, u32[]{:S(2)}) collective-permute-start(bf16[144,256]{1,0:T(8,128)(2,1)S(1)} %get-tuple-element.39), channel_id=1, source_target_pairs={{0,8},{8,16},{16,24},{24,0},{1,9},{9,17},{17,25},{25,1},{2,10},{10... | collective-permute-start | bytes 221192 | tf_op jit(solution)/shard_map/ppermute | solution.py:282
  21.5 6.6 %collective-permute-start.6 = (bf16[144,256]{1,0:T(8,128)(2,1)S(1)}, bf16[144,256]{1,0:T(8,128)(2,1)S(1)}, u32[]{:S(2)}, u32[]{:S(2)}) collective-permute-start(bf16[144,256]{1,0:T(8,128)(2,1)S(1)} %get-tuple-element.40), channel_id=1, source_target_pairs={{0,16},{8,24},{16,0},{24,8},{1,17},{9,25},{17,1},{25,9},{2,18},{10... | collective-permute-start | bytes 221192 | tf_op jit(solution)/shard_map/ppermute | solution.py:282
  24.2 4.4 %collective-permute-start.7 = (bf16[144,256]{1,0:T(8,128)(2,1)S(1)}, bf16[144,256]{1,0:T(8,128)(2,1)S(1)}, u32[]{:S(2)}, u32[]{:S(2)}) collective-permute-start(bf16[144,256]{1,0:T(8,128)(2,1)S(1)} %get-tuple-element.41), channel_id=1, source_target_pairs={{0,24},{8,0},{16,8},{24,16},{1,25},{9,1},{17,9},{25,17},{2,26},{10... | collective-permute-start | bytes 221192 | tf_op jit(solution)/shard_map/ppermute | solution.py:282
  26.8 29.3 %copy-start.2 = (bf16[256,128]{1,0:T(8,128)(2,1)S(1)}, bf16[256,128]{1,0:T(8,128)(2,1)}, u32[]{:S(2)}) copy-start(bf16[256,128]{1,0:T(8,128)(2,1)} %refs_2_.1) | copy-start | bytes 196612
  28.7 6.3 %collective-permute-start.10 = (bf16[144,256]{1,0:T(8,128)(2,1)S(1)}, bf16[144,256]{1,0:T(8,128)(2,1)S(1)}, u32[]{:S(2)}, u32[]{:S(2)}) collective-permute-start(bf16[144,256]{1,0:T(8,128)(2,1)S(1)} %get-tuple-element.47.refs_0_), channel_id=1, source_target_pairs={{0,96},{32,0},{64,32},{96,64},{128,224},{160,128},{192,160},{224,1... | collective-permute-start | bytes 221192 | tf_op jit(solution)/shard_map/ppermute | solution.py:330
  28.9 7.5 %collective-permute-start.9 = (bf16[144,256]{1,0:T(8,128)(2,1)S(1)}, bf16[144,256]{1,0:T(8,128)(2,1)S(1)}, u32[]{:S(2)}, u32[]{:S(2)}) collective-permute-start(bf16[144,256]{1,0:T(8,128)(2,1)S(1)} %get-tuple-element.47.refs_0_), channel_id=1, source_target_pairs={{0,64},{32,96},{64,0},{96,32},{128,192},{160,224},{192,128},{224,1... | collective-permute-start | bytes 221192 | tf_op jit(solution)/shard_map/ppermute | solution.py:330
  32.1 5.5 %collective-permute-start.8 = (bf16[144,256]{1,0:T(8,128)(2,1)S(1)}, bf16[144,256]{1,0:T(8,128)(2,1)S(1)}, u32[]{:S(2)}, u32[]{:S(2)}) collective-permute-start(bf16[144,256]{1,0:T(8,128)(2,1)S(1)} %get-tuple-element.47.refs_0_), channel_id=1, source_target_pairs={{0,32},{32,64},{64,96},{96,0},{128,160},{160,192},{192,224},{224,1... | collective-permute-start | bytes 221192 | tf_op jit(solution)/shard_map/ppermute | solution.py:330
  37.7 8.2 %collective-permute-start.11 = (bf16[128,256]{1,0:T(8,128)(2,1)S(1)}, bf16[128,256]{1,0:T(8,128)(2,1)S(1)}, u32[]{:S(2)}, u32[]{:S(2)}) collective-permute-start(bf16[128,256]{1,0:T(8,128)(2,1)S(1)} %get-tuple-element.50), channel_id=1, source_target_pairs={{0,224},{32,192},{64,160},{96,128},{128,96},{160,64},{192,32},{224... | collective-permute-start | bytes 196616 | tf_op jit(solution)/shard_map/ppermute | solution.py:336
  46.0 5.6 %collective-permute-start.12 = (bf16[128,256]{1,0:T(8,128)(2,1)S(1)}, bf16[128,256]{1,0:T(8,128)(2,1)S(1)}, u32[]{:S(2)}, u32[]{:S(2)}) collective-permute-start(bf16[128,256]{1,0:T(8,128)(2,1)S(1)} %get-tuple-element.53), channel_id=1, source_target_pairs={{0,8},{8,16},{16,24},{24,0},{1,9},{9,17},{17,25},{25,1},{2,10},{10... | collective-permute-start | bytes 196616 | tf_op jit(solution)/shard_map/ppermute | solution.py:282
  46.5 6.4 %collective-permute-start.13 = (bf16[128,256]{1,0:T(8,128)(2,1)S(1)}, bf16[128,256]{1,0:T(8,128)(2,1)S(1)}, u32[]{:S(2)}, u32[]{:S(2)}) collective-permute-start(bf16[128,256]{1,0:T(8,128)(2,1)S(1)} %get-tuple-element.54), channel_id=1, source_target_pairs={{0,16},{8,24},{16,0},{24,8},{1,17},{9,25},{17,1},{25,9},{2,18},{10... | collective-permute-start | bytes 196616 | tf_op jit(solution)/shard_map/ppermute | solution.py:282
  49.9 4.3 %collective-permute-start.14 = (bf16[128,256]{1,0:T(8,128)(2,1)S(1)}, bf16[128,256]{1,0:T(8,128)(2,1)S(1)}, u32[]{:S(2)}, u32[]{:S(2)}) collective-permute-start(bf16[128,256]{1,0:T(8,128)(2,1)S(1)} %get-tuple-element.55), channel_id=1, source_target_pairs={{0,24},{8,0},{16,8},{24,16},{1,25},{9,1},{17,9},{25,17},{2,26},{10... | collective-permute-start | bytes 196616 | tf_op jit(solution)/shard_map/ppermute | solution.py:282
  54.5 1.6 %collective-permute-start.15 = (bf16[128,1024]{1,0:T(8,128)(2,1)S(1)}, bf16[128,1024]{1,0:T(8,128)(2,1)S(1)}, u32[]{:S(2)}, u32[]{:S(2)}) collective-permute-start(bf16[128,1024]{1,0:T(8,128)(2,1)S(1)} %get-tuple-element.57), channel_id=1, source_target_pairs={{0,4},{4,0},{1,5},{5,1},{2,6},{6,2},{3,7},{7,3},{8,12},{12,8},{9,1... | collective-permute-start | bytes 786440 | tf_op jit(solution)/shard_map/ppermute | solution.py:282
  56.1 8.7 %copy-start.3 = (f32[2048]{0:T(1024)S(1)}, f32[2048]{0:T(1024)}, u32[]{:S(2)}) copy-start(f32[2048]{0:T(1024)} %param.17) | copy-start | bytes 24580
  56.7 3.8 %collective-permute-start.18 = (f32[8,256]{1,0:T(8,128)S(1)}, f32[8,256]{1,0:T(8,128)S(1)}, u32[]{:S(2)}, u32[]{:S(2)}) collective-permute-start(f32[8,256]{1,0:T(8,128)S(1)} %get-tuple-element.60.refs_1_), channel_id=1, source_target_pairs={{0,3},{1,0},{2,1},{3,2},{4,7},{5,4},{6,5},{7,6},{8,11},{9,8},{10,9... | collective-permute-start | bytes 24584 | tf_op jit(solution)/shard_map/ppermute | solution.py:282
  58.6 5.2 %collective-permute-start.17 = (f32[8,256]{1,0:T(8,128)S(1)}, f32[8,256]{1,0:T(8,128)S(1)}, u32[]{:S(2)}, u32[]{:S(2)}) collective-permute-start(f32[8,256]{1,0:T(8,128)S(1)} %get-tuple-element.60.refs_1_), channel_id=1, source_target_pairs={{0,2},{1,3},{2,0},{3,1},{4,6},{5,7},{6,4},{7,5},{8,10},{9,11},{10,... | collective-permute-start | bytes 24584 | tf_op jit(solution)/shard_map/ppermute | solution.py:282
  60.0 4.9 %collective-permute-start.16 = (f32[8,256]{1,0:T(8,128)S(1)}, f32[8,256]{1,0:T(8,128)S(1)}, u32[]{:S(2)}, u32[]{:S(2)}) collective-permute-start(f32[8,256]{1,0:T(8,128)S(1)} %get-tuple-element.60.refs_1_), channel_id=1, source_target_pairs={{0,1},{1,2},{2,3},{3,0},{4,5},{5,6},{6,7},{7,4},{8,9},{9,10},{10,1... | collective-permute-start | bytes 24584 | tf_op jit(solution)/shard_map/ppermute | solution.py:282

commit v6 on v5

--- a/solution.py
+++ b/solution.py
@@ -19,7 +19,7 @@
 FEATS = HERE * HEAD_DIM
 HALF = FEATS // 2
 PART = HALF // 4
-ROUND_Y = (0, 2, 3, 1)
+ROUND_Y = (0, 3, 2, 1)
 ROUND_X = (0, 1, 2, 3)
 LOGS = 16
 

time: 66.7 us -> 66.9 us (level)
  starting transfers between devices: 31.9 us -> 33.1 us
  waiting for transfers between devices: 19.1 us -> 18 us
    ppermute x15, waiting for transfers between devices: 14.2 us -> 13 us  [shifted(): return lax.ppermute(v, axis, [(i, (i + step) % size) for i in range(size)])]
    ppermute x15, starting transfers between devices: 19.7 us -> 20.9 us  [shifted(): return lax.ppermute(v, axis, [(i, (i + step) % size) for i in range(size)])]
  transfers between devices with their start and end apart: 19 -> 19, of which waited for: 15 -> 13; matrix products, arithmetic and copies ran while one was open for 0% -> 0% of each run, Pallas kernels for 7% -> 7%
where the time goes in v6:
time: 66.9 us; the launch traced here: 66.3 us
  starting transfers between devices  33.1 us (49%)
  waiting for transfers between devices  18 us (27%)
  Pallas kernels  7.94 us (12%)
  local copies, waits for them, and re-layouts  6.92 us (10%)
    ppermute x15, starting transfers between devices, shifted(): return lax.ppermute(v, axis, [(i, (i + step) % size) for i in range(size)])  20.9 us
    ppermute x15, waiting for transfers between devices, shifted(): return lax.ppermute(v, axis, [(i, (i + step) % size) for i in range(size)])  13 us
    pallas_call x10, Pallas kernels, kernel_call(): pl.pallas_call(ordered, out_shape=[jax.ShapeDtypeStruct(s, d) for s, d in...  7.94 us
    ppermute x3, starting transfers between devices, on_device(): lax.ppermute(row, 'z', [(i, i // 4 * 4 + (i + k) % 4) for i in range(8)])  6.27 us
    ppermute x1, starting transfers between devices, on_device(): far = lax.ppermute(total, 'z', [(i, 7 - i) for i in range(8)])  5.95 us
    unnamed x20, local copies, waits for them, and re-layouts  5.76 us
    ppermute x3, waiting for transfers between devices, on_device(): lax.ppermute(row, 'z', [(i, i // 4 * 4 + (i + k) % 4) for i in range(8)])  2.76 us
    ppermute x1, waiting for transfers between devices, on_device(): far = lax.ppermute(total, 'z', [(i, 7 - i) for i in range(8)])  2.25 us
  transfers between devices with their start and end apart: 19, of which 13 were waited for; matrix products, arithmetic and copies ran while one was open for 0% of the time, Pallas kernels for 7%

profile of v6, /device:TPU:32, one launch (start us, length us, event | category | flops | bytes accessed | tf_op | source)
XLA Modules:
  0.0 66.3 jit_solution(658488420347593547)
XLA Ops:
  0.0 1.2 %constant_dynamic-slice_fusion = (bf16[64,2048]{1,0:T(8,128)(2,1)S(1)}, bf16[64,2048]{1,0:T(8,128)(2,1)S(1)}, bf16[64,2048]{1,0:T(8,128)(2,1)S(1)}) fusion(bf16[64,8192]{1,0:T(8,128)(2,1)} %refs_0_.3, s32[]{:T(128)S(6)} %select_n.11, s32[]{:T(128)S(6)} %select_n.10, s32[]{:T(128)S(6)} %select_n.9), kind=kLoop, calls=%fused_computation | loop fusion | bytes 1572876 | tf_op jit(solution)/shard_map/dynamic_slice | solution.py:292
  1.2 1.7 %collective-permute-start.2 = (bf16[64,2048]{1,0:T(8,128)(2,1)S(1)}, bf16[64,2048]{1,0:T(8,128)(2,1)S(1)}, u32[]{:S(2)}, u32[]{:S(2)}) collective-permute-start(bf16[64,2048]{1,0:T(8,128)(2,1)S(1)} %get-tuple-element.61), channel_id=1, source_target_pairs={{0,1},{1,2},{2,3},{3,0},{4,5},{5,6},{6,7},{7,4},{8,9},{9,10},{10,1... | collective-permute-start | bytes 786440 | tf_op jit(solution)/shard_map/ppermute | solution.py:282
  2.8 2.9 %collective-permute-start.1 = (bf16[64,2048]{1,0:T(8,128)(2,1)S(1)}, bf16[64,2048]{1,0:T(8,128)(2,1)S(1)}, u32[]{:S(2)}, u32[]{:S(2)}) collective-permute-start(bf16[64,2048]{1,0:T(8,128)(2,1)S(1)} %get-tuple-element.62), channel_id=1, source_target_pairs={{0,2},{1,3},{2,0},{3,1},{4,6},{5,7},{6,4},{7,5},{8,10},{9,11},{10,... | collective-permute-start | bytes 786440 | tf_op jit(solution)/shard_map/ppermute | solution.py:282
  5.7 1.3 %collective-permute-start = (bf16[64,2048]{1,0:T(8,128)(2,1)S(1)}, bf16[64,2048]{1,0:T(8,128)(2,1)S(1)}, u32[]{:S(2)}, u32[]{:S(2)}) collective-permute-start(bf16[64,2048]{1,0:T(8,128)(2,1)S(1)} %get-tuple-element.63), channel_id=1, source_target_pairs={{0,3},{1,0},{2,1},{3,2},{4,7},{5,4},{6,5},{7,6},{8,11},{9,8},{10,9... | collective-permute-start | bytes 786440 | tf_op jit(solution)/shard_map/ppermute | solution.py:282
  7.1 0.0 copy-start.1
  7.1 0.8 %copy-done.1 = bf16[256,128]{1,0:T(8,128)(2,1)S(1)} copy-done((bf16[256,128]{1,0:T(8,128)(2,1)S(1)}, bf16[256,128]{1,0:T(8,128)(2,1)}, u32[]{:S(2)}) %copy-start.1) | copy-done | bytes 65560
  7.9 0.0 copy-start.4
  7.9 1.2 %copy-done.4 = bf16[256,2048]{1,0:T(8,128)(2,1)S(1)} copy-done((bf16[256,2048]{1,0:T(8,128)(2,1)S(1)}, bf16[256,2048]{1,0:T(8,128)(2,1)}, u32[]{:S(2)}) %copy-start.4) | copy-done | bytes 1048600
  9.1 0.0 copy-start.5
  9.1 0.8 %copy-done.5 = bf16[256,128]{1,0:T(8,128)(2,1)S(1)} copy-done((bf16[256,128]{1,0:T(8,128)(2,1)S(1)}, bf16[256,128]{1,0:T(8,128)(2,1)}, u32[]{:S(2)}) %copy-start.5) | copy-done | bytes 65560
  10.0 0.0 copy-start.6
  10.0 0.8 %copy-done.6 = f32[32,256]{1,0:T(8,128)S(1)} copy-done((f32[32,256]{1,0:T(8,128)S(1)}, f32[32,256]{1,0:T(8,128)}, u32[]{:S(2)}) %copy-start.6) | copy-done | bytes 32792
  10.7 0.8 %copy-done.7 = f32[32,256]{1,0:T(8,128)S(1)} copy-done((f32[32,256]{1,0:T(8,128)S(1)}, f32[32,256]{1,0:T(8,128)}, u32[]{:S(2)}) %copy-start.7) | copy-done | bytes 32792
  11.5 0.7 %copy-done.8 = f32[256]{0:T(256)S(1)} copy-done((f32[256]{0:T(256)S(1)}, f32[256]{0:T(256)}, u32[]{:S(2)}) %copy-start.8) | copy-done | bytes 1048
  12.2 0.7 copy-done.9
  12.8 3.5 %shard_map.91 = (bf16[32,256,256]{2,1,0:T(8,128)(2,1)S(1)}, f32[256,2048]{1,0:T(8,128)S(1)}, f32[256,2048]{1,0:T(8,128)S(1)}, f32[256,2048]{1,0:T(8,128)S(1)}, f...) custom-call(f32[32,256]{1,0:T(8,128)S(1)} %copy-done.6, ...), custom_call_target="tpu_custom_call" | custom-call | flops 4294967296 | bytes 12582912 | tf_op jit(solution)/shard_map/pallas_call | solution.py:35
  16.3 0.1 collective-permute-start.3
  16.4 1.2 %collective-permute-done.3.refs_6_.refs_3_.refs_7_ = f32[8,2048]{1,0:T(8,128)S(1)} collective-permute-done((f32[8,2048]{1,0:T(8,128)S(1)}, f32[8,2048]{1,0:T(8,128)S(1)}, u32[]{:S(2)}, u32[]{:S(2)}) %collective-permute-start.3) | collective-permute-done | bytes 65568 | tf_op jit(solution)/shard_map/ppermute | solution.py:282
  17.6 0.0 collective-permute-done.2.refs_3_
  17.6 0.0 collective-permute-done.1.refs_2_
  17.6 0.0 collective-permute-done.refs_1_
  17.6 0.0 copy-done
  17.7 0.6 shard_map.92
  18.3 0.3 collective-permute-start.4
  18.5 1.4 %collective-permute-done.4.refs_1_.refs_5_ = bf16[128,1024]{1,0:T(8,128)(2,1)S(1)} collective-permute-done((bf16[128,1024]{1,0:T(8,128)(2,1)S(1)}, bf16[128,1024]{1,0:T(8,128)(2,1)S(1)}, u32[]{:S(2)}, u32[]{:S(2)}) %collective-permute-start.4) | collective-permute-done | bytes 262176 | tf_op jit(solution)/shard_map/ppermute | solution.py:282
  19.9 0.3 shard_map.93
  20.2 1.6 %collective-permute-start.5 = (bf16[144,256]{1,0:T(8,128)(2,1)S(1)}, bf16[144,256]{1,0:T(8,128)(2,1)S(1)}, u32[]{:S(2)}, u32[]{:S(2)}) collective-permute-start(bf16[144,256]{1,0:T(8,128)(2,1)S(1)} %get-tuple-element.39), channel_id=1, source_target_pairs={{0,8},{8,16},{16,24},{24,0},{1,9},{9,17},{17,25},{25,1},{2,10},{10... | collective-permute-start | bytes 221192 | tf_op jit(solution)/shard_map/ppermute | solution.py:282
  21.8 2.7 %collective-permute-start.6 = (bf16[144,256]{1,0:T(8,128)(2,1)S(1)}, bf16[144,256]{1,0:T(8,128)(2,1)S(1)}, u32[]{:S(2)}, u32[]{:S(2)}) collective-permute-start(bf16[144,256]{1,0:T(8,128)(2,1)S(1)} %get-tuple-element.40), channel_id=1, source_target_pairs={{0,16},{8,24},{16,0},{24,8},{1,17},{9,25},{17,1},{25,9},{2,18},{10... | collective-permute-start | bytes 221192 | tf_op jit(solution)/shard_map/ppermute | solution.py:282
  24.5 1.4 %collective-permute-start.7 = (bf16[144,256]{1,0:T(8,128)(2,1)S(1)}, bf16[144,256]{1,0:T(8,128)(2,1)S(1)}, u32[]{:S(2)}, u32[]{:S(2)}) collective-permute-start(bf16[144,256]{1,0:T(8,128)(2,1)S(1)} %get-tuple-element.41), channel_id=1, source_target_pairs={{0,24},{8,0},{16,8},{24,16},{1,25},{9,1},{17,9},{25,17},{2,26},{10... | collective-permute-start | bytes 221192 | tf_op jit(solution)/shard_map/ppermute | solution.py:282
  25.9 1.2 %shard_map.94.refs_4_.refs_3_ = f32[256,2048]{1,0:T(8,128)S(1)} custom-call(bf16[256,2048]{1,0:T(8,128)(2,1)S(1)} %get-tuple-element.42.refs_0_, f32[256,2048]{1,0:T(8,128)S(1)} %get-tuple-element.43.refs_1_, bf16[32,256,256]{2,1,0:T(8,128)(2,1)S(1)} %get-tuple-element.44.refs_2_, f32[256,2048]{1,0:T(8,128)S(1)} %get-tuple-element.45.refs_3_, ...), custom_call_target="tpu_custom_call" | custom-call | flops 2147483648 | bytes 11534336 | tf_op jit(solution)/shard_map/pallas_call | solution.py:35
  27.1 0.0 copy-start.2
  27.1 0.0 collective-permute-done.5.refs_1_
  27.1 1.2 %collective-permute-done.6.refs_2_ = bf16[144,256]{1,0:T(8,128)(2,1)S(1)} collective-permute-done((bf16[144,256]{1,0:T(8,128)(2,1)S(1)}, bf16[144,256]{1,0:T(8,128)(2,1)S(1)}, u32[]{:S(2)}, u32[]{:S(2)}) %collective-permute-start.6) | collective-permute-done | bytes 73760 | tf_op jit(solution)/shard_map/ppermute | solution.py:282
  28.4 0.5 collective-permute-done.7.refs_3_
  28.9 0.1 shard_map.95
  29.0 0.2 collective-permute-start.10
  29.1 3.3 %collective-permute-start.9 = (bf16[144,256]{1,0:T(8,128)(2,1)S(1)}, bf16[144,256]{1,0:T(8,128)(2,1)S(1)}, u32[]{:S(2)}, u32[]{:S(2)}) collective-permute-start(bf16[144,256]{1,0:T(8,128)(2,1)S(1)} %get-tuple-element.47.refs_0_), channel_id=1, source_target_pairs={{0,64},{32,96},{64,0},{96,32},{128,192},{160,224},{192,128},{224,1... | collective-permute-start | bytes 221192 | tf_op jit(solution)/shard_map/ppermute | solution.py:330
  32.4 2.8 %collective-permute-start.8 = (bf16[144,256]{1,0:T(8,128)(2,1)S(1)}, bf16[144,256]{1,0:T(8,128)(2,1)S(1)}, u32[]{:S(2)}, u32[]{:S(2)}) collective-permute-start(bf16[144,256]{1,0:T(8,128)(2,1)S(1)} %get-tuple-element.47.refs_0_), channel_id=1, source_target_pairs={{0,32},{32,64},{64,96},{96,0},{128,160},{160,192},{192,224},{224,1... | collective-permute-start | bytes 221192 | tf_op jit(solution)/shard_map/ppermute | solution.py:330
  35.2 0.0 collective-permute-done.10.refs_3_
  35.2 1.5 %collective-permute-done.9.refs_2_ = bf16[144,256]{1,0:T(8,128)(2,1)S(1)} collective-permute-done((bf16[144,256]{1,0:T(8,128)(2,1)S(1)}, bf16[144,256]{1,0:T(8,128)(2,1)S(1)}, u32[]{:S(2)}, u32[]{:S(2)}) %collective-permute-start.9) | collective-permute-done | bytes 73760 | tf_op jit(solution)/shard_map/ppermute | solution.py:330
  36.8 1.2 %collective-permute-done.8.refs_1_ = bf16[144,256]{1,0:T(8,128)(2,1)S(1)} collective-permute-done((bf16[144,256]{1,0:T(8,128)(2,1)S(1)}, bf16[144,256]{1,0:T(8,128)(2,1)S(1)}, u32[]{:S(2)}, u32[]{:S(2)}) %collective-permute-start.8) | collective-permute-done | bytes 73760 | tf_op jit(solution)/shard_map/ppermute | solution.py:330
  38.0 0.1 shard_map.96
  38.1 5.9 %collective-permute-start.11 = (bf16[128,256]{1,0:T(8,128)(2,1)S(1)}, bf16[128,256]{1,0:T(8,128)(2,1)S(1)}, u32[]{:S(2)}, u32[]{:S(2)}) collective-permute-start(bf16[128,256]{1,0:T(8,128)(2,1)S(1)} %get-tuple-element.50), channel_id=1, source_target_pairs={{0,224},{32,192},{64,160},{96,128},{128,96},{160,64},{192,32},{224... | collective-permute-start | bytes 196616 | tf_op jit(solution)/shard_map/ppermute | solution.py:336
  44.1 2.2 %collective-permute-done.11.refs_2_ = bf16[128,256]{1,0:T(8,128)(2,1)S(1)} collective-permute-done((bf16[128,256]{1,0:T(8,128)(2,1)S(1)}, bf16[128,256]{1,0:T(8,128)(2,1)S(1)}, u32[]{:S(2)}, u32[]{:S(2)}) %collective-permute-start.11) | collective-permute-done | bytes 65568 | tf_op jit(solution)/shard_map/ppermute | solution.py:336
  46.3 0.1 shard_map.97
  46.4 0.4 collective-permute-start.12
  46.8 3.4 %collective-permute-start.13 = (bf16[128,256]{1,0:T(8,128)(2,1)S(1)}, bf16[128,256]{1,0:T(8,128)(2,1)S(1)}, u32[]{:S(2)}, u32[]{:S(2)}) collective-permute-start(bf16[128,256]{1,0:T(8,128)(2,1)S(1)} %get-tuple-element.54), channel_id=1, source_target_pairs={{0,16},{8,24},{16,0},{24,8},{1,17},{9,25},{17,1},{25,9},{2,18},{10... | collective-permute-start | bytes 196616 | tf_op jit(solution)/shard_map/ppermute | solution.py:282
  50.2 1.3 %collective-permute-start.14 = (bf16[128,256]{1,0:T(8,128)(2,1)S(1)}, bf16[128,256]{1,0:T(8,128)(2,1)S(1)}, u32[]{:S(2)}, u32[]{:S(2)}) collective-permute-start(bf16[128,256]{1,0:T(8,128)(2,1)S(1)} %get-tuple-element.55), channel_id=1, source_target_pairs={{0,24},{8,0},{16,8},{24,16},{1,25},{9,1},{17,9},{25,17},{2,26},{10... | collective-permute-start | bytes 196616 | tf_op jit(solution)/shard_map/ppermute | solution.py:282
  51.5 0.5 collective-permute-done.12.refs_1_
  52.0 1.2 %collective-permute-done.13.refs_2_ = bf16[128,256]{1,0:T(8,128)(2,1)S(1)} collective-permute-done((bf16[128,256]{1,0:T(8,128)(2,1)S(1)}, bf16[128,256]{1,0:T(8,128)(2,1)S(1)}, u32[]{:S(2)}, u32[]{:S(2)}) %collective-permute-start.13) | collective-permute-done | bytes 65568 | tf_op jit(solution)/shard_map/ppermute | solution.py:282
  53.2 1.3 %collective-permute-done.14.refs_3_ = bf16[128,256]{1,0:T(8,128)(2,1)S(1)} collective-permute-done((bf16[128,256]{1,0:T(8,128)(2,1)S(1)}, bf16[128,256]{1,0:T(8,128)(2,1)S(1)}, u32[]{:S(2)}, u32[]{:S(2)}) %collective-permute-start.14) | collective-permute-done | bytes 65568 | tf_op jit(solution)/shard_map/ppermute | solution.py:282
  54.5 0.3 shard_map.98
  54.8 0.1 collective-permute-start.15
  54.9 1.5 %collective-permute-done.15.refs_1_ = bf16[128,1024]{1,0:T(8,128)(2,1)S(1)} collective-permute-done((bf16[128,1024]{1,0:T(8,128)(2,1)S(1)}, bf16[128,1024]{1,0:T(8,128)(2,1)S(1)}, u32[]{:S(2)}, u32[]{:S(2)}) %collective-permute-start.15) | collective-permute-done | bytes 262176 | tf_op jit(solution)/shard_map/ppermute | solution.py:282
  56.4 0.0 copy-done.2
  56.4 0.6 shard_map.99
  57.0 2.0 %collective-permute-start.18 = (f32[8,256]{1,0:T(8,128)S(1)}, f32[8,256]{1,0:T(8,128)S(1)}, u32[]{:S(2)}, u32[]{:S(2)}) collective-permute-start(f32[8,256]{1,0:T(8,128)S(1)} %get-tuple-element.60.refs_1_), channel_id=1, source_target_pairs={{0,3},{1,0},{2,1},{3,2},{4,7},{5,4},{6,5},{7,6},{8,11},{9,8},{10,9... | collective-permute-start | bytes 24584 | tf_op jit(solution)/shard_map/ppermute | solution.py:282
  59.0 1.1 %collective-permute-start.17 = (f32[8,256]{1,0:T(8,128)S(1)}, f32[8,256]{1,0:T(8,128)S(1)}, u32[]{:S(2)}, u32[]{:S(2)}) collective-permute-start(f32[8,256]{1,0:T(8,128)S(1)} %get-tuple-element.60.refs_1_), channel_id=1, source_target_pairs={{0,2},{1,3},{2,0},{3,1},{4,6},{5,7},{6,4},{7,5},{8,10},{9,11},{10,... | collective-permute-start | bytes 24584 | tf_op jit(solution)/shard_map/ppermute | solution.py:282
  60.1 0.7 %collective-permute-start.16 = (f32[8,256]{1,0:T(8,128)S(1)}, f32[8,256]{1,0:T(8,128)S(1)}, u32[]{:S(2)}, u32[]{:S(2)}) collective-permute-start(f32[8,256]{1,0:T(8,128)S(1)} %get-tuple-element.60.refs_1_), channel_id=1, source_target_pairs={{0,1},{1,2},{2,3},{3,0},{4,5},{5,6},{6,7},{7,4},{8,9},{9,10},{10,1... | collective-permute-start | bytes 24584 | tf_op jit(solution)/shard_map/ppermute | solution.py:282
  60.8 0.0 collective-permute-done.18.refs_4_
  60.8 3.3 %collective-permute-done.17.refs_3_ = f32[8,256]{1,0:T(8,128)S(1)} collective-permute-done((f32[8,256]{1,0:T(8,128)S(1)}, f32[8,256]{1,0:T(8,128)S(1)}, u32[]{:S(2)}, u32[]{:S(2)}) %collective-permute-start.17) | collective-permute-done | bytes 8224 | tf_op jit(solution)/shard_map/ppermute | solution.py:282
  64.1 0.9 %collective-permute-done.16.refs_2_ = f32[8,256]{1,0:T(8,128)S(1)} collective-permute-done((f32[8,256]{1,0:T(8,128)S(1)}, f32[8,256]{1,0:T(8,128)S(1)}, u32[]{:S(2)}, u32[]{:S(2)}) %collective-permute-start.16) | collective-permute-done | bytes 8224 | tf_op jit(solution)/shard_map/ppermute | solution.py:282
  65.0 0.0 copy-done.3
  65.0 1.2 %shard_map.100 = bf16[256,2048]{1,0:T(8,128)(2,1)} custom-call(f32[256,2048]{1,0:T(8,128)S(1)} %get-tuple-element.59.refs_0_, f32[8,256]{1,0:T(8,128)S(1)} %get-tuple-element.60.refs_1_, f32[8,256]{1,0:T(8,128)S(1)} %collective-permute-done.16.refs_2_, f32[8,256]{1,0:T(8,128)S(1)} %collective-permute-done.17.refs_3_, ...), custom_call_target="tpu_custom_call" | custom-call | tf_op jit(solution)/shard_map/pallas_call | solution.py:35
  (5 shorter events, 0.0 us)
Async XLA Ops:
  1.2 16.5 %collective-permute-start.2 = (bf16[64,2048]{1,0:T(8,128)(2,1)S(1)}, bf16[64,2048]{1,0:T(8,128)(2,1)S(1)}, u32[]{:S(2)}, u32[]{:S(2)}) collective-permute-start(bf16[64,2048]{1,0:T(8,128)(2,1)S(1)} %get-tuple-element.61), channel_id=1, source_target_pairs={{0,1},{1,2},{2,3},{3,0},{4,5},{5,6},{6,7},{7,4},{8,9},{9,10},{10,1... | collective-permute-start | bytes 786440 | tf_op jit(solution)/shard_map/ppermute | solution.py:282
  2.8 14.8 %collective-permute-start.1 = (bf16[64,2048]{1,0:T(8,128)(2,1)S(1)}, bf16[64,2048]{1,0:T(8,128)(2,1)S(1)}, u32[]{:S(2)}, u32[]{:S(2)}) collective-permute-start(bf16[64,2048]{1,0:T(8,128)(2,1)S(1)} %get-tuple-element.62), channel_id=1, source_target_pairs={{0,2},{1,3},{2,0},{3,1},{4,6},{5,7},{6,4},{7,5},{8,10},{9,11},{10,... | collective-permute-start | bytes 786440 | tf_op jit(solution)/shard_map/ppermute | solution.py:282
  5.7 11.9 %collective-permute-start = (bf16[64,2048]{1,0:T(8,128)(2,1)S(1)}, bf16[64,2048]{1,0:T(8,128)(2,1)S(1)}, u32[]{:S(2)}, u32[]{:S(2)}) collective-permute-start(bf16[64,2048]{1,0:T(8,128)(2,1)S(1)} %get-tuple-element.63), channel_id=1, source_target_pairs={{0,3},{1,0},{2,1},{3,2},{4,7},{5,4},{6,5},{7,6},{8,11},{9,8},{10,9... | collective-permute-start | bytes 786440 | tf_op jit(solution)/shard_map/ppermute | solution.py:282
  7.1 0.8 %copy-start.1 = (bf16[256,128]{1,0:T(8,128)(2,1)S(1)}, bf16[256,128]{1,0:T(8,128)(2,1)}, u32[]{:S(2)}) copy-start(bf16[256,128]{1,0:T(8,128)(2,1)} %refs_2_.1) | copy-start | bytes 196612
  7.9 1.2 %copy-start.4 = (bf16[256,2048]{1,0:T(8,128)(2,1)S(1)}, bf16[256,2048]{1,0:T(8,128)(2,1)}, u32[]{:S(2)}) copy-start(bf16[256,2048]{1,0:T(8,128)(2,1)} %refs_6_.1) | copy-start | bytes 3145732
  9.1 0.8 %copy-start.5 = (bf16[256,128]{1,0:T(8,128)(2,1)S(1)}, bf16[256,128]{1,0:T(8,128)(2,1)}, u32[]{:S(2)}) copy-start(bf16[256,128]{1,0:T(8,128)(2,1)} %refs_4_.1) | copy-start | bytes 196612
  10.0 0.8 %copy-start.6 = (f32[32,256]{1,0:T(8,128)S(1)}, f32[32,256]{1,0:T(8,128)}, u32[]{:S(2)}) copy-start(f32[32,256]{1,0:T(8,128)} %refs_0_.2) | copy-start | bytes 98308
  10.7 0.8 %copy-start.7 = (f32[32,256]{1,0:T(8,128)S(1)}, f32[32,256]{1,0:T(8,128)}, u32[]{:S(2)}) copy-start(f32[32,256]{1,0:T(8,128)} %refs_1_.1) | copy-start | bytes 98308
  11.5 0.7 %copy-start.8 = (f32[256]{0:T(256)S(1)}, f32[256]{0:T(256)}, u32[]{:S(2)}) copy-start(f32[256]{0:T(256)} %param.15) | copy-start | bytes 3076
  12.2 0.7 copy-start.9
  12.8 4.8 %copy-start = (bf16[64,8192]{1,0:T(8,128)(2,1)S(1)}, bf16[64,8192]{1,0:T(8,128)(2,1)}, u32[]{:S(2)}) copy-start(bf16[64,8192]{1,0:T(8,128)(2,1)} %refs_0_.3) | copy-start | bytes 3145732
  16.3 1.3 %collective-permute-start.3 = (f32[8,2048]{1,0:T(8,128)S(1)}, f32[8,2048]{1,0:T(8,128)S(1)}, u32[]{:S(2)}, u32[]{:S(2)}) collective-permute-start(f32[8,2048]{1,0:T(8,128)S(1)} %get-tuple-element.35.refs_2_.refs_6_), channel_id=1, source_target_pairs={{0,4},{4,0},{1,5},{5,1},{2,6},{6,2},{3,7},{7,3},{8,12},{12,8},{9,1... | collective-permute-start | bytes 196616 | tf_op jit(solution)/shard_map/ppermute | solution.py:282
  18.3 1.6 %collective-permute-start.4 = (bf16[128,1024]{1,0:T(8,128)(2,1)S(1)}, bf16[128,1024]{1,0:T(8,128)(2,1)S(1)}, u32[]{:S(2)}, u32[]{:S(2)}) collective-permute-start(bf16[128,1024]{1,0:T(8,128)(2,1)S(1)} %get-tuple-element.37), channel_id=1, source_target_pairs={{0,4},{4,0},{1,5},{5,1},{2,6},{6,2},{3,7},{7,3},{8,12},{12,8},{9,1... | collective-permute-start | bytes 786440 | tf_op jit(solution)/shard_map/ppermute | solution.py:282
  20.2 6.9 %collective-permute-start.5 = (bf16[144,256]{1,0:T(8,128)(2,1)S(1)}, bf16[144,256]{1,0:T(8,128)(2,1)S(1)}, u32[]{:S(2)}, u32[]{:S(2)}) collective-permute-start(bf16[144,256]{1,0:T(8,128)(2,1)S(1)} %get-tuple-element.39), channel_id=1, source_target_pairs={{0,8},{8,16},{16,24},{24,0},{1,9},{9,17},{17,25},{25,1},{2,10},{10... | collective-permute-start | bytes 221192 | tf_op jit(solution)/shard_map/ppermute | solution.py:282
  21.8 6.6 %collective-permute-start.6 = (bf16[144,256]{1,0:T(8,128)(2,1)S(1)}, bf16[144,256]{1,0:T(8,128)(2,1)S(1)}, u32[]{:S(2)}, u32[]{:S(2)}) collective-permute-start(bf16[144,256]{1,0:T(8,128)(2,1)S(1)} %get-tuple-element.40), channel_id=1, source_target_pairs={{0,16},{8,24},{16,0},{24,8},{1,17},{9,25},{17,1},{25,9},{2,18},{10... | collective-permute-start | bytes 221192 | tf_op jit(solution)/shard_map/ppermute | solution.py:282
  24.5 4.4 %collective-permute-start.7 = (bf16[144,256]{1,0:T(8,128)(2,1)S(1)}, bf16[144,256]{1,0:T(8,128)(2,1)S(1)}, u32[]{:S(2)}, u32[]{:S(2)}) collective-permute-start(bf16[144,256]{1,0:T(8,128)(2,1)S(1)} %get-tuple-element.41), channel_id=1, source_target_pairs={{0,24},{8,0},{16,8},{24,16},{1,25},{9,1},{17,9},{25,17},{2,26},{10... | collective-permute-start | bytes 221192 | tf_op jit(solution)/shard_map/ppermute | solution.py:282
  27.1 29.3 %copy-start.2 = (bf16[256,128]{1,0:T(8,128)(2,1)S(1)}, bf16[256,128]{1,0:T(8,128)(2,1)}, u32[]{:S(2)}) copy-start(bf16[256,128]{1,0:T(8,128)(2,1)} %refs_2_.1) | copy-start | bytes 196612
  29.0 6.3 %collective-permute-start.10 = (bf16[144,256]{1,0:T(8,128)(2,1)S(1)}, bf16[144,256]{1,0:T(8,128)(2,1)S(1)}, u32[]{:S(2)}, u32[]{:S(2)}) collective-permute-start(bf16[144,256]{1,0:T(8,128)(2,1)S(1)} %get-tuple-element.47.refs_0_), channel_id=1, source_target_pairs={{0,96},{32,0},{64,32},{96,64},{128,224},{160,128},{192,160},{224,1... | collective-permute-start | bytes 221192 | tf_op jit(solution)/shard_map/ppermute | solution.py:330
  29.1 7.6 %collective-permute-start.9 = (bf16[144,256]{1,0:T(8,128)(2,1)S(1)}, bf16[144,256]{1,0:T(8,128)(2,1)S(1)}, u32[]{:S(2)}, u32[]{:S(2)}) collective-permute-start(bf16[144,256]{1,0:T(8,128)(2,1)S(1)} %get-tuple-element.47.refs_0_), channel_id=1, source_target_pairs={{0,64},{32,96},{64,0},{96,32},{128,192},{160,224},{192,128},{224,1... | collective-permute-start | bytes 221192 | tf_op jit(solution)/shard_map/ppermute | solution.py:330
  32.4 5.6 %collective-permute-start.8 = (bf16[144,256]{1,0:T(8,128)(2,1)S(1)}, bf16[144,256]{1,0:T(8,128)(2,1)S(1)}, u32[]{:S(2)}, u32[]{:S(2)}) collective-permute-start(bf16[144,256]{1,0:T(8,128)(2,1)S(1)} %get-tuple-element.47.refs_0_), channel_id=1, source_target_pairs={{0,32},{32,64},{64,96},{96,0},{128,160},{160,192},{192,224},{224,1... | collective-permute-start | bytes 221192 | tf_op jit(solution)/shard_map/ppermute | solution.py:330
  38.1 8.2 %collective-permute-start.11 = (bf16[128,256]{1,0:T(8,128)(2,1)S(1)}, bf16[128,256]{1,0:T(8,128)(2,1)S(1)}, u32[]{:S(2)}, u32[]{:S(2)}) collective-permute-start(bf16[128,256]{1,0:T(8,128)(2,1)S(1)} %get-tuple-element.50), channel_id=1, source_target_pairs={{0,224},{32,192},{64,160},{96,128},{128,96},{160,64},{192,32},{224... | collective-permute-start | bytes 196616 | tf_op jit(solution)/shard_map/ppermute | solution.py:336
  46.4 5.6 %collective-permute-start.12 = (bf16[128,256]{1,0:T(8,128)(2,1)S(1)}, bf16[128,256]{1,0:T(8,128)(2,1)S(1)}, u32[]{:S(2)}, u32[]{:S(2)}) collective-permute-start(bf16[128,256]{1,0:T(8,128)(2,1)S(1)} %get-tuple-element.53), channel_id=1, source_target_pairs={{0,8},{8,16},{16,24},{24,0},{1,9},{9,17},{17,25},{25,1},{2,10},{10... | collective-permute-start | bytes 196616 | tf_op jit(solution)/shard_map/ppermute | solution.py:282
  46.8 6.3 %collective-permute-start.13 = (bf16[128,256]{1,0:T(8,128)(2,1)S(1)}, bf16[128,256]{1,0:T(8,128)(2,1)S(1)}, u32[]{:S(2)}, u32[]{:S(2)}) collective-permute-start(bf16[128,256]{1,0:T(8,128)(2,1)S(1)} %get-tuple-element.54), channel_id=1, source_target_pairs={{0,16},{8,24},{16,0},{24,8},{1,17},{9,25},{17,1},{25,9},{2,18},{10... | collective-permute-start | bytes 196616 | tf_op jit(solution)/shard_map/ppermute | solution.py:282
  50.2 4.3 %collective-permute-start.14 = (bf16[128,256]{1,0:T(8,128)(2,1)S(1)}, bf16[128,256]{1,0:T(8,128)(2,1)S(1)}, u32[]{:S(2)}, u32[]{:S(2)}) collective-permute-start(bf16[128,256]{1,0:T(8,128)(2,1)S(1)} %get-tuple-element.55), channel_id=1, source_target_pairs={{0,24},{8,0},{16,8},{24,16},{1,25},{9,1},{17,9},{25,17},{2,26},{10... | collective-permute-start | bytes 196616 | tf_op jit(solution)/shard_map/ppermute | solution.py:282
  54.8 1.6 %collective-permute-start.15 = (bf16[128,1024]{1,0:T(8,128)(2,1)S(1)}, bf16[128,1024]{1,0:T(8,128)(2,1)S(1)}, u32[]{:S(2)}, u32[]{:S(2)}) collective-permute-start(bf16[128,1024]{1,0:T(8,128)(2,1)S(1)} %get-tuple-element.57), channel_id=1, source_target_pairs={{0,4},{4,0},{1,5},{5,1},{2,6},{6,2},{3,7},{7,3},{8,12},{12,8},{9,1... | collective-permute-start | bytes 786440 | tf_op jit(solution)/shard_map/ppermute | solution.py:282
  56.4 8.5 %copy-start.3 = (f32[2048]{0:T(1024)S(1)}, f32[2048]{0:T(1024)}, u32[]{:S(2)}) copy-start(f32[2048]{0:T(1024)} %param.17) | copy-start | bytes 24580
  57.0 3.8 %collective-permute-start.18 = (f32[8,256]{1,0:T(8,128)S(1)}, f32[8,256]{1,0:T(8,128)S(1)}, u32[]{:S(2)}, u32[]{:S(2)}) collective-permute-start(f32[8,256]{1,0:T(8,128)S(1)} %get-tuple-element.60.refs_1_), channel_id=1, source_target_pairs={{0,3},{1,0},{2,1},{3,2},{4,7},{5,4},{6,5},{7,6},{8,11},{9,8},{10,9... | collective-permute-start | bytes 24584 | tf_op jit(solution)/shard_map/ppermute | solution.py:282
  59.0 5.2 %collective-permute-start.17 = (f32[8,256]{1,0:T(8,128)S(1)}, f32[8,256]{1,0:T(8,128)S(1)}, u32[]{:S(2)}, u32[]{:S(2)}) collective-permute-start(f32[8,256]{1,0:T(8,128)S(1)} %get-tuple-element.60.refs_1_), channel_id=1, source_target_pairs={{0,2},{1,3},{2,0},{3,1},{4,6},{5,7},{6,4},{7,5},{8,10},{9,11},{10,... | collective-permute-start | bytes 24584 | tf_op jit(solution)/shard_map/ppermute | solution.py:282
  60.1 4.9 %collective-permute-start.16 = (f32[8,256]{1,0:T(8,128)S(1)}, f32[8,256]{1,0:T(8,128)S(1)}, u32[]{:S(2)}, u32[]{:S(2)}) collective-permute-start(f32[8,256]{1,0:T(8,128)S(1)} %get-tuple-element.60.refs_1_), channel_id=1, source_target_pairs={{0,1},{1,2},{2,3},{3,0},{4,5},{5,6},{6,7},{7,4},{8,9},{9,10},{10,1... | collective-permute-start | bytes 24584 | tf_op jit(solution)/shard_map/ppermute | solution.py:282
